TPU v7x, 32 devices: a whole 2x2x4 slice. The times are simulated.
32 devices in a mesh: group: 4 (over y, core), member: 8 (over z, x).
Axes of the slice: x: 2, y: 2, z: 4, core: 2. Of those that a mesh axis runs over, the one named last changes fastest.
Arguments:
- latent: bfloat16 [256, 1024], P(('group', 'member')), may hold values from -6 to 6
- out_grad: bfloat16 [256, 1024], P(('group', 'member')), may hold values from -6 to 6
- gates: bfloat16 [256, 22], P(('group', 'member')), may hold values from 0.019897461 to 0.29882812
- expert_ids: int32 [256, 22], P(('group', 'member')), may hold values from 0 to 31, all different within a row; in each aligned block of 8 rows (0 to 7, 8 to 15, ...) at most 6 rows name the same one
- up_weight: bfloat16 [8, 10752, 1024], P('member', 'group'), may hold values from -0.1875 to 0.1875
- down_weight: bfloat16 [8, 10752, 1024], P('member', 'group'), may hold values from -0.125 to 0.125
Outputs:
- latent_grad: float32 [256, 1024], P(('group', 'member'))
- up_grad: bfloat16 [8, 10752, 1024], P('member', 'group')
- down_grad: bfloat16 [8, 10752, 1024], P('member', 'group')
Inputs may be any that keep to these rules, and one draw needn't show every extreme that they name: `expert_ids`: the 22 experts of a token are distinct. Among the 8 tokens of one device no expert is named more than 6 times, and in every draw some expert is named exactly 6 times by the tokens of some device.
All inputs are finite; a program needn't handle non-finite values.
Results may differ from a plain program's by a relative error of at most 0.0057.
Values may be sent and summed in bfloat16 or wider, within the bound.
No kernel may reach another device: no remote copies, remote signals or barrier semaphores. Data moves between devices by JAX's collectives and lax.ppermute only.
A program may use at most 64 MiB of HBM per device.

v0:
```python
import jax
import jax.numpy as jnp
from jax import lax
from jax.sharding import PartitionSpec as P

HID = 2688


def slot_tables(routes, gate_lists, experts, most_rows):
    labels = jnp.arange(experts, dtype=jnp.int32)
    named = routes[..., None] == labels
    chosen = jnp.sum(named.astype(jnp.int32), axis=-2)
    before = jnp.cumsum(chosen, axis=-2) - chosen
    ranks = jnp.arange(most_rows, dtype=jnp.int32)
    table = (chosen[..., None] * (before[..., None] == ranks).astype(jnp.int32)).astype(jnp.float32)
    weight = jnp.sum(
        jnp.where(named, gate_lists.astype(jnp.float32)[..., None], jnp.float32(0.0)), axis=-2
    )
    return (table, table * weight[..., None])


def local(latent, out_grad, gates, expert_ids, up_weight, down_weight):
    tok_rows = latent.shape[0]
    width = latent.shape[1]
    top_count = expert_ids.shape[1]
    slice_rows = up_weight.shape[1]
    members = lax.axis_size("member")
    groups = lax.axis_size("group")
    local_experts = groups * slice_rows // HID
    slices = groups // local_experts
    experts = local_experts * members
    most_rows = min(tok_rows, max(2, (tok_rows * top_count + experts - 1) // experts))
    mine = lax.axis_index("group") // slices
    routes_column = lax.all_gather(expert_ids, "group", axis=0, tiled=True).reshape(
        groups, tok_rows, top_count
    )
    column_table, unused = slot_tables(
        routes_column, jnp.zeros(routes_column.shape, jnp.float32), experts, most_rows
    )
    column_table = column_table.reshape(groups, tok_rows, members, local_experts, most_rows)
    column_table = lax.dynamic_index_in_dim(column_table, mine, 3, keepdims=False)
    x_col, dy_col, gate_col = (
        lax.all_gather(latent, "group", axis=0, tiled=True),
        lax.all_gather(out_grad, "group", axis=0, tiled=True),
        lax.all_gather(gates, "group", axis=0, tiled=True),
    )
    zero_one, weighted = slot_tables(
        routes_column, gate_col.reshape(groups, tok_rows, top_count), experts, most_rows
    )
    weighted = weighted.reshape(groups, tok_rows, members, local_experts, most_rows)
    weighted = lax.dynamic_index_in_dim(weighted, mine, 3, keepdims=False)
    x_col = x_col.reshape(groups, tok_rows, width)
    dy_col = dy_col.reshape(groups, tok_rows, width)
    send_x = jnp.einsum(
        "gtms,gtl->mgsl",
        column_table.astype(jnp.bfloat16),
        x_col,
        preferred_element_type=jnp.float32,
    ).astype(jnp.bfloat16)
    send_dy = jnp.einsum(
        "gtms,gtl->mgsl", weighted, dy_col.astype(jnp.float32), precision=lax.Precision.HIGHEST
    ).astype(jnp.bfloat16)
    rows_x, rows_dy = (
        lax.all_to_all(send_x, "member", split_axis=0, concat_axis=0, tiled=True),
        lax.all_to_all(send_dy, "member", split_axis=0, concat_axis=0, tiled=True),
    )
    rows_x = rows_x.reshape(-1, width)
    rows_dy = rows_dy.reshape(-1, width)
    w_up = up_weight[0]
    w_down = down_weight[0]
    pre = jnp.einsum("rl,hl->rh", rows_x, w_up, preferred_element_type=jnp.float32)
    relu = jnp.maximum(pre, 0.0)
    act = (relu * relu).astype(jnp.bfloat16)
    hid_grad = jnp.einsum("rl,hl->rh", rows_dy, w_down, preferred_element_type=jnp.float32)
    pre_grad = (hid_grad * 2.0 * relu).astype(jnp.bfloat16)
    up_grad = jnp.einsum("rh,rl->hl", pre_grad, rows_x, preferred_element_type=jnp.float32).astype(
        jnp.bfloat16
    )
    down_grad = jnp.einsum("rh,rl->hl", act, rows_dy, preferred_element_type=jnp.float32).astype(
        jnp.bfloat16
    )
    part_grad = jnp.einsum("rh,hl->rl", pre_grad, w_up, preferred_element_type=jnp.float32).astype(
        jnp.bfloat16
    )
    part_grad = part_grad.reshape(members, groups, most_rows, width)
    returned = lax.all_to_all(part_grad, "member", split_axis=0, concat_axis=0, tiled=True)
    column_grad = jnp.einsum(
        "gtms,mgsl->gtl",
        column_table.astype(jnp.bfloat16),
        returned,
        preferred_element_type=jnp.float32,
    )
    latent_grad = lax.psum_scatter(
        column_grad.reshape(groups * tok_rows, width), "group", scatter_dimension=0, tiled=True
    )
    return (latent_grad, up_grad[None], down_grad[None])


def solution(mesh):
    in_specs = (
        P(("group", "member"), None),
        P(("group", "member"), None),
        P(("group", "member"), None),
        P(("group", "member"), None),
        P("member", "group", None),
        P("member", "group", None),
    )
    out_specs = (
        P(("group", "member"), None),
        P("member", "group", None),
        P("member", "group", None),
    )
    return jax.shard_map(local, mesh=mesh, in_specs=in_specs, out_specs=out_specs, check_vma=False)
```

profile of v0, /device:TPU:0, one launch (start us, length us, event | category | flops | bytes accessed | tf_op | source)
XLA Modules:
  0.0 123.0 jit_solution(6196416059324755865)
XLA Ops:
  7.2 6.4 %all_gather.12 = s32[32,22]{1,0:T(8,128)S(1)} all-gather(s32[8,22]{1,0:T(8,128)} %param.9), channel_id=1, replica_groups=mesh['group'=4,'member'=8] {'group'}, dimensions={0}, use_global_device_ids=true | all-gather | bytes 3520 | tf_op jit(solution)/shard_map/all_gather | solution.py:34
  13.5 0.1 copy.35
  13.6 0.2 convert_reduce_fusion
  13.8 0.1 copy.36
  13.9 5.7 %reduce_window_sum.15 = s32[4,8,8,4]{1,3,2,0:T(4,128)S(1)} reduce-window(s32[4,8,8,4]{1,3,2,0:T(4,128)S(1)} %bitcast.67, s32[]{:T(128)} %constant.30.clone.1), window={size=1x8x1x1 pad=0_0x7_0x0_0x0_0}, to_apply=%region_1.2 | reduce-window | flops 7168 | bytes 8196 | tf_op jit(solution)/shard_map/jit(cumsum)/reduce_window_sum | solution.py:13
  19.5 5.5 %all_gather.13 = bf16[32,22]{1,0:T(8,128)(2,1)S(1)} all-gather(bf16[8,22]{1,0:T(8,128)(2,1)} %param.8), channel_id=1, replica_groups=mesh['group'=4,'member'=8] {'group'}, dimensions={0}, use_global_device_ids=true | all-gather | bytes 1760 | tf_op jit(solution)/shard_map/all_gather | solution.py:45
  25.0 0.1 copy.39
  25.1 0.3 select_reduce_fusion
  25.4 0.1 copy.40
  25.5 5.5 %all_gather.14 = bf16[32,1024]{1,0:T(8,128)(2,1)S(1)} all-gather(bf16[8,1024]{1,0:T(8,128)(2,1)} %param.7), channel_id=1, replica_groups=mesh['group'=4,'member'=8] {'group'}, dimensions={0}, use_global_device_ids=true | all-gather | bytes 81920 | tf_op jit(solution)/shard_map/all_gather | solution.py:44
  31.0 0.0 copy-start.3
  31.0 0.5 fusion.24
  31.5 1.1 copy.42
  32.5 6.0 %all-to-all-start = ((bf16[8,4,6,1024]{3,1,2,0:T(4,128)(2,1)}), bf16[8,4,6,1024]{3,1,2,0:T(4,128)(2,1)S(1)}, u32[]{:S(2)}, u32[]{:S(2)}) async-start(bf16[8,4,6,1024]{3,1,2,0:T(4,128)(2,1)} %copy.42), calls=%async_computation | async-start | bytes 786432 | tf_op jit(solution)/shard_map/all_to_all | solution.py:65
  38.6 5.4 %all_gather.15 = bf16[32,1024]{1,0:T(8,128)(2,1)S(1)} all-gather(bf16[8,1024]{1,0:T(8,128)(2,1)} %param.6), channel_id=1, replica_groups=mesh['group'=4,'member'=8] {'group'}, dimensions={0}, use_global_device_ids=true | all-gather | bytes 81920 | tf_op jit(solution)/shard_map/all_gather | solution.py:43
  44.0 0.2 fusion.23
  44.2 1.1 copy.44
  45.3 5.4 %all-to-all-done = bf16[8,4,6,1024]{3,1,2,0:T(4,128)(2,1)S(1)} async-done(((bf16[8,4,6,1024]{3,1,2,0:T(4,128)(2,1)}), bf16[8,4,6,1024]{3,1,2,0:T(4,128)(2,1)S(1)}, u32[]{:S(2)}, u32[]{:S(2)}) %all-to-all-start) | async-done | bytes 393248 | tf_op jit(solution)/shard_map/all_to_all | solution.py:65
  50.7 0.0 copy-done.3
  50.7 3.6 %all-to-all-start.1 = ((bf16[8,4,6,1024]{3,1,2,0:T(4,128)(2,1)}), bf16[8,4,6,1024]{3,1,2,0:T(4,128)(2,1)S(1)}, u32[]{:S(2)}, u32[]{:S(2)}) async-start(bf16[8,4,6,1024]{3,1,2,0:T(4,128)(2,1)} %copy.44), calls=%async_computation.1 | async-start | bytes 786432 | tf_op jit(solution)/shard_map/all_to_all | solution.py:64
  54.4 0.1 copy.43
  54.5 0.1 reshape.58
  54.7 11.6 %all-to-all-done.1 = bf16[8,4,6,1024]{3,1,2,0:T(4,128)(2,1)S(1)} async-done(((bf16[8,4,6,1024]{3,1,2,0:T(4,128)(2,1)}), bf16[8,4,6,1024]{3,1,2,0:T(4,128)(2,1)S(1)}, u32[]{:S(2)}, u32[]{:S(2)}) %all-to-all-start.1) | async-done | bytes 393248 | tf_op jit(solution)/shard_map/all_to_all | solution.py:64
  66.3 0.1 copy.45
  66.4 0.1 reshape.60
  66.5 0.0 copy-start.2
  66.5 0.0 slice-start
  66.6 4.7 %fusion.11 = f32[192,2688]{1,0:T(8,128)S(1)} fusion(bf16[192,1024]{1,0:T(8,128)(2,1)S(1)} %reshape.60, bf16[1,2688,1024]{2,1,0:T(8,128)(2,1)} %param.10), kind=kOutput, calls=%fused_computation.11 | convolution fusion | flops 1057480704 | bytes 7962624 | tf_op jit(solution)/shard_map/rl,hl->rh/dot_general | solution.py:71
  71.3 0.0 slice-start.1
  71.3 4.6 %fusion.17 = bf16[192,2688]{1,0:T(8,128)(2,1)S(1)} fusion(f32[192,2688]{1,0:T(8,128)S(1)} %fusion.11, bf16[192,1024]{1,0:T(8,128)(2,1)S(1)} %reshape.58, bf16[1,2688,1024]{2,1,0:T(8,128)(2,1)} %param.11), kind=kOutput, calls=%fused_computation.13 | convolution fusion | flops 1058512896 | bytes 8994816 | tf_op jit(solution)/shard_map/rl,hl->rh/dot_general | solution.py:74
  75.9 0.0 copy-done.2
  75.9 0.0 copy-start
  75.9 1.0 copy-done
  76.9 0.0 slice-done
  76.9 0.0 slice-done.1
  76.9 1.3 %fusion.20 = bf16[192,1024]{1,0:T(8,128)(2,1)S(1)} fusion(bf16[192,2688]{1,0:T(8,128)(2,1)S(1)} %fusion.17, bf16[1,2688,1024]{2,1,0:T(8,128)(2,1)S(1)} %bitcast.65), kind=kOutput, calls=%fused_computation.15 | convolution fusion | flops 1057161216 | bytes 6930432 | tf_op jit(solution)/shard_map/rh,hl->rl/dot_general | solution.py:82
  78.2 0.1 reshape.61
  78.3 1.1 copy.46
  79.4 0.0 copy-start.1
  79.4 4.2 %all-to-all-start.2 = ((bf16[8,4,6,1024]{3,1,2,0:T(4,128)(2,1)}), bf16[8,4,6,1024]{3,1,2,0:T(4,128)(2,1)}, u32[]{:S(2)}, u32[]{:S(2)}) async-start(bf16[8,4,6,1024]{3,1,2,0:T(4,128)(2,1)} %copy.46), calls=%async_computation.2 | async-start | bytes 786432 | tf_op jit(solution)/shard_map/all_to_all | solution.py:86
  83.6 0.0 reduce-scatter.2.cloned.1.call-start
  83.7 4.1 %fusion.7 = bf16[1,2688,1024]{2,1,0:T(8,128)(2,1)} fusion(bf16[192,1024]{1,0:T(8,128)(2,1)S(1)} %reshape.58, f32[192,2688]{1,0:T(8,128)S(1)} %fusion.11), kind=kOutput, calls=%fused_computation.9 | convolution fusion | flops 1060749312 | bytes 7962624 | tf_op jit(solution)/shard_map/rh,rl->hl/dot_general | solution.py:79
  87.8 7.3 %all-to-all-done.2 = bf16[8,4,6,1024]{3,1,2,0:T(4,128)(2,1)} async-done(((bf16[8,4,6,1024]{3,1,2,0:T(4,128)(2,1)}), bf16[8,4,6,1024]{3,1,2,0:T(4,128)(2,1)}, u32[]{:S(2)}, u32[]{:S(2)}) %all-to-all-start.2) | async-done | bytes 393248 | tf_op jit(solution)/shard_map/all_to_all | solution.py:86
  95.1 2.2 %convolution_bitcast_fusion = f32[32,1024]{1,0:T(8,128)} fusion(bf16[8,4,6,1024]{3,1,2,0:T(4,128)(2,1)} %all-to-all-done.2, f32[4,8,8,4,6]{1,2,4,0,3:T(8,128)} %copy-done.3, s32[]{:T(128)S(6)} %select_n.12), kind=kOutput, calls=%fused_computation.20 | convolution fusion | flops 3145728 | bytes 573444 | tf_op jit(solution)/shard_map/gtms,mgsl->gtl/dot_general | solution.py:87
  97.3 0.0 reduce-scatter.2.cloned.1.call-update
  97.3 0.0 copy-done.1
  97.4 5.1 %fusion.6 = bf16[1,2688,1024]{2,1,0:T(8,128)(2,1)} fusion(bf16[192,2688]{1,0:T(8,128)(2,1)S(1)} %copy-done.1, bf16[192,1024]{1,0:T(8,128)(2,1)} %copy-done.2), kind=kOutput, calls=%fused_computation.8 | convolution fusion | flops 1059717120 | bytes 6930432 | tf_op jit(solution)/shard_map/rh,rl->hl/dot_general | solution.py:76
  102.4 13.7 %reduce-scatter.2.cloned.1.call-done = f32[8,1024]{1,0:T(8,128)} async-done(((f32[32,1024]{1,0:T(8,128)}), f32[8,1024]{1,0:T(8,128)}) %reduce-scatter.2.cloned.1.call-update) | async-done | bytes 32784 | tf_op jit(solution)/shard_map/reduce_scatter | solution.py:93
  (8 shorter events, 0.1 us)
Async XLA Ops:
  31.0 19.7 %copy-start.3 = (f32[4,8,8,4,6]{1,2,4,0,3:T(8,128)}, f32[4,8,8,4,6]{1,2,4,0,3:T(8,128)S(1)}, u32[]{:S(2)}) copy-start(f32[4,8,8,4,6]{1,2,4,0,3:T(8,128)S(1)} %select_convert_fusion) | copy-start | bytes 73732
  32.5 18.2 %all-to-all-start = ((bf16[8,4,6,1024]{3,1,2,0:T(4,128)(2,1)}), bf16[8,4,6,1024]{3,1,2,0:T(4,128)(2,1)S(1)}, u32[]{:S(2)}, u32[]{:S(2)}) async-start(bf16[8,4,6,1024]{3,1,2,0:T(4,128)(2,1)} %copy.42), calls=%async_computation | async-start | bytes 786432 | tf_op jit(solution)/shard_map/all_to_all | solution.py:65
  50.7 15.5 %all-to-all-start.1 = ((bf16[8,4,6,1024]{3,1,2,0:T(4,128)(2,1)}), bf16[8,4,6,1024]{3,1,2,0:T(4,128)(2,1)S(1)}, u32[]{:S(2)}, u32[]{:S(2)}) async-start(bf16[8,4,6,1024]{3,1,2,0:T(4,128)(2,1)} %copy.44), calls=%async_computation.1 | async-start | bytes 786432 | tf_op jit(solution)/shard_map/all_to_all | solution.py:64
  66.5 9.4 %copy-start.2 = (bf16[192,1024]{1,0:T(8,128)(2,1)}, bf16[192,1024]{1,0:T(8,128)(2,1)S(1)}, u32[]{:S(2)}) copy-start(bf16[192,1024]{1,0:T(8,128)(2,1)S(1)} %reshape.60) | copy-start | bytes 1179652
  66.5 10.3 %slice-start = ((s8[5505024]{0:T(1024)(128)(4,1)}), s8[4194304]{0:T(1024)(128)(4,1)S(1)}, s32[]{:S(2)}) async-start(s8[5505024]{0:T(1024)(128)(4,1)} %bitcast.64), calls=%async_computation.5 | async-start | bytes 8388608
  71.3 5.6 %slice-start.1 = ((s8[5505024]{0:T(1024)(128)(4,1)}), s8[1310720]{0:T(1024)(128)(4,1)S(1)}, s32[]{:S(2)}) async-start(s8[5505024]{0:T(1024)(128)(4,1)} %bitcast.64), calls=%async_computation.6 | async-start | bytes 2621440
  75.9 1.0 copy-start
  79.4 18.0 %copy-start.1 = (bf16[192,2688]{1,0:T(8,128)(2,1)S(1)}, bf16[192,2688]{1,0:T(8,128)(2,1)}, u32[]{:S(2)}) copy-start(bf16[192,2688]{1,0:T(8,128)(2,1)} %copy-done) | copy-start | bytes 3096580
  79.4 15.7 %all-to-all-start.2 = ((bf16[8,4,6,1024]{3,1,2,0:T(4,128)(2,1)}), bf16[8,4,6,1024]{3,1,2,0:T(4,128)(2,1)}, u32[]{:S(2)}, u32[]{:S(2)}) async-start(bf16[8,4,6,1024]{3,1,2,0:T(4,128)(2,1)} %copy.46), calls=%async_computation.2 | async-start | bytes 786432 | tf_op jit(solution)/shard_map/all_to_all | solution.py:86
  83.6 32.5 %reduce-scatter.2.cloned.1.call-start = ((), (), s32[]{:S(2)}) async-start(), calls=%async_computation.4 | async-start | bytes 163840 | tf_op jit(solution)/shard_map/reduce_scatter | solution.py:93
Sparse Core Ops, SparseCore 0:
  97.5 18.6 reduce-scatter.1
where the time goes:
time: 124 us; the launch traced here: 123 us
  waiting for transfers between devices  38.1 us (31%)
  blocking collectives  22.7 us (18%)
  matrix products  22.7 us (18%)
  between operations  14.2 us (11%)
  starting transfers between devices  13.9 us (11%)
  other arithmetic  6.13 us (5%)
  local copies, waits for them, and re-layouts  5.2 us (4%)
    reduce_scatter x1, waiting for transfers between devices, local(): lax.psum_scatter(column_grad.reshape(groups * tok_rows, width), 'group',...  13.7 us
    all_to_all x1, waiting for transfers between devices, local(): lax.all_to_all(send_x, 'member', split_axis=0, concat_axis=0, tiled=True)  11.6 us
    all_to_all x1, waiting for transfers between devices, local(): lax.all_to_all(part_grad, 'member', split_axis=0, concat_axis=0, tiled=True)  7.32 us
    all_gather x1, blocking collectives, local(): lax.all_gather(expert_ids, 'group', axis=0, tiled=True)  6.35 us
    all_to_all x1, starting transfers between devices, local(): lax.all_to_all(send_dy, 'member', split_axis=0, concat_axis=0, tiled=True)  6.04 us
    another operation x1, other arithmetic, slot_tables(): before = jnp.cumsum(chosen, axis=-2) - chosen  5.65 us
    all_gather x1, blocking collectives, local(): lax.all_gather(gates, 'group', axis=0, tiled=True)  5.47 us
    all_gather x1, blocking collectives, local(): lax.all_gather(out_grad, 'group', axis=0, tiled=True)  5.46 us
  transfers between devices with their start and end apart: 4, of which 4 were waited for; matrix products, arithmetic and copies ran while one was open for 9% of the time, Pallas kernels for 0%

commit v1 on v0

v1 whole, which is shorter than its diff:
```python
import jax
import jax.numpy as jnp
from jax import lax
from jax.sharding import PartitionSpec as P

HID = 2688
AXES = ("group", "member")


def rounds(members, devices):
    bits = []
    bit = 1
    while bit < devices:
        if bit != members:
            bits.append(bit)
        bit *= 2
    far = members // 2
    rest = [b for b in bits if b != far]
    rest = rest[1:] + rest[:1]
    return [(far, far)] + list(zip(rest, rest[1:] + rest[:1]))


def swap(value, pair, core, devices):
    even, odd = pair
    pairs = [(i, i ^ (odd if i & core else even)) for i in range(devices)]
    return lax.ppermute(value, AXES, pairs)


def local(latent, out_grad, gates, expert_ids, up_weight, down_weight):
    width = latent.shape[1]
    slice_rows = up_weight.shape[1]
    members = lax.axis_size("member")
    groups = lax.axis_size("group")
    devices = members * groups
    local_experts = groups * slice_rows // HID
    slices = groups // local_experts
    experts = local_experts * members
    mine = lax.axis_index("member") * local_experts + lax.axis_index("group") // slices
    plan = rounds(members, devices)

    labels = jnp.arange(128, dtype=jnp.int32)
    named = expert_ids[:, :, None] == labels
    dense = jnp.sum(
        jnp.where(named, gates.astype(jnp.float32)[:, :, None], jnp.float32(0.0)), axis=1
    ).astype(jnp.bfloat16)
    packed = lax.optimization_barrier(jnp.concatenate([latent, out_grad, dense], axis=1))
    for pair in plan:
        packed = jnp.concatenate([packed, swap(packed, pair, members, devices)], axis=0)
        packed = lax.optimization_barrier(packed)
    packed = jnp.concatenate([packed, swap(packed, (members, members), members, devices)], axis=0)
    x = packed[:, :width]
    gate = jnp.sum(
        jnp.where(labels == mine, packed[:, 2 * width :].astype(jnp.float32), jnp.float32(0.0)),
        axis=1,
        keepdims=True,
    )
    dy = (gate * packed[:, width : 2 * width].astype(jnp.float32)).astype(jnp.bfloat16)

    w_up = up_weight[0]
    w_down = down_weight[0]
    pre = jnp.einsum("rl,hl->hr", x, w_up, preferred_element_type=jnp.float32)
    relu = jnp.maximum(pre, 0.0)
    act = (relu * relu).astype(jnp.bfloat16)
    hid_grad = jnp.einsum("rl,hl->hr", dy, w_down, preferred_element_type=jnp.float32)
    pre_grad = (hid_grad * 2.0 * relu).astype(jnp.bfloat16)
    part = jnp.einsum("hr,hl->rl", pre_grad, w_up, preferred_element_type=jnp.float32).astype(
        jnp.bfloat16
    )
    up_grad = jnp.einsum("hr,rl->hl", pre_grad, x, preferred_element_type=jnp.float32).astype(
        jnp.bfloat16
    )
    down_grad = jnp.einsum("hr,rl->hl", act, dy, preferred_element_type=jnp.float32).astype(
        jnp.bfloat16
    )

    half = part.shape[0] // 2
    total = part[:half].astype(jnp.float32) + swap(
        part[half:], (members, members), members, devices
    ).astype(jnp.float32)
    for pair in reversed(plan):
        half = total.shape[0] // 2
        got = swap(total[half:].astype(jnp.bfloat16), pair, members, devices)
        total = total[:half] + got.astype(jnp.float32)
    return (total, up_grad[None], down_grad[None])


def solution(mesh):
    rows = P(AXES, None)
    weights = P("member", "group", None)
    return jax.shard_map(
        local,
        mesh=mesh,
        in_specs=(rows, rows, rows, rows, weights, weights),
        out_specs=(rows, weights, weights),
        check_vma=False,
    )
```

time: 124 us -> 61 us (0.49)
  blocking collectives: 22.7 us -> 0 us
  waiting for transfers between devices: 38.1 us -> 22.3 us
  between operations: 14.2 us -> 0.82 us
  matrix products: 22.7 us -> 15.9 us
  other arithmetic: 6.13 us -> 1.79 us
  starting transfers between devices: 13.9 us -> 17.6 us
  local copies, waits for them, and re-layouts: 5.2 us -> 2.31 us
    all_to_all x3 -> x0, waiting for transfers between devices: 24.4 us -> none  [the longest x1 11.6 us: local(): lax.all_to_all(send_x, 'member', split_axis=0, concat_axis=0, tiled=True)]
    all_gather x4 -> x0, blocking collectives: 22.7 us -> none  [the longest x1 6.35 us: local(): lax.all_gather(expert_ids, 'group', axis=0, tiled=True)]
    ppermute x0 -> x10, waiting for transfers between devices: none -> 22.3 us  [swap(): return lax.ppermute(value, AXES, pairs)]
    ppermute x0 -> x10, starting transfers between devices: none -> 17.6 us  [swap(): return lax.ppermute(value, AXES, pairs)]
    all_to_all x3 -> x0, starting transfers between devices: 13.9 us -> none  [the longest x1 6.04 us: local(): lax.all_to_all(send_dy, 'member', split_axis=0, concat_axis=0, tiled=True)]
    reduce_scatter x1 -> x0, waiting for transfers between devices: 13.7 us -> none  [local(): lax.psum_scatter(column_grad.reshape(groups * tok_rows, width), 'group',...]
    dot_general x8 -> x5, matrix products: 22.7 us -> 15.9 us  [the longest x1 4.25 us: local(): pre = jnp.einsum('rl,hl->hr', x, w_up, preferred_element_type=jnp.float32)]
    another operation x1 -> x0, other arithmetic: 5.65 us -> none  [slot_tables(): before = jnp.cumsum(chosen, axis=-2) - chosen]
  transfers between devices with their start and end apart: 4 -> 10, of which waited for: 4 -> 8; matrix products, arithmetic and copies ran while one was open for 9% -> 14% of each run, Pallas kernels for 0% -> 0%
where the time goes in v1:
time: 61 us; the launch traced here: 60.6 us
  waiting for transfers between devices  22.3 us (37%)
  starting transfers between devices  17.6 us (29%)
  matrix products  15.9 us (26%)
  local copies, waits for them, and re-layouts  2.31 us (4%)
  other arithmetic  1.79 us (3%)
  between operations  0.82 us (1%)
    ppermute x10, waiting for transfers between devices, swap(): return lax.ppermute(value, AXES, pairs)  22.3 us
    ppermute x10, starting transfers between devices, swap(): return lax.ppermute(value, AXES, pairs)  17.6 us
    dot_general x1, matrix products, local(): pre = jnp.einsum('rl,hl->hr', x, w_up, preferred_element_type=jnp.float32)  4.25 us
    dot_general x1, matrix products, local(): jnp.einsum('hr,rl->hl', act, dy, preferred_element_type=jnp.float32)  4.15 us
    dot_general x1, matrix products, local(): jnp.einsum('hr,rl->hl', pre_grad, x, preferred_element_type=jnp.float32)  4.08 us
    dot_general x1, matrix products, local(): jnp.einsum('rl,hl->hr', dy, w_down, preferred_element_type=jnp.float32)  1.76 us
    dot_general x1, matrix products, local(): jnp.einsum('hr,hl->rl', pre_grad, w_up, preferred_element_type=jnp.float32)  1.65 us
    unnamed x9, local copies, waits for them, and re-layouts  1.49 us
  transfers between devices with their start and end apart: 10, of which 8 were waited for; matrix products, arithmetic and copies ran while one was open for 14% of the time, Pallas kernels for 0%

profile of v1, /device:TPU:0, one launch (start us, length us, event | category | flops | bytes accessed | tf_op | source)
XLA Modules:
  0.0 60.6 jit_solution(12392113422993272460)
XLA Ops:
  0.6 0.8 %copy.10 = f32[8,22]{0,1:T(8,128)S(1)} copy(bf16[8,22]{1,0:T(8,128)(2,1)} %param.8) | data formatting | bytes 1056 | tf_op jit(solution)/shard_map/convert_element_type | solution.py:44
  1.4 0.8 %copy.9 = s32[8,22]{0,1:T(8,128)S(1)} copy(s32[8,22]{1,0:T(8,128)} %param.9) | data formatting | bytes 1408 | tf_op args[3]
  2.2 0.1 select_reduce_fusion.1
  2.3 0.7 %pad_maximum_fusion.7 = bf16[8,2176]{1,0:T(8,128)(2,1)S(1)} fusion(bf16[8,128]{1,0:T(8,128)(2,1)S(1)} %select_reduce_fusion.1, bf16[8,1024]{1,0:T(8,128)(2,1)} %param.7, bf16[8,1024]{1,0:T(8,128)(2,1)} %param.6), kind=kLoop, calls=%fused_computation.32 | loop fusion | flops 104448 | bytes 69632 | tf_op jit(solution)/shard_map/concatenate | solution.py:46
  3.0 4.0 %collective-permute-start = (bf16[8,2176]{1,0:T(8,128)(2,1)S(1)}, bf16[8,2176]{1,0:T(8,128)(2,1)S(1)}, u32[]{:S(2)}, u32[]{:S(2)}) collective-permute-start(bf16[8,2176]{1,0:T(8,128)(2,1)S(1)} %pad_maximum_fusion.7), channel_id=1, source_target_pairs={{0,4},{1,5},{2,6},{3,7},{4,0},{5,1},{6,2},{7,3},{8,12},{9,13},{10,... | collective-permute-start | bytes 104456 | tf_op jit(solution)/shard_map/ppermute | solution.py:26
  7.1 2.3 %collective-permute-done = bf16[8,2176]{1,0:T(8,128)(2,1)S(1)} collective-permute-done((bf16[8,2176]{1,0:T(8,128)(2,1)S(1)}, bf16[8,2176]{1,0:T(8,128)(2,1)S(1)}, u32[]{:S(2)}, u32[]{:S(2)}) %collective-permute-start) | collective-permute-done | bytes 34848 | tf_op jit(solution)/shard_map/ppermute | solution.py:26
  9.4 1.5 %collective-permute-start.1 = (bf16[16,2176]{1,0:T(8,128)(2,1)S(1)}, bf16[16,2176]{1,0:T(8,128)(2,1)S(1)}, u32[]{:S(2)}, u32[]{:S(2)}) collective-permute-start(bf16[16,2176]{1,0:T(8,128)(2,1)S(1)} %pad_maximum_fusion.4), channel_id=1, source_target_pairs={{0,2},{1,3},{2,0},{3,1},{4,6},{5,7},{6,4},{7,5},{8,24},{9,25},{10,... | collective-permute-start | bytes 208904 | tf_op jit(solution)/shard_map/ppermute | solution.py:26
  10.9 2.8 %collective-permute-done.1 = bf16[16,2176]{1,0:T(8,128)(2,1)S(1)} collective-permute-done((bf16[16,2176]{1,0:T(8,128)(2,1)S(1)}, bf16[16,2176]{1,0:T(8,128)(2,1)S(1)}, u32[]{:S(2)}, u32[]{:S(2)}) %collective-permute-start.1) | collective-permute-done | bytes 69664 | tf_op jit(solution)/shard_map/ppermute | solution.py:26
  13.7 1.8 %collective-permute-start.2 = (bf16[32,2176]{1,0:T(8,128)(2,1)S(1)}, bf16[32,2176]{1,0:T(8,128)(2,1)S(1)}, u32[]{:S(2)}, u32[]{:S(2)}) collective-permute-start(bf16[32,2176]{1,0:T(8,128)(2,1)S(1)} %pad_maximum_fusion.3), channel_id=1, source_target_pairs={{0,16},{1,17},{2,18},{3,19},{4,20},{5,21},{6,22},{7,23},{8,9},{9,8... | collective-permute-start | bytes 417800 | tf_op jit(solution)/shard_map/ppermute | solution.py:26
  15.5 3.3 %collective-permute-done.2 = bf16[32,2176]{1,0:T(8,128)(2,1)S(1)} collective-permute-done((bf16[32,2176]{1,0:T(8,128)(2,1)S(1)}, bf16[32,2176]{1,0:T(8,128)(2,1)S(1)}, u32[]{:S(2)}, u32[]{:S(2)}) %collective-permute-start.2) | collective-permute-done | bytes 139296 | tf_op jit(solution)/shard_map/ppermute | solution.py:26
  18.8 1.8 %collective-permute-start.3 = (bf16[64,2176]{1,0:T(8,128)(2,1)S(1)}, bf16[64,2176]{1,0:T(8,128)(2,1)S(1)}, u32[]{:S(2)}, u32[]{:S(2)}) collective-permute-start(bf16[64,2176]{1,0:T(8,128)(2,1)S(1)} %pad_maximum_fusion.2), channel_id=1, source_target_pairs={{0,1},{1,0},{2,3},{3,2},{4,5},{5,4},{6,7},{7,6},{8,10},{9,11},{10,... | collective-permute-start | bytes 835592 | tf_op jit(solution)/shard_map/ppermute | solution.py:26
  20.6 4.8 %collective-permute-done.3 = bf16[64,2176]{1,0:T(8,128)(2,1)S(1)} collective-permute-done((bf16[64,2176]{1,0:T(8,128)(2,1)S(1)}, bf16[64,2176]{1,0:T(8,128)(2,1)S(1)}, u32[]{:S(2)}, u32[]{:S(2)}) %collective-permute-start.3) | collective-permute-done | bytes 278560 | tf_op jit(solution)/shard_map/ppermute | solution.py:26
  25.5 0.1 collective-permute-start.4
  25.6 0.0 slice-start
  25.6 0.0 slice-start.1
  25.6 1.9 %collective-permute-done.4 = bf16[128,2176]{1,0:T(8,128)(2,1)S(1)} collective-permute-done((bf16[128,2176]{1,0:T(8,128)(2,1)S(1)}, bf16[128,2176]{1,0:T(8,128)(2,1)S(1)}, u32[]{:S(2)}, u32[]{:S(2)}) %collective-permute-start.4) | collective-permute-done | bytes 557088 | tf_op jit(solution)/shard_map/ppermute | solution.py:26
  27.5 4.3 %fusion.14 = f32[256,2688]{1,0:T(8,128)S(1)} fusion(bf16[1,2688,1024]{2,1,0:T(8,128)(2,1)} %param.10, bf16[128,2176]{1,0:T(8,128)(2,1)S(1)} %collective-permute-done.4, bf16[128,2176]{1,0:T(8,128)(2,1)S(1)} %pad_maximum_fusion), kind=kOutput, calls=%fused_computation.12 | convolution fusion | flops 1411022848 | bytes 9371648 | tf_op jit(solution)/shard_map/rl,hl->hr/dot_general | solution.py:61
  31.8 0.0 slice-start.2
  31.8 0.1 select_reduce_fusion
  31.9 0.0 slice-done
  31.9 0.0 slice-done.1
  31.9 0.0 slice-start.3
  31.9 1.8 %fusion.17 = bf16[256,2688]{1,0:T(8,128)(2,1)S(1)} fusion(f32[256,2688]{1,0:T(8,128)S(1)} %fusion.14, bf16[1,2688,1024]{2,1,0:T(8,128)(2,1)S(1)} %bitcast.25, bf16[128,2176]{1,0:T(8,128)(2,1)S(1)} %collective-permute-done.4, bf16[128,2176]{1,0:T(8,128)(2,1)S(1)} %pad_maximum_fusion, f32[256]{0:T(256)S(1)} %select_reduce_fusion), kind=kOutput, calls=%fused_computation.13 | convolution fusion | flops 1412923392 | bytes 10748928 | tf_op jit(solution)/shard_map/rl,hl->hr/dot_general | solution.py:64
  33.7 0.3 slice-done.2
  34.0 0.4 slice-done.3
  34.4 1.7 %fusion.20 = bf16[256,1024]{1,0:T(8,128)(2,1)S(1)} fusion(bf16[256,2688]{1,0:T(8,128)(2,1)S(1)} %fusion.17, bf16[1,2688,1024]{2,1,0:T(8,128)(2,1)S(1)} %bitcast.27), kind=kOutput, calls=%fused_computation.15 | convolution fusion | flops 1409548288 | bytes 7405568 | tf_op jit(solution)/shard_map/hr,hl->rl/dot_general | solution.py:66
  36.1 0.3 collective-permute-start.5
  36.3 1.3 %collective-permute-done.5 = bf16[128,1024]{1,0:T(8,128)(2,1)S(1)} collective-permute-done((bf16[128,1024]{1,0:T(8,128)(2,1)S(1)}, bf16[128,1024]{1,0:T(8,128)(2,1)S(1)}, u32[]{:S(2)}, u32[]{:S(2)}) %collective-permute-start.5) | collective-permute-done | bytes 262176 | tf_op jit(solution)/shard_map/ppermute | solution.py:26
  37.7 0.1 convert_add_fusion
  37.8 1.8 %collective-permute-start.6 = (bf16[64,1024]{1,0:T(8,128)(2,1)S(1)}, bf16[64,1024]{1,0:T(8,128)(2,1)S(1)}, u32[]{:S(2)}, u32[]{:S(2)}) collective-permute-start(bf16[64,1024]{1,0:T(8,128)(2,1)S(1)} %slice.75), channel_id=1, source_target_pairs={{0,1},{1,0},{2,3},{3,2},{4,5},{5,4},{6,7},{7,6},{8,10},{9,11},{10,... | collective-permute-start | bytes 393224 | tf_op jit(solution)/shard_map/ppermute | solution.py:26
  39.6 3.3 %collective-permute-done.6 = bf16[64,1024]{1,0:T(8,128)(2,1)S(1)} collective-permute-done((bf16[64,1024]{1,0:T(8,128)(2,1)S(1)}, bf16[64,1024]{1,0:T(8,128)(2,1)S(1)}, u32[]{:S(2)}, u32[]{:S(2)}) %collective-permute-start.6) | collective-permute-done | bytes 131104 | tf_op jit(solution)/shard_map/ppermute | solution.py:26
  42.9 1.8 %collective-permute-start.7 = (bf16[32,1024]{1,0:T(8,128)(2,1)S(1)}, bf16[32,1024]{1,0:T(8,128)(2,1)S(1)}, u32[]{:S(2)}, u32[]{:S(2)}) collective-permute-start(bf16[32,1024]{1,0:T(8,128)(2,1)S(1)} %slice.76), channel_id=1, source_target_pairs={{0,16},{1,17},{2,18},{3,19},{4,20},{5,21},{6,22},{7,23},{8,9},{9,8... | collective-permute-start | bytes 196616 | tf_op jit(solution)/shard_map/ppermute | solution.py:26
  44.7 2.5 %collective-permute-done.7 = bf16[32,1024]{1,0:T(8,128)(2,1)S(1)} collective-permute-done((bf16[32,1024]{1,0:T(8,128)(2,1)S(1)}, bf16[32,1024]{1,0:T(8,128)(2,1)S(1)}, u32[]{:S(2)}, u32[]{:S(2)}) %collective-permute-start.7) | collective-permute-done | bytes 65568 | tf_op jit(solution)/shard_map/ppermute | solution.py:26
  47.2 1.6 %collective-permute-start.8 = (bf16[16,1024]{1,0:T(8,128)(2,1)S(1)}, bf16[16,1024]{1,0:T(8,128)(2,1)S(1)}, u32[]{:S(2)}, u32[]{:S(2)}) collective-permute-start(bf16[16,1024]{1,0:T(8,128)(2,1)S(1)} %slice.77), channel_id=1, source_target_pairs={{0,2},{1,3},{2,0},{3,1},{4,6},{5,7},{6,4},{7,5},{8,24},{9,25},{10,... | collective-permute-start | bytes 98312 | tf_op jit(solution)/shard_map/ppermute | solution.py:26
  48.8 4.1 %fusion.7 = bf16[1,2688,1024]{2,1,0:T(8,128)(2,1)} fusion(f32[256,2688]{1,0:T(8,128)S(1)} %fusion.14, bf16[128,2176]{1,0:T(8,128)(2,1)S(1)} %collective-permute-done.4, bf16[128,2176]{1,0:T(8,128)(2,1)S(1)} %pad_maximum_fusion, f32[256]{0:T(256)S(1)} %select_reduce_fusion), kind=kOutput, calls=%fused_computation.9 | convolution fusion | flops 1414987776 | bytes 9372672 | tf_op jit(solution)/shard_map/hr,rl->hl/dot_general | solution.py:72
  53.0 0.0 collective-permute-done.8
  53.0 2.9 %collective-permute-start.9 = (bf16[8,1024]{1,0:T(8,128)(2,1)S(1)}, bf16[8,1024]{1,0:T(8,128)(2,1)S(1)}, u32[]{:S(2)}, u32[]{:S(2)}) collective-permute-start(bf16[8,1024]{1,0:T(8,128)(2,1)S(1)} %slice.78), channel_id=1, source_target_pairs={{0,4},{1,5},{2,6},{3,7},{4,0},{5,1},{6,2},{7,3},{8,12},{9,13},{10,... | collective-permute-start | bytes 49160 | tf_op jit(solution)/shard_map/ppermute | solution.py:26
  55.9 4.1 %fusion.6 = bf16[1,2688,1024]{2,1,0:T(8,128)(2,1)} fusion(bf16[256,2688]{1,0:T(8,128)(2,1)S(1)} %fusion.17, bf16[128,2176]{1,0:T(8,128)(2,1)S(1)} %collective-permute-done.4, bf16[128,2176]{1,0:T(8,128)(2,1)S(1)} %pad_maximum_fusion), kind=kOutput, calls=%fused_computation.8 | convolution fusion | flops 1413087232 | bytes 7995392 | tf_op jit(solution)/shard_map/hr,rl->hl/dot_general | solution.py:69
  60.0 0.0 collective-permute-done.9
  60.0 0.6 %slice_add_fusion.3 = f32[8,1024]{1,0:T(8,128)} fusion(f32[16,1024]{1,0:T(8,128)S(1)} %slice_add_fusion.2, bf16[8,1024]{1,0:T(8,128)(2,1)S(1)} %collective-permute-done.9), kind=kLoop, calls=%fused_computation.34 | loop fusion | flops 16384 | bytes 81920 | tf_op jit(solution)/shard_map/add | solution.py:83
  (15 shorter events, 0.2 us)
Async XLA Ops:
  3.0 6.3 %collective-permute-start = (bf16[8,2176]{1,0:T(8,128)(2,1)S(1)}, bf16[8,2176]{1,0:T(8,128)(2,1)S(1)}, u32[]{:S(2)}, u32[]{:S(2)}) collective-permute-start(bf16[8,2176]{1,0:T(8,128)(2,1)S(1)} %pad_maximum_fusion.7), channel_id=1, source_target_pairs={{0,4},{1,5},{2,6},{3,7},{4,0},{5,1},{6,2},{7,3},{8,12},{9,13},{10,... | collective-permute-start | bytes 104456 | tf_op jit(solution)/shard_map/ppermute | solution.py:26
  9.4 4.3 %collective-permute-start.1 = (bf16[16,2176]{1,0:T(8,128)(2,1)S(1)}, bf16[16,2176]{1,0:T(8,128)(2,1)S(1)}, u32[]{:S(2)}, u32[]{:S(2)}) collective-permute-start(bf16[16,2176]{1,0:T(8,128)(2,1)S(1)} %pad_maximum_fusion.4), channel_id=1, source_target_pairs={{0,2},{1,3},{2,0},{3,1},{4,6},{5,7},{6,4},{7,5},{8,24},{9,25},{10,... | collective-permute-start | bytes 208904 | tf_op jit(solution)/shard_map/ppermute | solution.py:26
  13.7 5.1 %collective-permute-start.2 = (bf16[32,2176]{1,0:T(8,128)(2,1)S(1)}, bf16[32,2176]{1,0:T(8,128)(2,1)S(1)}, u32[]{:S(2)}, u32[]{:S(2)}) collective-permute-start(bf16[32,2176]{1,0:T(8,128)(2,1)S(1)} %pad_maximum_fusion.3), channel_id=1, source_target_pairs={{0,16},{1,17},{2,18},{3,19},{4,20},{5,21},{6,22},{7,23},{8,9},{9,8... | collective-permute-start | bytes 417800 | tf_op jit(solution)/shard_map/ppermute | solution.py:26
  18.8 6.6 %collective-permute-start.3 = (bf16[64,2176]{1,0:T(8,128)(2,1)S(1)}, bf16[64,2176]{1,0:T(8,128)(2,1)S(1)}, u32[]{:S(2)}, u32[]{:S(2)}) collective-permute-start(bf16[64,2176]{1,0:T(8,128)(2,1)S(1)} %pad_maximum_fusion.2), channel_id=1, source_target_pairs={{0,1},{1,0},{2,3},{3,2},{4,5},{5,4},{6,7},{7,6},{8,10},{9,11},{10,... | collective-permute-start | bytes 835592 | tf_op jit(solution)/shard_map/ppermute | solution.py:26
  25.5 2.0 %collective-permute-start.4 = (bf16[128,2176]{1,0:T(8,128)(2,1)S(1)}, bf16[128,2176]{1,0:T(8,128)(2,1)S(1)}, u32[]{:S(2)}, u32[]{:S(2)}) collective-permute-start(bf16[128,2176]{1,0:T(8,128)(2,1)S(1)} %pad_maximum_fusion), channel_id=1, source_target_pairs={{0,8},{1,9},{2,10},{3,11},{4,12},{5,13},{6,14},{7,15},{8,0},{9,1},... | collective-permute-start | bytes 1671176 | tf_op jit(solution)/shard_map/ppermute | solution.py:26
  25.6 6.3 %slice-start = ((s8[5505024]{0:T(1024)(128)(4,1)}), s8[4194304]{0:T(1024)(128)(4,1)S(1)}, s32[]{:S(2)}) async-start(s8[5505024]{0:T(1024)(128)(4,1)} %bitcast.24), calls=%async_computation | async-start | bytes 8388608
  25.6 6.3 %slice-start.1 = ((s8[5505024]{0:T(1024)(128)(4,1)}), s8[1310720]{0:T(1024)(128)(4,1)S(1)}, s32[]{:S(2)}) async-start(s8[5505024]{0:T(1024)(128)(4,1)} %bitcast.24), calls=%async_computation.1 | async-start | bytes 2621440
  31.8 2.2 %slice-start.2 = ((s8[5505024]{0:T(1024)(128)(4,1)}), s8[4194304]{0:T(1024)(128)(4,1)S(1)}, s32[]{:S(2)}) async-start(s8[5505024]{0:T(1024)(128)(4,1)} %bitcast.26), calls=%async_computation.2 | async-start | bytes 8388608
  31.9 2.5 %slice-start.3 = ((s8[5505024]{0:T(1024)(128)(4,1)}), s8[1310720]{0:T(1024)(128)(4,1)S(1)}, s32[]{:S(2)}) async-start(s8[5505024]{0:T(1024)(128)(4,1)} %bitcast.26), calls=%async_computation.3 | async-start | bytes 2621440
  36.1 1.6 %collective-permute-start.5 = (bf16[128,1024]{1,0:T(8,128)(2,1)S(1)}, bf16[128,1024]{1,0:T(8,128)(2,1)S(1)}, u32[]{:S(2)}, u32[]{:S(2)}) collective-permute-start(bf16[128,1024]{1,0:T(8,128)(2,1)S(1)} %slice.57), channel_id=1, source_target_pairs={{0,8},{1,9},{2,10},{3,11},{4,12},{5,13},{6,14},{7,15},{8,0},{9,1},... | collective-permute-start | bytes 786440 | tf_op jit(solution)/shard_map/ppermute | solution.py:26
  37.8 5.0 %collective-permute-start.6 = (bf16[64,1024]{1,0:T(8,128)(2,1)S(1)}, bf16[64,1024]{1,0:T(8,128)(2,1)S(1)}, u32[]{:S(2)}, u32[]{:S(2)}) collective-permute-start(bf16[64,1024]{1,0:T(8,128)(2,1)S(1)} %slice.75), channel_id=1, source_target_pairs={{0,1},{1,0},{2,3},{3,2},{4,5},{5,4},{6,7},{7,6},{8,10},{9,11},{10,... | collective-permute-start | bytes 393224 | tf_op jit(solution)/shard_map/ppermute | solution.py:26
  42.9 4.3 %collective-permute-start.7 = (bf16[32,1024]{1,0:T(8,128)(2,1)S(1)}, bf16[32,1024]{1,0:T(8,128)(2,1)S(1)}, u32[]{:S(2)}, u32[]{:S(2)}) collective-permute-start(bf16[32,1024]{1,0:T(8,128)(2,1)S(1)} %slice.76), channel_id=1, source_target_pairs={{0,16},{1,17},{2,18},{3,19},{4,20},{5,21},{6,22},{7,23},{8,9},{9,8... | collective-permute-start | bytes 196616 | tf_op jit(solution)/shard_map/ppermute | solution.py:26
  47.2 5.8 %collective-permute-start.8 = (bf16[16,1024]{1,0:T(8,128)(2,1)S(1)}, bf16[16,1024]{1,0:T(8,128)(2,1)S(1)}, u32[]{:S(2)}, u32[]{:S(2)}) collective-permute-start(bf16[16,1024]{1,0:T(8,128)(2,1)S(1)} %slice.77), channel_id=1, source_target_pairs={{0,2},{1,3},{2,0},{3,1},{4,6},{5,7},{6,4},{7,5},{8,24},{9,25},{10,... | collective-permute-start | bytes 98312 | tf_op jit(solution)/shard_map/ppermute | solution.py:26
  53.0 7.0 %collective-permute-start.9 = (bf16[8,1024]{1,0:T(8,128)(2,1)S(1)}, bf16[8,1024]{1,0:T(8,128)(2,1)S(1)}, u32[]{:S(2)}, u32[]{:S(2)}) collective-permute-start(bf16[8,1024]{1,0:T(8,128)(2,1)S(1)} %slice.78), channel_id=1, source_target_pairs={{0,4},{1,5},{2,6},{3,7},{4,0},{5,1},{6,2},{7,3},{8,12},{9,13},{10,... | collective-permute-start | bytes 49160 | tf_op jit(solution)/shard_map/ppermute | solution.py:26

commit v2 on v1

v2 whole, which is shorter than its diff:
```python
import jax
import jax.numpy as jnp
from jax import lax
from jax.experimental import pallas as pl
from jax.experimental.pallas import tpu as pltpu
from jax.sharding import PartitionSpec as P

HID = 2688
LANES = 128
AXES = ("group", "member")
BF16 = jnp.bfloat16
F32 = jnp.float32
VMEM = pl.BlockSpec(memory_space=pltpu.VMEM)
ANY = pl.BlockSpec(memory_space=pl.ANY)
HBM = pl.BlockSpec(memory_space=pltpu.HBM)
S = jax.ShapeDtypeStruct
tie = lax.optimization_barrier


def rounds(members, devices):
    bits = []
    bit = 1
    while bit < devices:
        if bit != members:
            bits.append(bit)
        bit *= 2
    far = members // 2
    rest = [b for b in bits if b != far]
    rest = rest[1:] + rest[:1]
    return [(far, far)] + list(zip(rest, rest[1:] + rest[:1]))


def swap(value, pair, core, devices):
    even, odd = pair
    pairs = [(i, i ^ (odd if i & core else even)) for i in range(devices)]
    return lax.ppermute(value, AXES, pairs)


def dot(a, b, on_a, on_b):
    return lax.dot_general(a, b, (((on_a,), (on_b,)), ((), ())), preferred_element_type=F32)


def call(kernel, out, ins, name, scratch=(), outs=None, flops=0, moved=0, limit=16, aliases={}):
    return pl.pallas_call(
        kernel,
        out_shape=out,
        in_specs=ins,
        out_specs=jax.tree.map(lambda _: VMEM, out) if outs is None else outs,
        scratch_shapes=scratch,
        name=name,
        input_output_aliases=aliases,
        compiler_params=pltpu.CompilerParams(vmem_limit_bytes=limit << 20),
        cost_estimate=pl.CostEstimate(flops=flops, bytes_accessed=moved, transcendentals=0),
    )


def pack_kernel(latent, out_grad, gates, ids, packed, latent_in, out_grad_in, gates_in, ids_in, sems):
    copies = [
        pltpu.make_async_copy(source, target, sems.at[k])
        for k, (source, target) in enumerate(
            ((ids, ids_in), (gates, gates_in), (latent, latent_in), (out_grad, out_grad_in))
        )
    ]
    for copy in copies:
        copy.start()
    copies[0].wait()
    copies[1].wait()
    rows, width = latent.shape
    lane = lax.broadcasted_iota(jnp.int32, (rows, LANES), 1)
    weight = gates_in[...].astype(F32)
    chosen = ids_in[...]
    dense = jnp.zeros(lane.shape, F32)
    for k in range(gates.shape[1]):
        dense += jnp.where(chosen[:, k : k + 1] == lane, weight[:, k : k + 1], 0.0)
    packed[:, 2 * width :] = dense.astype(BF16)
    copies[2].wait()
    packed[:, :width] = latent_in[...]
    copies[3].wait()
    packed[:, width : 2 * width] = out_grad_in[...]


def in_hbm(*arrays):
    return [pltpu.with_memory_space_constraint(array, pltpu.HBM) for array in arrays]


def pack(latent, out_grad, gates, ids):
    rows, width = latent.shape
    return call(pack_kernel, S((rows, 2 * width + LANES), BF16), [HBM] * 4, "pack",
        (pltpu.VMEM(latent.shape, BF16), pltpu.VMEM(out_grad.shape, BF16), pltpu.VMEM(gates.shape, BF16), pltpu.VMEM(ids.shape, jnp.int32),
         pltpu.SemaphoreType.DMA((4,))), limit=4)(*in_hbm(latent, out_grad, gates, ids))


def load_kernel(weight, out, sem):
    copy = pltpu.make_async_copy(weight, out, sem)
    copy.start()
    copy.wait()


def load(weight, name):
    return call(load_kernel, S(weight.shape, weight.dtype), [HBM], name, (pltpu.SemaphoreType.DMA,),
        moved=2 * weight.size, limit=8)(*in_hbm(weight))


def gated(dyg, width, rows):
    groups = lax.axis_size("group")
    local_experts = groups * rows // HID
    mine = lax.axis_index("member") * local_experts + lax.axis_index("group") // (groups // local_experts)
    gates = dyg[:, width:].astype(F32)
    lane = lax.broadcasted_iota(jnp.int32, gates.shape, 1)
    gate = jnp.sum(jnp.where(lane == mine, gates, 0.0), axis=1, keepdims=True)
    return (gate * dyg[:, :width].astype(F32)).astype(BF16)


def pre_kernel(x, w_up, relu):
    relu[...] = jnp.maximum(dot(x[...], w_up[...], 1, 1), 0.0)


def hidden_kernel(dyg, w_down, w_up, relu, row_grad, act, pre_grad, part):
    row_grad[...] = gated(dyg[...], row_grad.shape[1], w_down.shape[0])
    hid_grad = dot(row_grad[...], w_down[...], 1, 1)
    act[...] = (relu[...] * relu[...]).astype(BF16)
    pre_grad[...] = (hid_grad * 2.0 * relu[...]).astype(BF16)
    part[...] = dot(pre_grad[...], w_up[...], 1, 0).astype(BF16)


def plain(x, dyg, w_up, w_down):
    relu = jnp.maximum(dot(x, w_up, 1, 1), 0.0)
    row_grad = gated(dyg, x.shape[1], w_up.shape[0])
    act = (relu * relu).astype(BF16)
    pre_grad = (dot(row_grad, w_down, 1, 1) * 2.0 * relu).astype(BF16)
    return row_grad, act, pre_grad, dot(pre_grad, w_up, 1, 0).astype(BF16)


def outer(a, b, name, blocks, first=0, last=None, into=None):
    n, width = a.shape[1], b.shape[1]
    step = n // blocks
    last = blocks if last is None else last
    count = last - first

    def kernel(a, b, *refs):
        out, buffer, sems = refs[-3:]
        copies = []
        for k in range(count):
            at = (first + k) * step
            rows = pl.ds(k * step, step)
            buffer[rows] = dot(a[:, at : at + step], b[...], 0, 0).astype(BF16)
            copies.append(pltpu.make_async_copy(buffer.at[rows], out.at[0, pl.ds(at, step)], sems.at[k]))
            copies[-1].start()
        for copy in copies:
            copy.wait()

    args = (a, b) if into is None else (a, b, into)
    return call(kernel, S((1, n, width), BF16), [VMEM, VMEM] + [ANY] * (len(args) - 2), name,
        (pltpu.VMEM((count * step, width), BF16), pltpu.SemaphoreType.DMA((count,))), ANY,
        flops=2 * a.shape[0] * count * step * width, moved=2 * count * step * width,
        aliases={} if into is None else {2: 0})(*args)


def local(latent, out_grad, gates, expert_ids, up_weight, down_weight):
    width = latent.shape[1]
    rows = up_weight.shape[1]
    members = lax.axis_size("member")
    groups = lax.axis_size("group")
    devices = members * groups
    core = (members, members)
    plan = rounds(members, devices)
    tokens = latent.shape[0] * devices
    flops = 2 * tokens * rows * width
    small = tokens <= 256 and rows % 384 == 0
    blocks, cut = rows // 384, (4 * rows // 384 + 6) // 7
    w_up, w_down = up_weight[0], down_weight[0]

    packed = pack(latent, out_grad, gates, expert_ids)
    for k, pair in enumerate(plan[:-1]):
        if small and k == 1:
            packed, w_up = tie((packed, w_up))
        if small and k == 2:
            packed, w_down = tie((packed, w_down))
        got = swap(packed, pair, members, devices)
        if small and k == 1:
            w_up = load(w_up, "load_up")
            got, w_up = tie((got, w_up))
        if small and k == 2:
            w_down = load(w_down, "load_down")
            got, w_down = tie((got, w_down))
        packed = tie(jnp.concatenate([packed, got], axis=0))
    x, dyg = tie((packed[:, :width], packed[:, width:]))
    got_x = swap(x, plan[-1], members, devices)
    got_dyg = swap(dyg, plan[-1], members, devices)
    x = tie(jnp.concatenate([x, got_x], axis=0))
    x = jnp.concatenate([x, swap(x, core, members, devices)], axis=0)
    dyg = tie(jnp.concatenate([dyg, got_dyg], axis=0))
    x, dyg = tie((x, dyg))
    got_dyg = swap(dyg, core, members, devices)
    dyg_all = jnp.concatenate([dyg, got_dyg], axis=0)
    if small:
        relu = call(pre_kernel, S((tokens, rows), F32), [VMEM] * 2, "pre", flops=flops)(x, w_up)
        row_grad, act, pre_grad, part = call(
            hidden_kernel,
            (S((tokens, width), BF16), S((tokens, rows), BF16), S((tokens, rows), BF16), S((tokens, width), BF16)),
            [VMEM] * 4, "hidden", flops=2 * flops)(dyg_all, w_down, w_up, relu)
    else:
        row_grad, act, pre_grad, part = plain(x, dyg_all, w_up, w_down)

    half = tokens // 2
    total = part[:half].astype(F32) + swap(part[half:], core, members, devices).astype(F32)
    for k, pair in enumerate(reversed(plan)):
        half = total.shape[0] // 2
        got = swap(total[half:].astype(BF16), pair, members, devices)
        if small and k == 0:
            up_grad = outer(pre_grad, x, "up", blocks)
            got, up_grad = tie((got, up_grad))
        if small and k == 1:
            down_grad = outer(act, row_grad, "down", blocks, 0, cut)
            got, down_grad = tie((got, down_grad))
        if small and k == 2:
            down_grad = outer(act, row_grad, "down_rest", blocks, cut, blocks, down_grad)
            got, down_grad = tie((got, down_grad))
        total = total[:half] + got.astype(F32)
    if not small:
        up_grad = dot(pre_grad, x, 0, 0).astype(BF16)[None]
        down_grad = dot(act, row_grad, 0, 0).astype(BF16)[None]
    return (total, up_grad, down_grad)


def solution(mesh):
    rows = P(AXES, None)
    weights = P("member", "group", None)
    return jax.shard_map(
        local,
        mesh=mesh,
        in_specs=(rows, rows, rows, rows, weights, weights),
        out_specs=(rows, weights, weights),
        check_vma=False,
    )
```

time: 61 us -> 50.6 us (0.83)
  Pallas kernels: 0 us -> 18 us
  matrix products: 15.9 us -> 0 us
  waiting for transfers between devices: 22.3 us -> 13.4 us
  local copies, waits for them, and re-layouts: 2.31 us -> 0.08 us
  other arithmetic: 1.79 us -> 0.89 us
    pallas_call x0 -> x8, Pallas kernels: none -> 18 us  [the longest x3 6.78 us: outer(): call(kernel, S((1, n, width), BF16), [VMEM, VMEM] + [ANY] * (len(args) -...]
    dot_general x5 -> x0, matrix products: 15.9 us -> none  [the longest x1 4.25 us: local(): pre = jnp.einsum('rl,hl->hr', x, w_up, preferred_element_type=jnp.float32)]
    ppermute x10 -> x12, waiting for transfers between devices: 22.3 us -> 13.4 us  [swap(): return lax.ppermute(value, AXES, pairs)]
    unnamed x9 -> x0, local copies, waits for them, and re-layouts: 1.49 us -> none
    convert_element_type x1 -> x0, local copies, waits for them, and re-layouts: 0.77 us -> none  [local(): gates.astype(jnp.float32)[:, :, None]]
    concatenate x5 -> x7, other arithmetic: 0.83 us -> 0.17 us  [the longest x1 0.05 us: local(): dyg_all = jnp.concatenate([dyg, got_dyg], axis=0)]
    ppermute x10 -> x12, starting transfers between devices: 17.6 us -> 17.2 us  [swap(): return lax.ppermute(value, AXES, pairs)]
  transfers between devices with their start and end apart: 10 -> 12, of which waited for: 8 -> 10; matrix products, arithmetic and copies ran while one was open for 14% -> 0% of each run, Pallas kernels for 0% -> 27%
where the time goes in v2:
time: 50.6 us; the launch traced here: 50.4 us
  Pallas kernels  18 us (36%)
  starting transfers between devices  17.2 us (34%)
  waiting for transfers between devices  13.4 us (26%)
  other arithmetic  0.89 us (2%)
  between operations  0.84 us (2%)
    ppermute x12, starting transfers between devices, swap(): return lax.ppermute(value, AXES, pairs)  17.2 us
    ppermute x12, waiting for transfers between devices, swap(): return lax.ppermute(value, AXES, pairs)  13.4 us
    pallas_call x3, Pallas kernels, outer(): call(kernel, S((1, n, width), BF16), [VMEM, VMEM] + [ANY] * (len(args) -...  6.78 us
    pallas_call x2, Pallas kernels, load(): call(load_kernel, S(weight.shape, weight.dtype), [HBM], name, (pltpu.Sema...  5.14 us
    pallas_call x1, Pallas kernels, local(): call(hidden_kernel, (S((tokens, width), BF16), S((tokens, rows), BF16), S...  3.5 us
    pallas_call x1, Pallas kernels, local(): call(pre_kernel, S((tokens, rows), F32), [VMEM] * 2, 'pre', flops=flops)  1.69 us
  transfers between devices with their start and end apart: 12, of which 10 were waited for; matrix products, arithmetic and copies ran while one was open for 0% of the time, Pallas kernels for 27%

profile of v2, /device:TPU:0, one launch (start us, length us, event | category | flops | bytes accessed | tf_op | source)
XLA Modules:
  0.0 50.4 jit_solution(10109712285498950585)
XLA Ops:
  0.6 0.9 %pack.1 = bf16[8,2176]{1,0:T(8,128)(2,1)S(1)} custom-call(bf16[8,1024]{1,0:T(8,128)(2,1)} %latent.1, bf16[8,1024]{1,0:T(8,128)(2,1)} %out_grad.1, bf16[8,22]{1,0:T(8,128)(2,1)} %gates.1, s32[8,22]{1,0:T(8,128)} %ids.1), custom_call_target="tpu_custom_call" | custom-call | tf_op jit(solution)/shard_map/pack/pallas_call | solution.py:88
  1.5 4.1 %collective-permute-start = (bf16[8,2176]{1,0:T(8,128)(2,1)S(1)}, bf16[8,2176]{1,0:T(8,128)(2,1)S(1)}, u32[]{:S(2)}, u32[]{:S(2)}) collective-permute-start(bf16[8,2176]{1,0:T(8,128)(2,1)S(1)} %pack.1), channel_id=1, source_target_pairs={{0,4},{1,5},{2,6},{3,7},{4,0},{5,1},{6,2},{7,3},{8,12},{9,13},{10,... | collective-permute-start | bytes 104456 | tf_op jit(solution)/shard_map/ppermute | solution.py:36
  5.6 2.3 %collective-permute-done = bf16[8,2176]{1,0:T(8,128)(2,1)S(1)} collective-permute-done((bf16[8,2176]{1,0:T(8,128)(2,1)S(1)}, bf16[8,2176]{1,0:T(8,128)(2,1)S(1)}, u32[]{:S(2)}, u32[]{:S(2)}) %collective-permute-start) | collective-permute-done | bytes 34848 | tf_op jit(solution)/shard_map/ppermute | solution.py:36
  7.9 1.5 %collective-permute-start.1 = (bf16[16,2176]{1,0:T(8,128)(2,1)S(1)}, bf16[16,2176]{1,0:T(8,128)(2,1)S(1)}, u32[]{:S(2)}, u32[]{:S(2)}) collective-permute-start(bf16[16,2176]{1,0:T(8,128)(2,1)S(1)} %pad_maximum_fusion.6), channel_id=1, source_target_pairs={{0,2},{1,3},{2,0},{3,1},{4,6},{5,7},{6,4},{7,5},{8,24},{9,25},{10,... | collective-permute-start | bytes 208904 | tf_op jit(solution)/shard_map/ppermute | solution.py:36
  9.4 2.6 %load_up.1.w_up = bf16[2688,1024]{1,0:T(8,128)(2,1)S(1)} custom-call(bf16[2688,1024]{1,0:T(8,128)(2,1)} %bitcast.2), custom_call_target="tpu_custom_call" | custom-call | bytes 5505024 | tf_op jit(solution)/shard_map/load_up/pallas_call | solution.py:100
  12.0 0.2 collective-permute-done.1
  12.2 1.8 %collective-permute-start.2 = (bf16[32,2176]{1,0:T(8,128)(2,1)S(1)}, bf16[32,2176]{1,0:T(8,128)(2,1)S(1)}, u32[]{:S(2)}, u32[]{:S(2)}) collective-permute-start(bf16[32,2176]{1,0:T(8,128)(2,1)S(1)} %pad_maximum_fusion.5), channel_id=1, source_target_pairs={{0,16},{1,17},{2,18},{3,19},{4,20},{5,21},{6,22},{7,23},{8,9},{9,8... | collective-permute-start | bytes 417800 | tf_op jit(solution)/shard_map/ppermute | solution.py:36
  14.0 2.6 %load_down.1.w_down = bf16[2688,1024]{1,0:T(8,128)(2,1)S(1)} custom-call(bf16[2688,1024]{1,0:T(8,128)(2,1)} %bitcast.3), custom_call_target="tpu_custom_call" | custom-call | bytes 5505024 | tf_op jit(solution)/shard_map/load_down/pallas_call | solution.py:100
  16.6 0.8 %collective-permute-done.2 = bf16[32,2176]{1,0:T(8,128)(2,1)S(1)} collective-permute-done((bf16[32,2176]{1,0:T(8,128)(2,1)S(1)}, bf16[32,2176]{1,0:T(8,128)(2,1)S(1)}, u32[]{:S(2)}, u32[]{:S(2)}) %collective-permute-start.2) | collective-permute-done | bytes 139296 | tf_op jit(solution)/shard_map/ppermute | solution.py:36
  17.4 1.8 %collective-permute-start.3 = (bf16[64,1024]{1,0:T(8,128)(2,1)S(1)}, bf16[64,1024]{1,0:T(8,128)(2,1)S(1)}, u32[]{:S(2)}, u32[]{:S(2)}) collective-permute-start(bf16[64,1024]{1,0:T(8,128)(2,1)S(1)} %slice.52), channel_id=1, source_target_pairs={{0,1},{1,0},{2,3},{3,2},{4,5},{5,4},{6,7},{7,6},{8,10},{9,11},{10,... | collective-permute-start | bytes 393224 | tf_op jit(solution)/shard_map/ppermute | solution.py:36
  19.2 0.3 collective-permute-start.5
  19.5 2.9 %collective-permute-done.3 = bf16[64,1024]{1,0:T(8,128)(2,1)S(1)} collective-permute-done((bf16[64,1024]{1,0:T(8,128)(2,1)S(1)}, bf16[64,1024]{1,0:T(8,128)(2,1)S(1)}, u32[]{:S(2)}, u32[]{:S(2)}) %collective-permute-start.3) | collective-permute-done | bytes 131104 | tf_op jit(solution)/shard_map/ppermute | solution.py:36
  22.5 0.1 collective-permute-start.4
  22.6 1.8 %collective-permute-done.5 = bf16[64,1152]{1,0:T(8,128)(2,1)S(1)} collective-permute-done((bf16[64,1152]{1,0:T(8,128)(2,1)S(1)}, bf16[64,1152]{1,0:T(8,128)(2,1)S(1)}, u32[]{:S(2)}, u32[]{:S(2)}) %collective-permute-start.5) | collective-permute-done | bytes 147488 | tf_op jit(solution)/shard_map/ppermute | solution.py:36
  24.4 0.0 collective-permute-done.4
  24.4 0.1 collective-permute-start.6
  24.5 1.7 %pre.1.relu = f32[256,2688]{1,0:T(8,128)S(1)} custom-call(bf16[256,1024]{1,0:T(8,128)(2,1)S(1)} %pad_maximum_fusion.1.x.b, bf16[2688,1024]{1,0:T(8,128)(2,1)S(1)} %load_up.1.w_up), custom_call_target="tpu_custom_call" | custom-call | flops 1409286144 | tf_op jit(solution)/shard_map/pre/pallas_call | solution.py:197
  26.2 0.0 collective-permute-done.6
  26.3 3.5 %hidden.1 = (bf16[256,1024]{1,0:T(8,128)(2,1)S(1)}, bf16[256,2688]{1,0:T(8,128)(2,1)S(1)}, bf16[256,2688]{1,0:T(8,128)(2,1)S(1)}, bf16[256,1024]{1,0:T(8,128)(2,1)S(1)}) custom-call(bf16[256,1152]{1,0:T(8,128)(2,1)S(1)} %pad_maximum_fusion.dyg, bf16[2688,1024]{1,0:T(8,128)(2,1)S(1)} %load_down.1.w_down, bf16[2688,1024]{1,0:T(8,128)(2,1)S(1)} %load_up.1.w_up, ...), custom_call_target="tpu_custom_call" | custom-call | flops 2818572288 | tf_op jit(solution)/shard_map/hidden/pallas_call | solution.py:198
  29.8 0.6 %collective-permute-start.7 = (bf16[128,1024]{1,0:T(8,128)(2,1)S(1)}, bf16[128,1024]{1,0:T(8,128)(2,1)S(1)}, u32[]{:S(2)}, u32[]{:S(2)}) collective-permute-start(bf16[128,1024]{1,0:T(8,128)(2,1)S(1)} %slice.43), channel_id=1, source_target_pairs={{0,8},{1,9},{2,10},{3,11},{4,12},{5,13},{6,14},{7,15},{8,0},{9,1},... | collective-permute-start | bytes 786440 | tf_op jit(solution)/shard_map/ppermute | solution.py:36
  30.4 1.2 %collective-permute-done.7 = bf16[128,1024]{1,0:T(8,128)(2,1)S(1)} collective-permute-done((bf16[128,1024]{1,0:T(8,128)(2,1)S(1)}, bf16[128,1024]{1,0:T(8,128)(2,1)S(1)}, u32[]{:S(2)}, u32[]{:S(2)}) %collective-permute-start.7) | collective-permute-done | bytes 262176 | tf_op jit(solution)/shard_map/ppermute | solution.py:36
  31.5 0.1 convert_add_fusion
  31.6 1.5 %collective-permute-start.8 = (bf16[64,1024]{1,0:T(8,128)(2,1)S(1)}, bf16[64,1024]{1,0:T(8,128)(2,1)S(1)}, u32[]{:S(2)}, u32[]{:S(2)}) collective-permute-start(bf16[64,1024]{1,0:T(8,128)(2,1)S(1)} %slice.71), channel_id=1, source_target_pairs={{0,1},{1,0},{2,3},{3,2},{4,5},{5,4},{6,7},{7,6},{8,10},{9,11},{10,... | collective-permute-start | bytes 393224 | tf_op jit(solution)/shard_map/ppermute | solution.py:36
  33.1 2.9 %up.1 = bf16[1,2688,1024]{2,1,0:T(8,128)(2,1)} custom-call(bf16[256,2688]{1,0:T(8,128)(2,1)S(1)} %get-tuple-element.38.a, bf16[256,1024]{1,0:T(8,128)(2,1)S(1)} %pad_maximum_fusion.1.x.b), custom_call_target="tpu_custom_call" | custom-call | flops 1409286144 | bytes 5505024 | tf_op jit(solution)/shard_map/up/pallas_call | solution.py:153
  36.0 0.7 %collective-permute-done.8 = bf16[64,1024]{1,0:T(8,128)(2,1)S(1)} collective-permute-done((bf16[64,1024]{1,0:T(8,128)(2,1)S(1)}, bf16[64,1024]{1,0:T(8,128)(2,1)S(1)}, u32[]{:S(2)}, u32[]{:S(2)}) %collective-permute-start.8) | collective-permute-done | bytes 131104 | tf_op jit(solution)/shard_map/ppermute | solution.py:36
  36.7 1.6 %collective-permute-start.9 = (bf16[32,1024]{1,0:T(8,128)(2,1)S(1)}, bf16[32,1024]{1,0:T(8,128)(2,1)S(1)}, u32[]{:S(2)}, u32[]{:S(2)}) collective-permute-start(bf16[32,1024]{1,0:T(8,128)(2,1)S(1)} %slice.72), channel_id=1, source_target_pairs={{0,16},{1,17},{2,18},{3,19},{4,20},{5,21},{6,22},{7,23},{8,9},{9,8... | collective-permute-start | bytes 196616 | tf_op jit(solution)/shard_map/ppermute | solution.py:36
  38.3 2.1 %down.1.refs_0_ = bf16[1,2688,1024]{2,1,0:T(8,128)(2,1)} custom-call(bf16[256,2688]{1,0:T(8,128)(2,1)S(1)} %get-tuple-element.40.a, bf16[256,1024]{1,0:T(8,128)(2,1)S(1)} %get-tuple-element.41.b), custom_call_target="tpu_custom_call" | custom-call | flops 805306368 | bytes 3145728 | tf_op jit(solution)/shard_map/down/pallas_call | solution.py:153
  40.4 0.7 %collective-permute-done.9 = bf16[32,1024]{1,0:T(8,128)(2,1)S(1)} collective-permute-done((bf16[32,1024]{1,0:T(8,128)(2,1)S(1)}, bf16[32,1024]{1,0:T(8,128)(2,1)S(1)}, u32[]{:S(2)}, u32[]{:S(2)}) %collective-permute-start.9) | collective-permute-done | bytes 65568 | tf_op jit(solution)/shard_map/ppermute | solution.py:36
  41.1 1.4 %collective-permute-start.10 = (bf16[16,1024]{1,0:T(8,128)(2,1)S(1)}, bf16[16,1024]{1,0:T(8,128)(2,1)S(1)}, u32[]{:S(2)}, u32[]{:S(2)}) collective-permute-start(bf16[16,1024]{1,0:T(8,128)(2,1)S(1)} %slice.73), channel_id=1, source_target_pairs={{0,2},{1,3},{2,0},{3,1},{4,6},{5,7},{6,4},{7,5},{8,24},{9,25},{10,... | collective-permute-start | bytes 98312 | tf_op jit(solution)/shard_map/ppermute | solution.py:36
  42.4 1.8 %down_rest.1 = bf16[1,2688,1024]{2,1,0:T(8,128)(2,1)} custom-call(bf16[256,2688]{1,0:T(8,128)(2,1)S(1)} %get-tuple-element.40.a, bf16[256,1024]{1,0:T(8,128)(2,1)S(1)} %get-tuple-element.41.b, bf16[1,2688,1024]{2,1,0:T(8,128)(2,1)} %down.1.refs_0_), custom_call_target="tpu_custom_call", output_to_operand_aliasing={{}: (2, {})} | custom-call | flops 603979776 | bytes 2359296 | tf_op jit(solution)/shard_map/down_rest/pallas_call | solution.py:153
  44.3 0.8 %collective-permute-done.10 = bf16[16,1024]{1,0:T(8,128)(2,1)S(1)} collective-permute-done((bf16[16,1024]{1,0:T(8,128)(2,1)S(1)}, bf16[16,1024]{1,0:T(8,128)(2,1)S(1)}, u32[]{:S(2)}, u32[]{:S(2)}) %collective-permute-start.10) | collective-permute-done | bytes 32800 | tf_op jit(solution)/shard_map/ppermute | solution.py:36
  45.1 2.5 %collective-permute-start.11 = (bf16[8,1024]{1,0:T(8,128)(2,1)S(1)}, bf16[8,1024]{1,0:T(8,128)(2,1)S(1)}, u32[]{:S(2)}, u32[]{:S(2)}) collective-permute-start(bf16[8,1024]{1,0:T(8,128)(2,1)S(1)} %slice.74), channel_id=1, source_target_pairs={{0,4},{1,5},{2,6},{3,7},{4,0},{5,1},{6,2},{7,3},{8,12},{9,13},{10,... | collective-permute-start | bytes 49160 | tf_op jit(solution)/shard_map/ppermute | solution.py:36
  47.6 2.2 %collective-permute-done.11 = bf16[8,1024]{1,0:T(8,128)(2,1)S(1)} collective-permute-done((bf16[8,1024]{1,0:T(8,128)(2,1)S(1)}, bf16[8,1024]{1,0:T(8,128)(2,1)S(1)}, u32[]{:S(2)}, u32[]{:S(2)}) %collective-permute-start.11) | collective-permute-done | bytes 16416 | tf_op jit(solution)/shard_map/ppermute | solution.py:36
  49.8 0.6 %slice_add_fusion.3 = f32[8,1024]{1,0:T(8,128)} fusion(f32[16,1024]{1,0:T(8,128)S(1)} %slice_add_fusion.2, bf16[8,1024]{1,0:T(8,128)(2,1)S(1)} %collective-permute-done.11), kind=kLoop, calls=%fused_computation.15 | loop fusion | flops 16384 | bytes 81920 | tf_op jit(solution)/shard_map/add | solution.py:219
  (17 shorter events, 0.3 us)
Async XLA Ops:
  1.5 6.4 %collective-permute-start = (bf16[8,2176]{1,0:T(8,128)(2,1)S(1)}, bf16[8,2176]{1,0:T(8,128)(2,1)S(1)}, u32[]{:S(2)}, u32[]{:S(2)}) collective-permute-start(bf16[8,2176]{1,0:T(8,128)(2,1)S(1)} %pack.1), channel_id=1, source_target_pairs={{0,4},{1,5},{2,6},{3,7},{4,0},{5,1},{6,2},{7,3},{8,12},{9,13},{10,... | collective-permute-start | bytes 104456 | tf_op jit(solution)/shard_map/ppermute | solution.py:36
  7.9 4.3 %collective-permute-start.1 = (bf16[16,2176]{1,0:T(8,128)(2,1)S(1)}, bf16[16,2176]{1,0:T(8,128)(2,1)S(1)}, u32[]{:S(2)}, u32[]{:S(2)}) collective-permute-start(bf16[16,2176]{1,0:T(8,128)(2,1)S(1)} %pad_maximum_fusion.6), channel_id=1, source_target_pairs={{0,2},{1,3},{2,0},{3,1},{4,6},{5,7},{6,4},{7,5},{8,24},{9,25},{10,... | collective-permute-start | bytes 208904 | tf_op jit(solution)/shard_map/ppermute | solution.py:36
  12.2 5.1 %collective-permute-start.2 = (bf16[32,2176]{1,0:T(8,128)(2,1)S(1)}, bf16[32,2176]{1,0:T(8,128)(2,1)S(1)}, u32[]{:S(2)}, u32[]{:S(2)}) collective-permute-start(bf16[32,2176]{1,0:T(8,128)(2,1)S(1)} %pad_maximum_fusion.5), channel_id=1, source_target_pairs={{0,16},{1,17},{2,18},{3,19},{4,20},{5,21},{6,22},{7,23},{8,9},{9,8... | collective-permute-start | bytes 417800 | tf_op jit(solution)/shard_map/ppermute | solution.py:36
  17.4 5.0 %collective-permute-start.3 = (bf16[64,1024]{1,0:T(8,128)(2,1)S(1)}, bf16[64,1024]{1,0:T(8,128)(2,1)S(1)}, u32[]{:S(2)}, u32[]{:S(2)}) collective-permute-start(bf16[64,1024]{1,0:T(8,128)(2,1)S(1)} %slice.52), channel_id=1, source_target_pairs={{0,1},{1,0},{2,3},{3,2},{4,5},{5,4},{6,7},{7,6},{8,10},{9,11},{10,... | collective-permute-start | bytes 393224 | tf_op jit(solution)/shard_map/ppermute | solution.py:36
  19.2 5.1 %collective-permute-start.5 = (bf16[64,1152]{1,0:T(8,128)(2,1)S(1)}, bf16[64,1152]{1,0:T(8,128)(2,1)S(1)}, u32[]{:S(2)}, u32[]{:S(2)}) collective-permute-start(bf16[64,1152]{1,0:T(8,128)(2,1)S(1)} %slice.53), channel_id=1, source_target_pairs={{0,1},{1,0},{2,3},{3,2},{4,5},{5,4},{6,7},{7,6},{8,10},{9,11},{10,... | collective-permute-start | bytes 442376 | tf_op jit(solution)/shard_map/ppermute | solution.py:36
  22.5 1.9 %collective-permute-start.4 = (bf16[128,1024]{1,0:T(8,128)(2,1)S(1)}, bf16[128,1024]{1,0:T(8,128)(2,1)S(1)}, u32[]{:S(2)}, u32[]{:S(2)}) collective-permute-start(bf16[128,1024]{1,0:T(8,128)(2,1)S(1)} %pad_maximum_fusion.4), channel_id=1, source_target_pairs={{0,8},{1,9},{2,10},{3,11},{4,12},{5,13},{6,14},{7,15},{8,0},{9,1},... | collective-permute-start | bytes 786440 | tf_op jit(solution)/shard_map/ppermute | solution.py:36
  24.4 1.8 %collective-permute-start.6 = (bf16[128,1152]{1,0:T(8,128)(2,1)S(1)}, bf16[128,1152]{1,0:T(8,128)(2,1)S(1)}, u32[]{:S(2)}, u32[]{:S(2)}) collective-permute-start(bf16[128,1152]{1,0:T(8,128)(2,1)S(1)} %pad_maximum_fusion.2), channel_id=1, source_target_pairs={{0,8},{1,9},{2,10},{3,11},{4,12},{5,13},{6,14},{7,15},{8,0},{9,1},... | collective-permute-start | bytes 884744 | tf_op jit(solution)/shard_map/ppermute | solution.py:36
  29.8 1.7 %collective-permute-start.7 = (bf16[128,1024]{1,0:T(8,128)(2,1)S(1)}, bf16[128,1024]{1,0:T(8,128)(2,1)S(1)}, u32[]{:S(2)}, u32[]{:S(2)}) collective-permute-start(bf16[128,1024]{1,0:T(8,128)(2,1)S(1)} %slice.43), channel_id=1, source_target_pairs={{0,8},{1,9},{2,10},{3,11},{4,12},{5,13},{6,14},{7,15},{8,0},{9,1},... | collective-permute-start | bytes 786440 | tf_op jit(solution)/shard_map/ppermute | solution.py:36
  31.6 5.0 %collective-permute-start.8 = (bf16[64,1024]{1,0:T(8,128)(2,1)S(1)}, bf16[64,1024]{1,0:T(8,128)(2,1)S(1)}, u32[]{:S(2)}, u32[]{:S(2)}) collective-permute-start(bf16[64,1024]{1,0:T(8,128)(2,1)S(1)} %slice.71), channel_id=1, source_target_pairs={{0,1},{1,0},{2,3},{3,2},{4,5},{5,4},{6,7},{7,6},{8,10},{9,11},{10,... | collective-permute-start | bytes 393224 | tf_op jit(solution)/shard_map/ppermute | solution.py:36
  36.7 4.3 %collective-permute-start.9 = (bf16[32,1024]{1,0:T(8,128)(2,1)S(1)}, bf16[32,1024]{1,0:T(8,128)(2,1)S(1)}, u32[]{:S(2)}, u32[]{:S(2)}) collective-permute-start(bf16[32,1024]{1,0:T(8,128)(2,1)S(1)} %slice.72), channel_id=1, source_target_pairs={{0,16},{1,17},{2,18},{3,19},{4,20},{5,21},{6,22},{7,23},{8,9},{9,8... | collective-permute-start | bytes 196616 | tf_op jit(solution)/shard_map/ppermute | solution.py:36
  41.1 4.0 %collective-permute-start.10 = (bf16[16,1024]{1,0:T(8,128)(2,1)S(1)}, bf16[16,1024]{1,0:T(8,128)(2,1)S(1)}, u32[]{:S(2)}, u32[]{:S(2)}) collective-permute-start(bf16[16,1024]{1,0:T(8,128)(2,1)S(1)} %slice.73), channel_id=1, source_target_pairs={{0,2},{1,3},{2,0},{3,1},{4,6},{5,7},{6,4},{7,5},{8,24},{9,25},{10,... | collective-permute-start | bytes 98312 | tf_op jit(solution)/shard_map/ppermute | solution.py:36
  45.1 4.7 %collective-permute-start.11 = (bf16[8,1024]{1,0:T(8,128)(2,1)S(1)}, bf16[8,1024]{1,0:T(8,128)(2,1)S(1)}, u32[]{:S(2)}, u32[]{:S(2)}) collective-permute-start(bf16[8,1024]{1,0:T(8,128)(2,1)S(1)} %slice.74), channel_id=1, source_target_pairs={{0,4},{1,5},{2,6},{3,7},{4,0},{5,1},{6,2},{7,3},{8,12},{9,13},{10,... | collective-permute-start | bytes 49160 | tf_op jit(solution)/shard_map/ppermute | solution.py:36

commit v3 on v2

--- a/solution.py
+++ b/solution.py
@@ -17,23 +17,15 @@
 tie = lax.optimization_barrier
 
 
-def rounds(members, devices):
-    bits = []
-    bit = 1
-    while bit < devices:
-        if bit != members:
-            bits.append(bit)
-        bit *= 2
-    far = members // 2
-    rest = [b for b in bits if b != far]
-    rest = rest[1:] + rest[:1]
-    return [(far, far)] + list(zip(rest, rest[1:] + rest[:1]))
-
-
-def swap(value, pair, core, devices):
-    even, odd = pair
-    pairs = [(i, i ^ (odd if i & core else even)) for i in range(devices)]
-    return lax.ppermute(value, AXES, pairs)
+def stages(members, devices):
+    bits = [1 << k for k in range(1, devices.bit_length() - 1)]
+    bits = [b for b in bits if b < members] + [1] + [b for b in bits if b > members]
+    pairs = [bits[k : k + 2] for k in range(0, len(bits), 2)]
+    return [pair if len(pair) == 1 else [pair[0], pair[1], pair[0] ^ pair[1]] for pair in pairs]
+
+
+def swap(value, mask, devices):
+    return lax.ppermute(value, AXES, [(i, i ^ mask) for i in range(devices)])
 
 
 def dot(a, b, on_a, on_b):
@@ -162,36 +154,31 @@
     members = lax.axis_size("member")
     groups = lax.axis_size("group")
     devices = members * groups
-    core = (members, members)
-    plan = rounds(members, devices)
+    core = members
+    plan = stages(members, devices)
     tokens = latent.shape[0] * devices
     flops = 2 * tokens * rows * width
     small = tokens <= 256 and rows % 384 == 0
-    blocks, cut = rows // 384, (4 * rows // 384 + 6) // 7
+    blocks = rows // 384
     w_up, w_down = up_weight[0], down_weight[0]
 
-    packed = pack(latent, out_grad, gates, expert_ids)
-    for k, pair in enumerate(plan[:-1]):
+    rows_all = pack(latent, out_grad, gates, expert_ids)
+    for k, masks in enumerate(plan):
+        if small and k == 0:
+            rows_all, w_up = tie((rows_all, w_up))
         if small and k == 1:
-            packed, w_up = tie((packed, w_up))
-        if small and k == 2:
-            packed, w_down = tie((packed, w_down))
-        got = swap(packed, pair, members, devices)
+            rows_all, w_down = tie((rows_all, w_down))
+        got = [swap(rows_all, mask, devices) for mask in masks]
+        if small and k == 0:
+            w_up = load(w_up, "load_up")
+            got[0], w_up = tie((got[0], w_up))
         if small and k == 1:
-            w_up = load(w_up, "load_up")
-            got, w_up = tie((got, w_up))
-        if small and k == 2:
             w_down = load(w_down, "load_down")
-            got, w_down = tie((got, w_down))
-        packed = tie(jnp.concatenate([packed, got], axis=0))
-    x, dyg = tie((packed[:, :width], packed[:, width:]))
-    got_x = swap(x, plan[-1], members, devices)
-    got_dyg = swap(dyg, plan[-1], members, devices)
-    x = tie(jnp.concatenate([x, got_x], axis=0))
-    x = jnp.concatenate([x, swap(x, core, members, devices)], axis=0)
-    dyg = tie(jnp.concatenate([dyg, got_dyg], axis=0))
-    x, dyg = tie((x, dyg))
-    got_dyg = swap(dyg, core, members, devices)
+            got[0], w_down = tie((got[0], w_down))
+        rows_all = tie(jnp.concatenate([rows_all] + got, axis=0))
+    x, dyg = tie((rows_all[:, :width], rows_all[:, width:]))
+    x = jnp.concatenate([x, swap(x, core, devices)], axis=0)
+    got_dyg = swap(dyg, core, devices)
     dyg_all = jnp.concatenate([dyg, got_dyg], axis=0)
     if small:
         relu = call(pre_kernel, S((tokens, rows), F32), [VMEM] * 2, "pre", flops=flops)(x, w_up)
@@ -203,20 +190,18 @@
         row_grad, act, pre_grad, part = plain(x, dyg_all, w_up, w_down)
 
     half = tokens // 2
-    total = part[:half].astype(F32) + swap(part[half:], core, members, devices).astype(F32)
-    for k, pair in enumerate(reversed(plan)):
-        half = total.shape[0] // 2
-        got = swap(total[half:].astype(BF16), pair, members, devices)
+    total = part[:half].astype(F32) + swap(part[half:], core, devices).astype(F32)
+    for k, masks in enumerate(reversed(plan)):
+        count = total.shape[0] // (len(masks) + 1)
+        cut = [total[j * count : (j + 1) * count] for j in range(len(masks) + 1)]
+        got = [swap(block.astype(BF16), mask, devices) for block, mask in zip(cut[1:], masks)]
         if small and k == 0:
             up_grad = outer(pre_grad, x, "up", blocks)
-            got, up_grad = tie((got, up_grad))
+            got[0], up_grad = tie((got[0], up_grad))
         if small and k == 1:
-            down_grad = outer(act, row_grad, "down", blocks, 0, cut)
-            got, down_grad = tie((got, down_grad))
-        if small and k == 2:
-            down_grad = outer(act, row_grad, "down_rest", blocks, cut, blocks, down_grad)
-            got, down_grad = tie((got, down_grad))
-        total = total[:half] + got.astype(F32)
+            down_grad = outer(act, row_grad, "down", blocks)
+            got[0], down_grad = tie((got[0], down_grad))
+        total = cut[0] + sum(block.astype(F32) for block in got)
     if not small:
         up_grad = dot(pre_grad, x, 0, 0).astype(BF16)[None]
         down_grad = dot(act, row_grad, 0, 0).astype(BF16)[None]

time: 50.6 us -> 45.6 us (0.901)
  waiting for transfers between devices: 13.4 us -> 9.56 us
  Pallas kernels: 18 us -> 17 us
    ppermute x12 -> x15, waiting for transfers between devices: 13.4 us -> 9.56 us  [swap(): return lax.ppermute(value, AXES, [(i, i ^ mask) for i in range(devices)])]
    pallas_call x3 -> x2, Pallas kernels: 6.78 us -> 5.77 us  [outer(): call(kernel, S((1, n, width), BF16), [VMEM, VMEM] + [ANY] * (len(args) -...]
    ppermute x12 -> x15, starting transfers between devices: 17.2 us -> 17.1 us  [swap(): return lax.ppermute(value, AXES, [(i, i ^ mask) for i in range(devices)])]
  transfers between devices with their start and end apart: 12 -> 15, of which waited for: 10 -> 10; matrix products, arithmetic and copies ran while one was open for 0% -> 0% of each run, Pallas kernels for 27% -> 28%
where the time goes in v3:
time: 45.6 us; the launch traced here: 45.4 us
  starting transfers between devices  17.1 us (38%)
  Pallas kernels  17 us (37%)
  waiting for transfers between devices  9.56 us (21%)
  other arithmetic  0.83 us (2%)
  between operations  0.82 us (2%)
    ppermute x15, starting transfers between devices, swap(): return lax.ppermute(value, AXES, [(i, i ^ mask) for i in range(devices)])  17.1 us
    ppermute x15, waiting for transfers between devices, swap(): return lax.ppermute(value, AXES, [(i, i ^ mask) for i in range(devices)])  9.56 us
    pallas_call x2, Pallas kernels, outer(): call(kernel, S((1, n, width), BF16), [VMEM, VMEM] + [ANY] * (len(args) -...  5.77 us
    pallas_call x2, Pallas kernels, load(): call(load_kernel, S(weight.shape, weight.dtype), [HBM], name, (pltpu.Sema...  5.14 us
    pallas_call x1, Pallas kernels, local(): call(hidden_kernel, (S((tokens, width), BF16), S((tokens, rows), BF16), S...  3.5 us
    pallas_call x1, Pallas kernels, local(): call(pre_kernel, S((tokens, rows), F32), [VMEM] * 2, 'pre', flops=flops)  1.69 us
  transfers between devices with their start and end apart: 15, of which 10 were waited for; matrix products, arithmetic and copies ran while one was open for 0% of the time, Pallas kernels for 28%

profile of v3, /device:TPU:0, one launch (start us, length us, event | category | flops | bytes accessed | tf_op | source)
XLA Modules:
  0.0 45.4 jit_solution(9805376833798552772)
XLA Ops:
  0.6 0.9 %pack.1 = bf16[8,2176]{1,0:T(8,128)(2,1)S(1)} custom-call(bf16[8,1024]{1,0:T(8,128)(2,1)} %latent.1, bf16[8,1024]{1,0:T(8,128)(2,1)} %out_grad.1, bf16[8,22]{1,0:T(8,128)(2,1)} %gates.1, s32[8,22]{1,0:T(8,128)} %ids.1), custom_call_target="tpu_custom_call" | custom-call | tf_op jit(solution)/shard_map/pack/pallas_call | solution.py:80
  1.5 3.1 %collective-permute-start = (bf16[8,2176]{1,0:T(8,128)(2,1)S(1)}, bf16[8,2176]{1,0:T(8,128)(2,1)S(1)}, u32[]{:S(2)}, u32[]{:S(2)}) collective-permute-start(bf16[8,2176]{1,0:T(8,128)(2,1)S(1)} %pack.1), channel_id=1, source_target_pairs={{0,2},{1,3},{2,0},{3,1},{4,6},{5,7},{6,4},{7,5},{8,10},{9,11},{10,... | collective-permute-start | bytes 104456 | tf_op jit(solution)/shard_map/ppermute | solution.py:28
  4.6 2.5 %collective-permute-start.2 = (bf16[8,2176]{1,0:T(8,128)(2,1)S(1)}, bf16[8,2176]{1,0:T(8,128)(2,1)S(1)}, u32[]{:S(2)}, u32[]{:S(2)}) collective-permute-start(bf16[8,2176]{1,0:T(8,128)(2,1)S(1)} %pack.1), channel_id=1, source_target_pairs={{0,6},{1,7},{2,4},{3,5},{4,2},{5,3},{6,0},{7,1},{8,14},{9,15},{10,... | collective-permute-start | bytes 104456 | tf_op jit(solution)/shard_map/ppermute | solution.py:28
  7.1 0.1 collective-permute-start.1
  7.2 2.6 %load_up.1.w_up = bf16[2688,1024]{1,0:T(8,128)(2,1)S(1)} custom-call(bf16[2688,1024]{1,0:T(8,128)(2,1)} %bitcast.2), custom_call_target="tpu_custom_call" | custom-call | bytes 5505024 | tf_op jit(solution)/shard_map/load_up/pallas_call | solution.py:92
  9.8 0.0 collective-permute-done
  9.8 1.0 %collective-permute-done.2 = bf16[8,2176]{1,0:T(8,128)(2,1)S(1)} collective-permute-done((bf16[8,2176]{1,0:T(8,128)(2,1)S(1)}, bf16[8,2176]{1,0:T(8,128)(2,1)S(1)}, u32[]{:S(2)}, u32[]{:S(2)}) %collective-permute-start.2) | collective-permute-done | bytes 34848 | tf_op jit(solution)/shard_map/ppermute | solution.py:28
  10.8 1.5 %collective-permute-done.1 = bf16[8,2176]{1,0:T(8,128)(2,1)S(1)} collective-permute-done((bf16[8,2176]{1,0:T(8,128)(2,1)S(1)}, bf16[8,2176]{1,0:T(8,128)(2,1)S(1)}, u32[]{:S(2)}, u32[]{:S(2)}) %collective-permute-start.1) | collective-permute-done | bytes 34848 | tf_op jit(solution)/shard_map/ppermute | solution.py:28
  12.3 1.6 %collective-permute-start.3 = (bf16[32,2176]{1,0:T(8,128)(2,1)S(1)}, bf16[32,2176]{1,0:T(8,128)(2,1)S(1)}, u32[]{:S(2)}, u32[]{:S(2)}) collective-permute-start(bf16[32,2176]{1,0:T(8,128)(2,1)S(1)} %pad_maximum_fusion.2), channel_id=1, source_target_pairs={{0,1},{1,0},{2,3},{3,2},{4,5},{5,4},{6,7},{7,6},{8,9},{9,8},{10,11... | collective-permute-start | bytes 417800 | tf_op jit(solution)/shard_map/ppermute | solution.py:28
  13.9 1.5 %collective-permute-start.5 = (bf16[32,2176]{1,0:T(8,128)(2,1)S(1)}, bf16[32,2176]{1,0:T(8,128)(2,1)S(1)}, u32[]{:S(2)}, u32[]{:S(2)}) collective-permute-start(bf16[32,2176]{1,0:T(8,128)(2,1)S(1)} %pad_maximum_fusion.2), channel_id=1, source_target_pairs={{0,17},{1,16},{2,19},{3,18},{4,21},{5,20},{6,23},{7,22},{8,25},{9,... | collective-permute-start | bytes 417800 | tf_op jit(solution)/shard_map/ppermute | solution.py:28
  15.4 0.5 %collective-permute-start.4 = (bf16[32,2176]{1,0:T(8,128)(2,1)S(1)}, bf16[32,2176]{1,0:T(8,128)(2,1)S(1)}, u32[]{:S(2)}, u32[]{:S(2)}) collective-permute-start(bf16[32,2176]{1,0:T(8,128)(2,1)S(1)} %pad_maximum_fusion.2), channel_id=1, source_target_pairs={{0,16},{1,17},{2,18},{3,19},{4,20},{5,21},{6,22},{7,23},{8,24},{9,... | collective-permute-start | bytes 417800 | tf_op jit(solution)/shard_map/ppermute | solution.py:28
  15.9 2.6 %load_down.1.w_down = bf16[2688,1024]{1,0:T(8,128)(2,1)S(1)} custom-call(bf16[2688,1024]{1,0:T(8,128)(2,1)} %bitcast.3), custom_call_target="tpu_custom_call" | custom-call | bytes 5505024 | tf_op jit(solution)/shard_map/load_down/pallas_call | solution.py:92
  18.4 0.2 collective-permute-done.3
  18.7 1.9 %collective-permute-done.5 = bf16[32,2176]{1,0:T(8,128)(2,1)S(1)} collective-permute-done((bf16[32,2176]{1,0:T(8,128)(2,1)S(1)}, bf16[32,2176]{1,0:T(8,128)(2,1)S(1)}, u32[]{:S(2)}, u32[]{:S(2)}) %collective-permute-start.5) | collective-permute-done | bytes 139296 | tf_op jit(solution)/shard_map/ppermute | solution.py:28
  20.6 1.3 %collective-permute-done.4 = bf16[32,2176]{1,0:T(8,128)(2,1)S(1)} collective-permute-done((bf16[32,2176]{1,0:T(8,128)(2,1)S(1)}, bf16[32,2176]{1,0:T(8,128)(2,1)S(1)}, u32[]{:S(2)}, u32[]{:S(2)}) %collective-permute-start.4) | collective-permute-done | bytes 139296 | tf_op jit(solution)/shard_map/ppermute | solution.py:28
  22.0 0.1 collective-permute-start.7
  22.1 0.5 %collective-permute-start.6 = (bf16[128,1152]{1,0:T(8,128)(2,1)S(1)}, bf16[128,1152]{1,0:T(8,128)(2,1)S(1)}, u32[]{:S(2)}, u32[]{:S(2)}) collective-permute-start(bf16[128,1152]{1,0:T(8,128)(2,1)S(1)} %slice.55), channel_id=1, source_target_pairs={{0,8},{1,9},{2,10},{3,11},{4,12},{5,13},{6,14},{7,15},{8,0},{9,1},... | collective-permute-start | bytes 884744 | tf_op jit(solution)/shard_map/ppermute | solution.py:28
  22.6 1.0 %collective-permute-done.7 = bf16[128,1024]{1,0:T(8,128)(2,1)S(1)} collective-permute-done((bf16[128,1024]{1,0:T(8,128)(2,1)S(1)}, bf16[128,1024]{1,0:T(8,128)(2,1)S(1)}, u32[]{:S(2)}, u32[]{:S(2)}) %collective-permute-start.7) | collective-permute-done | bytes 262176 | tf_op jit(solution)/shard_map/ppermute | solution.py:28
  23.6 1.7 %pre.1.relu = f32[256,2688]{1,0:T(8,128)S(1)} custom-call(bf16[256,1024]{1,0:T(8,128)(2,1)S(1)} %constant_dynamic-update-slice_fusion.x.b, bf16[2688,1024]{1,0:T(8,128)(2,1)S(1)} %load_up.1.w_up), custom_call_target="tpu_custom_call" | custom-call | flops 1409286144 | tf_op jit(solution)/shard_map/pre/pallas_call | solution.py:184
  25.3 0.0 collective-permute-done.6
  25.4 3.5 %hidden.1 = (bf16[256,1024]{1,0:T(8,128)(2,1)S(1)}, bf16[256,2688]{1,0:T(8,128)(2,1)S(1)}, bf16[256,2688]{1,0:T(8,128)(2,1)S(1)}, bf16[256,1024]{1,0:T(8,128)(2,1)S(1)}) custom-call(bf16[256,1152]{1,0:T(8,128)(2,1)S(1)} %pad_maximum_fusion.dyg, bf16[2688,1024]{1,0:T(8,128)(2,1)S(1)} %load_down.1.w_down, bf16[2688,1024]{1,0:T(8,128)(2,1)S(1)} %load_up.1.w_up, ...), custom_call_target="tpu_custom_call" | custom-call | flops 2818572288 | tf_op jit(solution)/shard_map/hidden/pallas_call | solution.py:185
  28.9 0.2 collective-permute-start.8
  29.1 1.4 %collective-permute-done.8 = bf16[128,1024]{1,0:T(8,128)(2,1)S(1)} collective-permute-done((bf16[128,1024]{1,0:T(8,128)(2,1)S(1)}, bf16[128,1024]{1,0:T(8,128)(2,1)S(1)}, u32[]{:S(2)}, u32[]{:S(2)}) %collective-permute-start.8) | collective-permute-done | bytes 262176 | tf_op jit(solution)/shard_map/ppermute | solution.py:28
  30.5 0.1 convert_add_fusion
  30.6 1.6 %collective-permute-start.9 = (bf16[32,1024]{1,0:T(8,128)(2,1)S(1)}, bf16[32,1024]{1,0:T(8,128)(2,1)S(1)}, u32[]{:S(2)}, u32[]{:S(2)}) collective-permute-start(bf16[32,1024]{1,0:T(8,128)(2,1)S(1)} %get-tuple-element.43), channel_id=1, source_target_pairs={{0,1},{1,0},{2,3},{3,2},{4,5},{5,4},{6,7},{7,6},{8,9},{9,8},{10,11... | collective-permute-start | bytes 196616 | tf_op jit(solution)/shard_map/ppermute | solution.py:28
  32.2 0.7 %collective-permute-start.11 = (bf16[32,1024]{1,0:T(8,128)(2,1)S(1)}, bf16[32,1024]{1,0:T(8,128)(2,1)S(1)}, u32[]{:S(2)}, u32[]{:S(2)}) collective-permute-start(bf16[32,1024]{1,0:T(8,128)(2,1)S(1)} %get-tuple-element.44), channel_id=1, source_target_pairs={{0,17},{1,16},{2,19},{3,18},{4,21},{5,20},{6,23},{7,22},{8,25},{9,... | collective-permute-start | bytes 196616 | tf_op jit(solution)/shard_map/ppermute | solution.py:28
  32.9 1.3 %collective-permute-start.10 = (bf16[32,1024]{1,0:T(8,128)(2,1)S(1)}, bf16[32,1024]{1,0:T(8,128)(2,1)S(1)}, u32[]{:S(2)}, u32[]{:S(2)}) collective-permute-start(bf16[32,1024]{1,0:T(8,128)(2,1)S(1)} %get-tuple-element.45), channel_id=1, source_target_pairs={{0,16},{1,17},{2,18},{3,19},{4,20},{5,21},{6,22},{7,23},{8,24},{9,... | collective-permute-start | bytes 196616 | tf_op jit(solution)/shard_map/ppermute | solution.py:28
  34.2 2.9 %up.1 = bf16[1,2688,1024]{2,1,0:T(8,128)(2,1)} custom-call(bf16[256,2688]{1,0:T(8,128)(2,1)S(1)} %get-tuple-element.32.a, bf16[256,1024]{1,0:T(8,128)(2,1)S(1)} %constant_dynamic-update-slice_fusion.x.b), custom_call_target="tpu_custom_call" | custom-call | flops 1409286144 | bytes 5505024 | tf_op jit(solution)/shard_map/up/pallas_call | solution.py:145
  37.1 0.0 collective-permute-done.9
  37.1 0.3 collective-permute-done.11
  37.4 0.4 collective-permute-done.10
  37.9 0.4 collective-permute-start.12
  38.3 1.8 %collective-permute-start.14 = (bf16[8,1024]{1,0:T(8,128)(2,1)S(1)}, bf16[8,1024]{1,0:T(8,128)(2,1)S(1)}, u32[]{:S(2)}, u32[]{:S(2)}) collective-permute-start(bf16[8,1024]{1,0:T(8,128)(2,1)S(1)} %get-tuple-element.47), channel_id=1, source_target_pairs={{0,6},{1,7},{2,4},{3,5},{4,2},{5,3},{6,0},{7,1},{8,14},{9,15},{10,... | collective-permute-start | bytes 49160 | tf_op jit(solution)/shard_map/ppermute | solution.py:28
  40.1 1.3 %collective-permute-start.13 = (bf16[8,1024]{1,0:T(8,128)(2,1)S(1)}, bf16[8,1024]{1,0:T(8,128)(2,1)S(1)}, u32[]{:S(2)}, u32[]{:S(2)}) collective-permute-start(bf16[8,1024]{1,0:T(8,128)(2,1)S(1)} %get-tuple-element.48), channel_id=1, source_target_pairs={{0,4},{1,5},{2,6},{3,7},{4,0},{5,1},{6,2},{7,3},{8,12},{9,13},{10,... | collective-permute-start | bytes 49160 | tf_op jit(solution)/shard_map/ppermute | solution.py:28
  41.5 2.9 %down.1 = bf16[1,2688,1024]{2,1,0:T(8,128)(2,1)} custom-call(bf16[256,2688]{1,0:T(8,128)(2,1)S(1)} %get-tuple-element.34.a, bf16[256,1024]{1,0:T(8,128)(2,1)S(1)} %get-tuple-element.35.b), custom_call_target="tpu_custom_call" | custom-call | flops 1409286144 | bytes 5505024 | tf_op jit(solution)/shard_map/down/pallas_call | solution.py:145
  44.4 0.0 collective-permute-done.12
  44.4 0.0 collective-permute-done.14
  44.4 0.4 collective-permute-done.13
  44.8 0.6 %slice_add_fusion.1 = f32[8,1024]{1,0:T(8,128)} fusion(f32[32,1024]{1,0:T(8,128)S(1)} %get-tuple-element.40, bf16[8,1024]{1,0:T(8,128)(2,1)S(1)} %collective-permute-done.14, bf16[8,1024]{1,0:T(8,128)(2,1)S(1)} %collective-permute-done.13, bf16[8,1024]{1,0:T(8,128)(2,1)S(1)} %collective-permute-done.12), kind=kLoop, calls=%fused_computation.5 | loop fusion | flops 49152 | bytes 114688 | tf_op jit(solution)/shard_map/add | solution.py:204
  (11 shorter events, 0.3 us)
Async XLA Ops:
  1.5 8.3 %collective-permute-start = (bf16[8,2176]{1,0:T(8,128)(2,1)S(1)}, bf16[8,2176]{1,0:T(8,128)(2,1)S(1)}, u32[]{:S(2)}, u32[]{:S(2)}) collective-permute-start(bf16[8,2176]{1,0:T(8,128)(2,1)S(1)} %pack.1), channel_id=1, source_target_pairs={{0,2},{1,3},{2,0},{3,1},{4,6},{5,7},{6,4},{7,5},{8,10},{9,11},{10,... | collective-permute-start | bytes 104456 | tf_op jit(solution)/shard_map/ppermute | solution.py:28
  4.6 6.2 %collective-permute-start.2 = (bf16[8,2176]{1,0:T(8,128)(2,1)S(1)}, bf16[8,2176]{1,0:T(8,128)(2,1)S(1)}, u32[]{:S(2)}, u32[]{:S(2)}) collective-permute-start(bf16[8,2176]{1,0:T(8,128)(2,1)S(1)} %pack.1), channel_id=1, source_target_pairs={{0,6},{1,7},{2,4},{3,5},{4,2},{5,3},{6,0},{7,1},{8,14},{9,15},{10,... | collective-permute-start | bytes 104456 | tf_op jit(solution)/shard_map/ppermute | solution.py:28
  7.1 5.2 %collective-permute-start.1 = (bf16[8,2176]{1,0:T(8,128)(2,1)S(1)}, bf16[8,2176]{1,0:T(8,128)(2,1)S(1)}, u32[]{:S(2)}, u32[]{:S(2)}) collective-permute-start(bf16[8,2176]{1,0:T(8,128)(2,1)S(1)} %pack.1), channel_id=1, source_target_pairs={{0,4},{1,5},{2,6},{3,7},{4,0},{5,1},{6,2},{7,3},{8,12},{9,13},{10,... | collective-permute-start | bytes 104456 | tf_op jit(solution)/shard_map/ppermute | solution.py:28
  12.3 6.3 %collective-permute-start.3 = (bf16[32,2176]{1,0:T(8,128)(2,1)S(1)}, bf16[32,2176]{1,0:T(8,128)(2,1)S(1)}, u32[]{:S(2)}, u32[]{:S(2)}) collective-permute-start(bf16[32,2176]{1,0:T(8,128)(2,1)S(1)} %pad_maximum_fusion.2), channel_id=1, source_target_pairs={{0,1},{1,0},{2,3},{3,2},{4,5},{5,4},{6,7},{7,6},{8,9},{9,8},{10,11... | collective-permute-start | bytes 417800 | tf_op jit(solution)/shard_map/ppermute | solution.py:28
  13.9 6.7 %collective-permute-start.5 = (bf16[32,2176]{1,0:T(8,128)(2,1)S(1)}, bf16[32,2176]{1,0:T(8,128)(2,1)S(1)}, u32[]{:S(2)}, u32[]{:S(2)}) collective-permute-start(bf16[32,2176]{1,0:T(8,128)(2,1)S(1)} %pad_maximum_fusion.2), channel_id=1, source_target_pairs={{0,17},{1,16},{2,19},{3,18},{4,21},{5,20},{6,23},{7,22},{8,25},{9,... | collective-permute-start | bytes 417800 | tf_op jit(solution)/shard_map/ppermute | solution.py:28
  15.4 6.5 %collective-permute-start.4 = (bf16[32,2176]{1,0:T(8,128)(2,1)S(1)}, bf16[32,2176]{1,0:T(8,128)(2,1)S(1)}, u32[]{:S(2)}, u32[]{:S(2)}) collective-permute-start(bf16[32,2176]{1,0:T(8,128)(2,1)S(1)} %pad_maximum_fusion.2), channel_id=1, source_target_pairs={{0,16},{1,17},{2,18},{3,19},{4,20},{5,21},{6,22},{7,23},{8,24},{9,... | collective-permute-start | bytes 417800 | tf_op jit(solution)/shard_map/ppermute | solution.py:28
  22.0 1.6 %collective-permute-start.7 = (bf16[128,1024]{1,0:T(8,128)(2,1)S(1)}, bf16[128,1024]{1,0:T(8,128)(2,1)S(1)}, u32[]{:S(2)}, u32[]{:S(2)}) collective-permute-start(bf16[128,1024]{1,0:T(8,128)(2,1)S(1)} %slice.54), channel_id=1, source_target_pairs={{0,8},{1,9},{2,10},{3,11},{4,12},{5,13},{6,14},{7,15},{8,0},{9,1},... | collective-permute-start | bytes 786440 | tf_op jit(solution)/shard_map/ppermute | solution.py:28
  22.1 3.2 %collective-permute-start.6 = (bf16[128,1152]{1,0:T(8,128)(2,1)S(1)}, bf16[128,1152]{1,0:T(8,128)(2,1)S(1)}, u32[]{:S(2)}, u32[]{:S(2)}) collective-permute-start(bf16[128,1152]{1,0:T(8,128)(2,1)S(1)} %slice.55), channel_id=1, source_target_pairs={{0,8},{1,9},{2,10},{3,11},{4,12},{5,13},{6,14},{7,15},{8,0},{9,1},... | collective-permute-start | bytes 884744 | tf_op jit(solution)/shard_map/ppermute | solution.py:28
  28.9 1.6 %collective-permute-start.8 = (bf16[128,1024]{1,0:T(8,128)(2,1)S(1)}, bf16[128,1024]{1,0:T(8,128)(2,1)S(1)}, u32[]{:S(2)}, u32[]{:S(2)}) collective-permute-start(bf16[128,1024]{1,0:T(8,128)(2,1)S(1)} %slice.45), channel_id=1, source_target_pairs={{0,8},{1,9},{2,10},{3,11},{4,12},{5,13},{6,14},{7,15},{8,0},{9,1},... | collective-permute-start | bytes 786440 | tf_op jit(solution)/shard_map/ppermute | solution.py:28
  30.6 6.4 %collective-permute-start.9 = (bf16[32,1024]{1,0:T(8,128)(2,1)S(1)}, bf16[32,1024]{1,0:T(8,128)(2,1)S(1)}, u32[]{:S(2)}, u32[]{:S(2)}) collective-permute-start(bf16[32,1024]{1,0:T(8,128)(2,1)S(1)} %get-tuple-element.43), channel_id=1, source_target_pairs={{0,1},{1,0},{2,3},{3,2},{4,5},{5,4},{6,7},{7,6},{8,9},{9,8},{10,11... | collective-permute-start | bytes 196616 | tf_op jit(solution)/shard_map/ppermute | solution.py:28
  32.2 5.2 %collective-permute-start.11 = (bf16[32,1024]{1,0:T(8,128)(2,1)S(1)}, bf16[32,1024]{1,0:T(8,128)(2,1)S(1)}, u32[]{:S(2)}, u32[]{:S(2)}) collective-permute-start(bf16[32,1024]{1,0:T(8,128)(2,1)S(1)} %get-tuple-element.44), channel_id=1, source_target_pairs={{0,17},{1,16},{2,19},{3,18},{4,21},{5,20},{6,23},{7,22},{8,25},{9,... | collective-permute-start | bytes 196616 | tf_op jit(solution)/shard_map/ppermute | solution.py:28
  32.9 5.0 %collective-permute-start.10 = (bf16[32,1024]{1,0:T(8,128)(2,1)S(1)}, bf16[32,1024]{1,0:T(8,128)(2,1)S(1)}, u32[]{:S(2)}, u32[]{:S(2)}) collective-permute-start(bf16[32,1024]{1,0:T(8,128)(2,1)S(1)} %get-tuple-element.45), channel_id=1, source_target_pairs={{0,16},{1,17},{2,18},{3,19},{4,20},{5,21},{6,22},{7,23},{8,24},{9,... | collective-permute-start | bytes 196616 | tf_op jit(solution)/shard_map/ppermute | solution.py:28
  37.9 6.4 %collective-permute-start.12 = (bf16[8,1024]{1,0:T(8,128)(2,1)S(1)}, bf16[8,1024]{1,0:T(8,128)(2,1)S(1)}, u32[]{:S(2)}, u32[]{:S(2)}) collective-permute-start(bf16[8,1024]{1,0:T(8,128)(2,1)S(1)} %get-tuple-element.46), channel_id=1, source_target_pairs={{0,2},{1,3},{2,0},{3,1},{4,6},{5,7},{6,4},{7,5},{8,10},{9,11},{10,... | collective-permute-start | bytes 49160 | tf_op jit(solution)/shard_map/ppermute | solution.py:28
  38.3 6.0 %collective-permute-start.14 = (bf16[8,1024]{1,0:T(8,128)(2,1)S(1)}, bf16[8,1024]{1,0:T(8,128)(2,1)S(1)}, u32[]{:S(2)}, u32[]{:S(2)}) collective-permute-start(bf16[8,1024]{1,0:T(8,128)(2,1)S(1)} %get-tuple-element.47), channel_id=1, source_target_pairs={{0,6},{1,7},{2,4},{3,5},{4,2},{5,3},{6,0},{7,1},{8,14},{9,15},{10,... | collective-permute-start | bytes 49160 | tf_op jit(solution)/shard_map/ppermute | solution.py:28
  40.1 4.6 %collective-permute-start.13 = (bf16[8,1024]{1,0:T(8,128)(2,1)S(1)}, bf16[8,1024]{1,0:T(8,128)(2,1)S(1)}, u32[]{:S(2)}, u32[]{:S(2)}) collective-permute-start(bf16[8,1024]{1,0:T(8,128)(2,1)S(1)} %get-tuple-element.48), channel_id=1, source_target_pairs={{0,4},{1,5},{2,6},{3,7},{4,0},{5,1},{6,2},{7,3},{8,12},{9,13},{10,... | collective-permute-start | bytes 49160 | tf_op jit(solution)/shard_map/ppermute | solution.py:28

commit v4 on v3

--- a/solution.py
+++ b/solution.py
@@ -8,6 +8,7 @@
 HID = 2688
 LANES = 128
 AXES = ("group", "member")
+TIED = (0, 2, 1, 2)
 BF16 = jnp.bfloat16
 F32 = jnp.float32
 VMEM = pl.BlockSpec(memory_space=pltpu.VMEM)
@@ -19,20 +20,23 @@
 
 def stages(members, devices):
     bits = [1 << k for k in range(1, devices.bit_length() - 1)]
-    bits = [b for b in bits if b < members] + [1] + [b for b in bits if b > members]
+    bits = [b for b in reversed(bits) if b < members] + [1] + [b for b in bits if b > members]
     pairs = [bits[k : k + 2] for k in range(0, len(bits), 2)]
-    return [pair if len(pair) == 1 else [pair[0], pair[1], pair[0] ^ pair[1]] for pair in pairs]
-
-
-def swap(value, mask, devices):
-    return lax.ppermute(value, AXES, [(i, i ^ mask) for i in range(devices)])
+    groups = [pair if len(pair) == 1 else [pair[0], pair[1], pair[0] ^ pair[1]] for pair in pairs]
+    others = groups[::-1] if len(bits) % 2 == 0 else groups
+    return [list(zip(even, odd)) for even, odd in zip(groups, others)]
+
+
+def swap(value, masks, core, devices):
+    even, odd = masks
+    return lax.ppermute(value, AXES, [(i, i ^ (odd if i & core else even)) for i in range(devices)])
 
 
 def dot(a, b, on_a, on_b):
     return lax.dot_general(a, b, (((on_a,), (on_b,)), ((), ())), preferred_element_type=F32)
 
 
-def call(kernel, out, ins, name, scratch=(), outs=None, flops=0, moved=0, limit=16, aliases={}):
+def call(kernel, out, ins, name, scratch=(), outs=None, flops=0, moved=0, limit=16):
     return pl.pallas_call(
         kernel,
         out_shape=out,
@@ -40,7 +44,6 @@
         out_specs=jax.tree.map(lambda _: VMEM, out) if outs is None else outs,
         scratch_shapes=scratch,
         name=name,
-        input_output_aliases=aliases,
         compiler_params=pltpu.CompilerParams(vmem_limit_bytes=limit << 20),
         cost_estimate=pl.CostEstimate(flops=flops, bytes_accessed=moved, transcendentals=0),
     )
@@ -107,10 +110,9 @@
     relu[...] = jnp.maximum(dot(x[...], w_up[...], 1, 1), 0.0)
 
 
-def hidden_kernel(dyg, w_down, w_up, relu, row_grad, act, pre_grad, part):
+def hidden_kernel(dyg, w_down, w_up, relu, row_grad, pre_grad, part):
     row_grad[...] = gated(dyg[...], row_grad.shape[1], w_down.shape[0])
     hid_grad = dot(row_grad[...], w_down[...], 1, 1)
-    act[...] = (relu[...] * relu[...]).astype(BF16)
     pre_grad[...] = (hid_grad * 2.0 * relu[...]).astype(BF16)
     part[...] = dot(pre_grad[...], w_up[...], 1, 0).astype(BF16)
 
@@ -123,29 +125,25 @@
     return row_grad, act, pre_grad, dot(pre_grad, w_up, 1, 0).astype(BF16)
 
 
-def outer(a, b, name, blocks, first=0, last=None, into=None):
+def outer(a, b, name, blocks):
     n, width = a.shape[1], b.shape[1]
     step = n // blocks
-    last = blocks if last is None else last
-    count = last - first
-
-    def kernel(a, b, *refs):
-        out, buffer, sems = refs[-3:]
+
+    def kernel(a, b, out, buffer, sems):
         copies = []
-        for k in range(count):
-            at = (first + k) * step
+        for k in range(blocks):
             rows = pl.ds(k * step, step)
-            buffer[rows] = dot(a[:, at : at + step], b[...], 0, 0).astype(BF16)
-            copies.append(pltpu.make_async_copy(buffer.at[rows], out.at[0, pl.ds(at, step)], sems.at[k]))
+            left = a[:, k * step : (k + 1) * step]
+            left = (left * left).astype(BF16) if a.dtype == F32 else left
+            buffer[rows] = dot(left, b[...], 0, 0).astype(BF16)
+            copies.append(pltpu.make_async_copy(buffer.at[rows], out.at[0, rows], sems.at[k]))
             copies[-1].start()
         for copy in copies:
             copy.wait()
 
-    args = (a, b) if into is None else (a, b, into)
-    return call(kernel, S((1, n, width), BF16), [VMEM, VMEM] + [ANY] * (len(args) - 2), name,
-        (pltpu.VMEM((count * step, width), BF16), pltpu.SemaphoreType.DMA((count,))), ANY,
-        flops=2 * a.shape[0] * count * step * width, moved=2 * count * step * width,
-        aliases={} if into is None else {2: 0})(*args)
+    return call(kernel, S((1, n, width), BF16), [VMEM, VMEM], name,
+        (pltpu.VMEM((n, width), BF16), pltpu.SemaphoreType.DMA((blocks,))), ANY,
+        flops=2 * a.shape[0] * n * width, moved=2 * n * width)(a, b)
 
 
 def local(latent, out_grad, gates, expert_ids, up_weight, down_weight):
@@ -154,7 +152,7 @@
     members = lax.axis_size("member")
     groups = lax.axis_size("group")
     devices = members * groups
-    core = members
+    core = (members, members)
     plan = stages(members, devices)
     tokens = latent.shape[0] * devices
     flops = 2 * tokens * rows * width
@@ -168,39 +166,43 @@
             rows_all, w_up = tie((rows_all, w_up))
         if small and k == 1:
             rows_all, w_down = tie((rows_all, w_down))
-        got = [swap(rows_all, mask, devices) for mask in masks]
+        got = [swap(rows_all, mask, members, devices) for mask in masks]
+        t = TIED[k % 4]
         if small and k == 0:
             w_up = load(w_up, "load_up")
-            got[0], w_up = tie((got[0], w_up))
+            got[t], w_up = tie((got[t], w_up))
         if small and k == 1:
             w_down = load(w_down, "load_down")
-            got[0], w_down = tie((got[0], w_down))
+            got[t], w_down = tie((got[t], w_down))
         rows_all = tie(jnp.concatenate([rows_all] + got, axis=0))
     x, dyg = tie((rows_all[:, :width], rows_all[:, width:]))
-    x = jnp.concatenate([x, swap(x, core, devices)], axis=0)
-    got_dyg = swap(dyg, core, devices)
+    got_x = swap(x, core, members, devices)
+    got_x, dyg = tie((got_x, dyg))
+    x = jnp.concatenate([x, got_x], axis=0)
+    got_dyg = swap(dyg, core, members, devices)
     dyg_all = jnp.concatenate([dyg, got_dyg], axis=0)
     if small:
         relu = call(pre_kernel, S((tokens, rows), F32), [VMEM] * 2, "pre", flops=flops)(x, w_up)
-        row_grad, act, pre_grad, part = call(
+        row_grad, pre_grad, part = call(
             hidden_kernel,
-            (S((tokens, width), BF16), S((tokens, rows), BF16), S((tokens, rows), BF16), S((tokens, width), BF16)),
+            (S((tokens, width), BF16), S((tokens, rows), BF16), S((tokens, width), BF16)),
             [VMEM] * 4, "hidden", flops=2 * flops)(dyg_all, w_down, w_up, relu)
     else:
         row_grad, act, pre_grad, part = plain(x, dyg_all, w_up, w_down)
 
     half = tokens // 2
-    total = part[:half].astype(F32) + swap(part[half:], core, devices).astype(F32)
+    total = part[:half].astype(F32) + swap(part[half:], core, members, devices).astype(F32)
     for k, masks in enumerate(reversed(plan)):
         count = total.shape[0] // (len(masks) + 1)
         cut = [total[j * count : (j + 1) * count] for j in range(len(masks) + 1)]
-        got = [swap(block.astype(BF16), mask, devices) for block, mask in zip(cut[1:], masks)]
+        got = [swap(block.astype(BF16), mask, members, devices) for block, mask in zip(cut[1:], masks)]
+        t = TIED[(2 + k) % 4]
         if small and k == 0:
             up_grad = outer(pre_grad, x, "up", blocks)
-            got[0], up_grad = tie((got[0], up_grad))
+            got[t], up_grad = tie((got[t], up_grad))
         if small and k == 1:
-            down_grad = outer(act, row_grad, "down", blocks)
-            got[0], down_grad = tie((got[0], down_grad))
+            down_grad = outer(relu, row_grad, "down", blocks)
+            got[t], down_grad = tie((got[t], down_grad))
         total = cut[0] + sum(block.astype(F32) for block in got)
     if not small:
         up_grad = dot(pre_grad, x, 0, 0).astype(BF16)[None]

time: 45.6 us -> 43.2 us (0.947)
  waiting for transfers between devices: 9.56 us -> 7.49 us
    ppermute x15, waiting for transfers between devices: 9.56 us -> 7.49 us  [swap(): lax.ppermute(value, AXES, [(i, i ^ (odd if i & core else even)) for i in...]
  transfers between devices with their start and end apart: 15 -> 15, of which waited for: 10 -> 7; matrix products, arithmetic and copies ran while one was open for 0% -> 0% of each run, Pallas kernels for 28% -> 29%
where the time goes in v4:
time: 43.2 us; the launch traced here: 43 us
  starting transfers between devices  17 us (39%)
  Pallas kernels  16.7 us (39%)
  waiting for transfers between devices  7.49 us (17%)
  other arithmetic  0.84 us (2%)
  between operations  0.81 us (2%)
    ppermute x15, starting transfers between devices, swap(): lax.ppermute(value, AXES, [(i, i ^ (odd if i & core else even)) for i in...  17 us
    ppermute x15, waiting for transfers between devices, swap(): lax.ppermute(value, AXES, [(i, i ^ (odd if i & core else even)) for i in...  7.49 us
    pallas_call x2, Pallas kernels, outer(): call(kernel, S((1, n, width), BF16), [VMEM, VMEM], name, (pltpu.VMEM((n,...  5.77 us
    pallas_call x2, Pallas kernels, load(): call(load_kernel, S(weight.shape, weight.dtype), [HBM], name, (pltpu.Sema...  5.14 us
    pallas_call x1, Pallas kernels, local(): call(hidden_kernel, (S((tokens, width), BF16), S((tokens, rows), BF16), S...  3.24 us
    pallas_call x1, Pallas kernels, local(): call(pre_kernel, S((tokens, rows), F32), [VMEM] * 2, 'pre', flops=flops)  1.69 us
    pallas_call x1, Pallas kernels, pack(): call(pack_kernel, S((rows, 2 * width + LANES), BF16), [HBM] * 4, 'pack',...  0.88 us
  transfers between devices with their start and end apart: 15, of which 7 were waited for; matrix products, arithmetic and copies ran while one was open for 0% of the time, Pallas kernels for 29%

profile of v4, /device:TPU:0, one launch (start us, length us, event | category | flops | bytes accessed | tf_op | source)
XLA Modules:
  0.0 43.0 jit_solution(14111600817501347307)
XLA Ops:
  0.6 0.9 %pack.1 = bf16[8,2176]{1,0:T(8,128)(2,1)S(1)} custom-call(bf16[8,1024]{1,0:T(8,128)(2,1)} %latent.1, bf16[8,1024]{1,0:T(8,128)(2,1)} %out_grad.1, bf16[8,22]{1,0:T(8,128)(2,1)} %gates.1, s32[8,22]{1,0:T(8,128)} %ids.1), custom_call_target="tpu_custom_call" | custom-call | tf_op jit(solution)/shard_map/pack/pallas_call | solution.py:83
  1.5 4.1 %collective-permute-start = (bf16[8,2176]{1,0:T(8,128)(2,1)S(1)}, bf16[8,2176]{1,0:T(8,128)(2,1)S(1)}, u32[]{:S(2)}, u32[]{:S(2)}) collective-permute-start(bf16[8,2176]{1,0:T(8,128)(2,1)S(1)} %pack.1), channel_id=1, source_target_pairs={{0,4},{1,5},{2,6},{3,7},{4,0},{5,1},{6,2},{7,3},{8,9},{9,8},{10,11... | collective-permute-start | bytes 104456 | tf_op jit(solution)/shard_map/ppermute | solution.py:32
  5.6 1.3 %collective-permute-start.2 = (bf16[8,2176]{1,0:T(8,128)(2,1)S(1)}, bf16[8,2176]{1,0:T(8,128)(2,1)S(1)}, u32[]{:S(2)}, u32[]{:S(2)}) collective-permute-start(bf16[8,2176]{1,0:T(8,128)(2,1)S(1)} %pack.1), channel_id=1, source_target_pairs={{0,6},{1,7},{2,4},{3,5},{4,2},{5,3},{6,0},{7,1},{8,25},{9,24},{10,... | collective-permute-start | bytes 104456 | tf_op jit(solution)/shard_map/ppermute | solution.py:32
  7.0 0.2 collective-permute-start.1
  7.2 2.6 %load_up.1.w_up = bf16[2688,1024]{1,0:T(8,128)(2,1)S(1)} custom-call(bf16[2688,1024]{1,0:T(8,128)(2,1)} %bitcast.2), custom_call_target="tpu_custom_call" | custom-call | bytes 5505024 | tf_op jit(solution)/shard_map/load_up/pallas_call | solution.py:95
  9.8 0.0 collective-permute-done
  9.8 1.6 %collective-permute-done.2 = bf16[8,2176]{1,0:T(8,128)(2,1)S(1)} collective-permute-done((bf16[8,2176]{1,0:T(8,128)(2,1)S(1)}, bf16[8,2176]{1,0:T(8,128)(2,1)S(1)}, u32[]{:S(2)}, u32[]{:S(2)}) %collective-permute-start.2) | collective-permute-done | bytes 34848 | tf_op jit(solution)/shard_map/ppermute | solution.py:32
  11.4 0.0 collective-permute-done.1
  11.4 2.5 %collective-permute-start.5 = (bf16[32,2176]{1,0:T(8,128)(2,1)S(1)}, bf16[32,2176]{1,0:T(8,128)(2,1)S(1)}, u32[]{:S(2)}, u32[]{:S(2)}) collective-permute-start(bf16[32,2176]{1,0:T(8,128)(2,1)S(1)} %pad_maximum_fusion.2), channel_id=1, source_target_pairs={{0,17},{1,16},{2,19},{3,18},{4,21},{5,20},{6,23},{7,22},{8,14},{9,... | collective-permute-start | bytes 417800 | tf_op jit(solution)/shard_map/ppermute | solution.py:32
  13.9 0.5 %collective-permute-start.4 = (bf16[32,2176]{1,0:T(8,128)(2,1)S(1)}, bf16[32,2176]{1,0:T(8,128)(2,1)S(1)}, u32[]{:S(2)}, u32[]{:S(2)}) collective-permute-start(bf16[32,2176]{1,0:T(8,128)(2,1)S(1)} %pad_maximum_fusion.2), channel_id=1, source_target_pairs={{0,16},{1,17},{2,18},{3,19},{4,20},{5,21},{6,22},{7,23},{8,10},{9,... | collective-permute-start | bytes 417800 | tf_op jit(solution)/shard_map/ppermute | solution.py:32
  14.4 0.5 %collective-permute-start.3 = (bf16[32,2176]{1,0:T(8,128)(2,1)S(1)}, bf16[32,2176]{1,0:T(8,128)(2,1)S(1)}, u32[]{:S(2)}, u32[]{:S(2)}) collective-permute-start(bf16[32,2176]{1,0:T(8,128)(2,1)S(1)} %pad_maximum_fusion.2), channel_id=1, source_target_pairs={{0,1},{1,0},{2,3},{3,2},{4,5},{5,4},{6,7},{7,6},{8,12},{9,13},{10,... | collective-permute-start | bytes 417800 | tf_op jit(solution)/shard_map/ppermute | solution.py:32
  14.9 2.6 %load_down.1.w_down = bf16[2688,1024]{1,0:T(8,128)(2,1)S(1)} custom-call(bf16[2688,1024]{1,0:T(8,128)(2,1)} %bitcast.3), custom_call_target="tpu_custom_call" | custom-call | bytes 5505024 | tf_op jit(solution)/shard_map/load_down/pallas_call | solution.py:95
  17.5 0.0 collective-permute-done.5
  17.5 1.4 %collective-permute-done.4 = bf16[32,2176]{1,0:T(8,128)(2,1)S(1)} collective-permute-done((bf16[32,2176]{1,0:T(8,128)(2,1)S(1)}, bf16[32,2176]{1,0:T(8,128)(2,1)S(1)}, u32[]{:S(2)}, u32[]{:S(2)}) %collective-permute-start.4) | collective-permute-done | bytes 139296 | tf_op jit(solution)/shard_map/ppermute | solution.py:32
  18.9 0.5 %collective-permute-done.3 = bf16[32,2176]{1,0:T(8,128)(2,1)S(1)} collective-permute-done((bf16[32,2176]{1,0:T(8,128)(2,1)S(1)}, bf16[32,2176]{1,0:T(8,128)(2,1)S(1)}, u32[]{:S(2)}, u32[]{:S(2)}) %collective-permute-start.3) | collective-permute-done | bytes 139296 | tf_op jit(solution)/shard_map/ppermute | solution.py:32
  19.6 0.1 collective-permute-start.6
  19.6 1.5 %collective-permute-done.6 = bf16[128,1024]{1,0:T(8,128)(2,1)S(1)} collective-permute-done((bf16[128,1024]{1,0:T(8,128)(2,1)S(1)}, bf16[128,1024]{1,0:T(8,128)(2,1)S(1)}, u32[]{:S(2)}, u32[]{:S(2)}) %collective-permute-start.6) | collective-permute-done | bytes 262176 | tf_op jit(solution)/shard_map/ppermute | solution.py:32
  21.2 0.1 collective-permute-start.7
  21.3 1.7 %pre.1.relu.a = f32[256,2688]{1,0:T(8,128)S(1)} custom-call(bf16[256,1024]{1,0:T(8,128)(2,1)S(1)} %constant_dynamic-update-slice_fusion.x.b, bf16[2688,1024]{1,0:T(8,128)(2,1)S(1)} %load_up.1.w_up), custom_call_target="tpu_custom_call" | custom-call | flops 1409286144 | tf_op jit(solution)/shard_map/pre/pallas_call | solution.py:185
  23.0 0.0 collective-permute-done.7
  23.1 3.2 %hidden.1 = (bf16[256,1024]{1,0:T(8,128)(2,1)S(1)}, bf16[256,2688]{1,0:T(8,128)(2,1)S(1)}, bf16[256,1024]{1,0:T(8,128)(2,1)S(1)}) custom-call(bf16[256,1152]{1,0:T(8,128)(2,1)S(1)} %pad_maximum_fusion.dyg, bf16[2688,1024]{1,0:T(8,128)(2,1)S(1)} %load_down.1.w_down, bf16[2688,1024]{1,0:T(8,128)(2,1)S(1)} %load_up.1.w_up, f32[256,2688]{1,0:T(8,128)S(1)} %pre.1.relu.a), custom_call_target="tpu_custom_call" | custom-call | flops 2818572288 | tf_op jit(solution)/shard_map/hidden/pallas_call | solution.py:186
  26.4 0.4 %collective-permute-start.8 = (bf16[128,1024]{1,0:T(8,128)(2,1)S(1)}, bf16[128,1024]{1,0:T(8,128)(2,1)S(1)}, u32[]{:S(2)}, u32[]{:S(2)}) collective-permute-start(bf16[128,1024]{1,0:T(8,128)(2,1)S(1)} %slice.45), channel_id=1, source_target_pairs={{0,8},{1,9},{2,10},{3,11},{4,12},{5,13},{6,14},{7,15},{8,0},{9,1},... | collective-permute-start | bytes 786440 | tf_op jit(solution)/shard_map/ppermute | solution.py:32
  26.8 1.2 %collective-permute-done.8 = bf16[128,1024]{1,0:T(8,128)(2,1)S(1)} collective-permute-done((bf16[128,1024]{1,0:T(8,128)(2,1)S(1)}, bf16[128,1024]{1,0:T(8,128)(2,1)S(1)}, u32[]{:S(2)}, u32[]{:S(2)}) %collective-permute-start.8) | collective-permute-done | bytes 262176 | tf_op jit(solution)/shard_map/ppermute | solution.py:32
  28.0 0.1 convert_add_fusion
  28.1 1.1 %collective-permute-start.9 = (bf16[32,1024]{1,0:T(8,128)(2,1)S(1)}, bf16[32,1024]{1,0:T(8,128)(2,1)S(1)}, u32[]{:S(2)}, u32[]{:S(2)}) collective-permute-start(bf16[32,1024]{1,0:T(8,128)(2,1)S(1)} %get-tuple-element.45), channel_id=1, source_target_pairs={{0,1},{1,0},{2,3},{3,2},{4,5},{5,4},{6,7},{7,6},{8,12},{9,13},{10,... | collective-permute-start | bytes 196616 | tf_op jit(solution)/shard_map/ppermute | solution.py:32
  29.2 2.0 %collective-permute-start.11 = (bf16[32,1024]{1,0:T(8,128)(2,1)S(1)}, bf16[32,1024]{1,0:T(8,128)(2,1)S(1)}, u32[]{:S(2)}, u32[]{:S(2)}) collective-permute-start(bf16[32,1024]{1,0:T(8,128)(2,1)S(1)} %get-tuple-element.46), channel_id=1, source_target_pairs={{0,17},{1,16},{2,19},{3,18},{4,21},{5,20},{6,23},{7,22},{8,14},{9,... | collective-permute-start | bytes 196616 | tf_op jit(solution)/shard_map/ppermute | solution.py:32
  31.1 0.5 %collective-permute-start.10 = (bf16[32,1024]{1,0:T(8,128)(2,1)S(1)}, bf16[32,1024]{1,0:T(8,128)(2,1)S(1)}, u32[]{:S(2)}, u32[]{:S(2)}) collective-permute-start(bf16[32,1024]{1,0:T(8,128)(2,1)S(1)} %get-tuple-element.47), channel_id=1, source_target_pairs={{0,16},{1,17},{2,18},{3,19},{4,20},{5,21},{6,22},{7,23},{8,10},{9,... | collective-permute-start | bytes 196616 | tf_op jit(solution)/shard_map/ppermute | solution.py:32
  31.6 2.9 %up.1 = bf16[1,2688,1024]{2,1,0:T(8,128)(2,1)} custom-call(bf16[256,2688]{1,0:T(8,128)(2,1)S(1)} %get-tuple-element.35.a, bf16[256,1024]{1,0:T(8,128)(2,1)S(1)} %constant_dynamic-update-slice_fusion.x.b), custom_call_target="tpu_custom_call" | custom-call | flops 1409286144 | bytes 5505024 | tf_op jit(solution)/shard_map/up/pallas_call | solution.py:144
  34.5 0.9 %collective-permute-done.10 = bf16[32,1024]{1,0:T(8,128)(2,1)S(1)} collective-permute-done((bf16[32,1024]{1,0:T(8,128)(2,1)S(1)}, bf16[32,1024]{1,0:T(8,128)(2,1)S(1)}, u32[]{:S(2)}, u32[]{:S(2)}) %collective-permute-start.10) | collective-permute-done | bytes 65568 | tf_op jit(solution)/shard_map/ppermute | solution.py:32
  35.4 0.0 collective-permute-done.9
  35.4 0.0 collective-permute-done.11
  35.5 1.3 %collective-permute-start.12 = (bf16[8,1024]{1,0:T(8,128)(2,1)S(1)}, bf16[8,1024]{1,0:T(8,128)(2,1)S(1)}, u32[]{:S(2)}, u32[]{:S(2)}) collective-permute-start(bf16[8,1024]{1,0:T(8,128)(2,1)S(1)} %get-tuple-element.48), channel_id=1, source_target_pairs={{0,4},{1,5},{2,6},{3,7},{4,0},{5,1},{6,2},{7,3},{8,9},{9,8},{10,11... | collective-permute-start | bytes 49160 | tf_op jit(solution)/shard_map/ppermute | solution.py:32
  36.8 1.3 %collective-permute-start.14 = (bf16[8,1024]{1,0:T(8,128)(2,1)S(1)}, bf16[8,1024]{1,0:T(8,128)(2,1)S(1)}, u32[]{:S(2)}, u32[]{:S(2)}) collective-permute-start(bf16[8,1024]{1,0:T(8,128)(2,1)S(1)} %get-tuple-element.49), channel_id=1, source_target_pairs={{0,6},{1,7},{2,4},{3,5},{4,2},{5,3},{6,0},{7,1},{8,25},{9,24},{10,... | collective-permute-start | bytes 49160 | tf_op jit(solution)/shard_map/ppermute | solution.py:32
  38.1 0.9 %collective-permute-start.13 = (bf16[8,1024]{1,0:T(8,128)(2,1)S(1)}, bf16[8,1024]{1,0:T(8,128)(2,1)S(1)}, u32[]{:S(2)}, u32[]{:S(2)}) collective-permute-start(bf16[8,1024]{1,0:T(8,128)(2,1)S(1)} %get-tuple-element.50), channel_id=1, source_target_pairs={{0,2},{1,3},{2,0},{3,1},{4,6},{5,7},{6,4},{7,5},{8,24},{9,25},{10,... | collective-permute-start | bytes 49160 | tf_op jit(solution)/shard_map/ppermute | solution.py:32
  39.0 2.9 %down.1 = bf16[1,2688,1024]{2,1,0:T(8,128)(2,1)} custom-call(f32[256,2688]{1,0:T(8,128)S(1)} %pre.1.relu.a, bf16[256,1024]{1,0:T(8,128)(2,1)S(1)} %get-tuple-element.37.b), custom_call_target="tpu_custom_call" | custom-call | flops 1409286144 | bytes 5505024 | tf_op jit(solution)/shard_map/down/pallas_call | solution.py:144
  41.9 0.4 collective-permute-done.14
  42.3 0.0 collective-permute-done.12
  42.3 0.0 collective-permute-done.13
  42.3 0.6 %slice_add_fusion.1 = f32[8,1024]{1,0:T(8,128)} fusion(f32[32,1024]{1,0:T(8,128)S(1)} %get-tuple-element.42, bf16[8,1024]{1,0:T(8,128)(2,1)S(1)} %collective-permute-done.14, bf16[8,1024]{1,0:T(8,128)(2,1)S(1)} %collective-permute-done.13, bf16[8,1024]{1,0:T(8,128)(2,1)S(1)} %collective-permute-done.12), kind=kLoop, calls=%fused_computation.5 | loop fusion | flops 49152 | bytes 114688 | tf_op jit(solution)/shard_map/add | solution.py:206
  (11 shorter events, 0.3 us)
Async XLA Ops:
  1.5 8.3 %collective-permute-start = (bf16[8,2176]{1,0:T(8,128)(2,1)S(1)}, bf16[8,2176]{1,0:T(8,128)(2,1)S(1)}, u32[]{:S(2)}, u32[]{:S(2)}) collective-permute-start(bf16[8,2176]{1,0:T(8,128)(2,1)S(1)} %pack.1), channel_id=1, source_target_pairs={{0,4},{1,5},{2,6},{3,7},{4,0},{5,1},{6,2},{7,3},{8,9},{9,8},{10,11... | collective-permute-start | bytes 104456 | tf_op jit(solution)/shard_map/ppermute | solution.py:32
  5.6 5.7 %collective-permute-start.2 = (bf16[8,2176]{1,0:T(8,128)(2,1)S(1)}, bf16[8,2176]{1,0:T(8,128)(2,1)S(1)}, u32[]{:S(2)}, u32[]{:S(2)}) collective-permute-start(bf16[8,2176]{1,0:T(8,128)(2,1)S(1)} %pack.1), channel_id=1, source_target_pairs={{0,6},{1,7},{2,4},{3,5},{4,2},{5,3},{6,0},{7,1},{8,25},{9,24},{10,... | collective-permute-start | bytes 104456 | tf_op jit(solution)/shard_map/ppermute | solution.py:32
  7.0 4.4 %collective-permute-start.1 = (bf16[8,2176]{1,0:T(8,128)(2,1)S(1)}, bf16[8,2176]{1,0:T(8,128)(2,1)S(1)}, u32[]{:S(2)}, u32[]{:S(2)}) collective-permute-start(bf16[8,2176]{1,0:T(8,128)(2,1)S(1)} %pack.1), channel_id=1, source_target_pairs={{0,2},{1,3},{2,0},{3,1},{4,6},{5,7},{6,4},{7,5},{8,24},{9,25},{10,... | collective-permute-start | bytes 104456 | tf_op jit(solution)/shard_map/ppermute | solution.py:32
  11.4 6.1 %collective-permute-start.5 = (bf16[32,2176]{1,0:T(8,128)(2,1)S(1)}, bf16[32,2176]{1,0:T(8,128)(2,1)S(1)}, u32[]{:S(2)}, u32[]{:S(2)}) collective-permute-start(bf16[32,2176]{1,0:T(8,128)(2,1)S(1)} %pad_maximum_fusion.2), channel_id=1, source_target_pairs={{0,17},{1,16},{2,19},{3,18},{4,21},{5,20},{6,23},{7,22},{8,14},{9,... | collective-permute-start | bytes 417800 | tf_op jit(solution)/shard_map/ppermute | solution.py:32
  13.9 5.1 %collective-permute-start.4 = (bf16[32,2176]{1,0:T(8,128)(2,1)S(1)}, bf16[32,2176]{1,0:T(8,128)(2,1)S(1)}, u32[]{:S(2)}, u32[]{:S(2)}) collective-permute-start(bf16[32,2176]{1,0:T(8,128)(2,1)S(1)} %pad_maximum_fusion.2), channel_id=1, source_target_pairs={{0,16},{1,17},{2,18},{3,19},{4,20},{5,21},{6,22},{7,23},{8,10},{9,... | collective-permute-start | bytes 417800 | tf_op jit(solution)/shard_map/ppermute | solution.py:32
  14.4 5.1 %collective-permute-start.3 = (bf16[32,2176]{1,0:T(8,128)(2,1)S(1)}, bf16[32,2176]{1,0:T(8,128)(2,1)S(1)}, u32[]{:S(2)}, u32[]{:S(2)}) collective-permute-start(bf16[32,2176]{1,0:T(8,128)(2,1)S(1)} %pad_maximum_fusion.2), channel_id=1, source_target_pairs={{0,1},{1,0},{2,3},{3,2},{4,5},{5,4},{6,7},{7,6},{8,12},{9,13},{10,... | collective-permute-start | bytes 417800 | tf_op jit(solution)/shard_map/ppermute | solution.py:32
  19.6 1.6 %collective-permute-start.6 = (bf16[128,1024]{1,0:T(8,128)(2,1)S(1)}, bf16[128,1024]{1,0:T(8,128)(2,1)S(1)}, u32[]{:S(2)}, u32[]{:S(2)}) collective-permute-start(bf16[128,1024]{1,0:T(8,128)(2,1)S(1)} %slice.54), channel_id=1, source_target_pairs={{0,8},{1,9},{2,10},{3,11},{4,12},{5,13},{6,14},{7,15},{8,0},{9,1},... | collective-permute-start | bytes 786440 | tf_op jit(solution)/shard_map/ppermute | solution.py:32
  21.2 1.9 %collective-permute-start.7 = (bf16[128,1152]{1,0:T(8,128)(2,1)S(1)}, bf16[128,1152]{1,0:T(8,128)(2,1)S(1)}, u32[]{:S(2)}, u32[]{:S(2)}) collective-permute-start(bf16[128,1152]{1,0:T(8,128)(2,1)S(1)} %slice.55), channel_id=1, source_target_pairs={{0,8},{1,9},{2,10},{3,11},{4,12},{5,13},{6,14},{7,15},{8,0},{9,1},... | collective-permute-start | bytes 884744 | tf_op jit(solution)/shard_map/ppermute | solution.py:32
  26.4 1.6 %collective-permute-start.8 = (bf16[128,1024]{1,0:T(8,128)(2,1)S(1)}, bf16[128,1024]{1,0:T(8,128)(2,1)S(1)}, u32[]{:S(2)}, u32[]{:S(2)}) collective-permute-start(bf16[128,1024]{1,0:T(8,128)(2,1)S(1)} %slice.45), channel_id=1, source_target_pairs={{0,8},{1,9},{2,10},{3,11},{4,12},{5,13},{6,14},{7,15},{8,0},{9,1},... | collective-permute-start | bytes 786440 | tf_op jit(solution)/shard_map/ppermute | solution.py:32
  28.1 7.3 %collective-permute-start.9 = (bf16[32,1024]{1,0:T(8,128)(2,1)S(1)}, bf16[32,1024]{1,0:T(8,128)(2,1)S(1)}, u32[]{:S(2)}, u32[]{:S(2)}) collective-permute-start(bf16[32,1024]{1,0:T(8,128)(2,1)S(1)} %get-tuple-element.45), channel_id=1, source_target_pairs={{0,1},{1,0},{2,3},{3,2},{4,5},{5,4},{6,7},{7,6},{8,12},{9,13},{10,... | collective-permute-start | bytes 196616 | tf_op jit(solution)/shard_map/ppermute | solution.py:32
  29.2 6.2 %collective-permute-start.11 = (bf16[32,1024]{1,0:T(8,128)(2,1)S(1)}, bf16[32,1024]{1,0:T(8,128)(2,1)S(1)}, u32[]{:S(2)}, u32[]{:S(2)}) collective-permute-start(bf16[32,1024]{1,0:T(8,128)(2,1)S(1)} %get-tuple-element.46), channel_id=1, source_target_pairs={{0,17},{1,16},{2,19},{3,18},{4,21},{5,20},{6,23},{7,22},{8,14},{9,... | collective-permute-start | bytes 196616 | tf_op jit(solution)/shard_map/ppermute | solution.py:32
  31.1 4.3 %collective-permute-start.10 = (bf16[32,1024]{1,0:T(8,128)(2,1)S(1)}, bf16[32,1024]{1,0:T(8,128)(2,1)S(1)}, u32[]{:S(2)}, u32[]{:S(2)}) collective-permute-start(bf16[32,1024]{1,0:T(8,128)(2,1)S(1)} %get-tuple-element.47), channel_id=1, source_target_pairs={{0,16},{1,17},{2,18},{3,19},{4,20},{5,21},{6,22},{7,23},{8,10},{9,... | collective-permute-start | bytes 196616 | tf_op jit(solution)/shard_map/ppermute | solution.py:32
  35.5 6.9 %collective-permute-start.12 = (bf16[8,1024]{1,0:T(8,128)(2,1)S(1)}, bf16[8,1024]{1,0:T(8,128)(2,1)S(1)}, u32[]{:S(2)}, u32[]{:S(2)}) collective-permute-start(bf16[8,1024]{1,0:T(8,128)(2,1)S(1)} %get-tuple-element.48), channel_id=1, source_target_pairs={{0,4},{1,5},{2,6},{3,7},{4,0},{5,1},{6,2},{7,3},{8,9},{9,8},{10,11... | collective-permute-start | bytes 49160 | tf_op jit(solution)/shard_map/ppermute | solution.py:32
  36.8 5.5 %collective-permute-start.14 = (bf16[8,1024]{1,0:T(8,128)(2,1)S(1)}, bf16[8,1024]{1,0:T(8,128)(2,1)S(1)}, u32[]{:S(2)}, u32[]{:S(2)}) collective-permute-start(bf16[8,1024]{1,0:T(8,128)(2,1)S(1)} %get-tuple-element.49), channel_id=1, source_target_pairs={{0,6},{1,7},{2,4},{3,5},{4,2},{5,3},{6,0},{7,1},{8,25},{9,24},{10,... | collective-permute-start | bytes 49160 | tf_op jit(solution)/shard_map/ppermute | solution.py:32
  38.1 4.2 %collective-permute-start.13 = (bf16[8,1024]{1,0:T(8,128)(2,1)S(1)}, bf16[8,1024]{1,0:T(8,128)(2,1)S(1)}, u32[]{:S(2)}, u32[]{:S(2)}) collective-permute-start(bf16[8,1024]{1,0:T(8,128)(2,1)S(1)} %get-tuple-element.50), channel_id=1, source_target_pairs={{0,2},{1,3},{2,0},{3,1},{4,6},{5,7},{6,4},{7,5},{8,24},{9,25},{10,... | collective-permute-start | bytes 49160 | tf_op jit(solution)/shard_map/ppermute | solution.py:32

commit v5 on v4

--- a/solution.py
+++ b/solution.py
@@ -85,15 +85,26 @@
          pltpu.SemaphoreType.DMA((4,))), limit=4)(*in_hbm(latent, out_grad, gates, ids))
 
 
-def load_kernel(weight, out, sem):
-    copy = pltpu.make_async_copy(weight, out, sem)
-    copy.start()
-    copy.wait()
-
-
-def load(weight, name):
-    return call(load_kernel, S(weight.shape, weight.dtype), [HBM], name, (pltpu.SemaphoreType.DMA,),
-        moved=2 * weight.size, limit=8)(*in_hbm(weight))
+def load(weight, name, keep):
+    rows, width = weight.shape
+    step = 384
+
+    def kernel(weight, *refs):
+        whole, turned, sems = refs if keep else (refs[1], refs[0], refs[2])
+        copies = []
+        for k in range(rows // step):
+            at = pl.ds(k * step, step)
+            copies.append(pltpu.make_async_copy(weight.at[at], whole.at[at], sems.at[k]))
+            copies[-1].start()
+        for k, copy in enumerate(copies):
+            copy.wait()
+            turned[:, k * step : (k + 1) * step] = whole[k * step : (k + 1) * step].T
+
+    turned = S((width, rows), BF16)
+    sems = pltpu.SemaphoreType.DMA((rows // step,))
+    scratch = (sems,) if keep else (pltpu.VMEM((rows, width), BF16), sems)
+    out = (S((rows, width), BF16), turned) if keep else turned
+    return call(kernel, out, [HBM], name, scratch, moved=2 * weight.size)(*in_hbm(weight))
 
 
 def gated(dyg, width, rows):
@@ -106,15 +117,20 @@
     return (gate * dyg[:, :width].astype(F32)).astype(BF16)
 
 
-def pre_kernel(x, w_up, relu):
-    relu[...] = jnp.maximum(dot(x[...], w_up[...], 1, 1), 0.0)
-
-
-def hidden_kernel(dyg, w_down, w_up, relu, row_grad, pre_grad, part):
-    row_grad[...] = gated(dyg[...], row_grad.shape[1], w_down.shape[0])
-    hid_grad = dot(row_grad[...], w_down[...], 1, 1)
+def hidden(x, dyg, up_turned, down_turned, relu, row_grad, pre_grad):
+    row_grad[...] = gated(dyg[...], row_grad.shape[1], relu.shape[1])
+    relu[...] = jnp.maximum(dot(x[...], up_turned[...], 1, 0), 0.0)
+    hid_grad = dot(row_grad[...], down_turned[...], 1, 0)
     pre_grad[...] = (hid_grad * 2.0 * relu[...]).astype(BF16)
+
+
+def hidden_part(x, dyg, up_turned, down_turned, w_up, relu, row_grad, pre_grad, part):
+    hidden(x, dyg, up_turned, down_turned, relu, row_grad, pre_grad)
     part[...] = dot(pre_grad[...], w_up[...], 1, 0).astype(BF16)
+
+
+def part_kernel(pre_grad, w_up, part):
+    part[...] = dot(pre_grad[...], w_up[...], 1, 0)
 
 
 def plain(x, dyg, w_up, w_down):
@@ -125,25 +141,27 @@
     return row_grad, act, pre_grad, dot(pre_grad, w_up, 1, 0).astype(BF16)
 
 
-def outer(a, b, name, blocks):
-    n, width = a.shape[1], b.shape[1]
-    step = n // blocks
-
-    def kernel(a, b, out, buffer, sems):
+def outer(a, b, name):
+    n, width = a[0].shape[1], b[0].shape[1]
+    step = 384
+    blocks = n // step
+
+    def kernel(a_0, a_1, b_0, b_1, out, buffer, sems):
         copies = []
+        right = jnp.concatenate([b_0[...], b_1[...]], axis=0)
         for k in range(blocks):
             rows = pl.ds(k * step, step)
-            left = a[:, k * step : (k + 1) * step]
-            left = (left * left).astype(BF16) if a.dtype == F32 else left
-            buffer[rows] = dot(left, b[...], 0, 0).astype(BF16)
+            left = jnp.concatenate([a_0[:, k * step : (k + 1) * step], a_1[:, k * step : (k + 1) * step]], axis=0)
+            left = (left * left).astype(BF16) if left.dtype == F32 else left
+            buffer[rows] = dot(left, right, 0, 0).astype(BF16)
             copies.append(pltpu.make_async_copy(buffer.at[rows], out.at[0, rows], sems.at[k]))
             copies[-1].start()
         for copy in copies:
             copy.wait()
 
-    return call(kernel, S((1, n, width), BF16), [VMEM, VMEM], name,
+    return call(kernel, S((1, n, width), BF16), [VMEM] * 4, name,
         (pltpu.VMEM((n, width), BF16), pltpu.SemaphoreType.DMA((blocks,))), ANY,
-        flops=2 * a.shape[0] * n * width, moved=2 * n * width)(a, b)
+        flops=4 * a[0].shape[0] * n * width, moved=2 * n * width)(*a, *b)
 
 
 def local(latent, out_grad, gates, expert_ids, up_weight, down_weight):
@@ -157,7 +175,6 @@
     tokens = latent.shape[0] * devices
     flops = 2 * tokens * rows * width
     small = tokens <= 256 and rows % 384 == 0
-    blocks = rows // 384
     w_up, w_down = up_weight[0], down_weight[0]
 
     rows_all = pack(latent, out_grad, gates, expert_ids)
@@ -169,39 +186,42 @@
         got = [swap(rows_all, mask, members, devices) for mask in masks]
         t = TIED[k % 4]
         if small and k == 0:
-            w_up = load(w_up, "load_up")
-            got[t], w_up = tie((got[t], w_up))
+            w_up, up_turned = load(w_up, "load_up", True)
+            got[t], w_up, up_turned = tie((got[t], w_up, up_turned))
         if small and k == 1:
-            w_down = load(w_down, "load_down")
-            got[t], w_down = tie((got[t], w_down))
+            down_turned = load(w_down, "load_down", False)
+            got[t], down_turned = tie((got[t], down_turned))
         rows_all = tie(jnp.concatenate([rows_all] + got, axis=0))
     x, dyg = tie((rows_all[:, :width], rows_all[:, width:]))
     got_x = swap(x, core, members, devices)
-    got_x, dyg = tie((got_x, dyg))
-    x = jnp.concatenate([x, got_x], axis=0)
     got_dyg = swap(dyg, core, members, devices)
-    dyg_all = jnp.concatenate([dyg, got_dyg], axis=0)
+    half = tokens // 2
     if small:
-        relu = call(pre_kernel, S((tokens, rows), F32), [VMEM] * 2, "pre", flops=flops)(x, w_up)
-        row_grad, pre_grad, part = call(
-            hidden_kernel,
-            (S((tokens, width), BF16), S((tokens, rows), BF16), S((tokens, width), BF16)),
-            [VMEM] * 4, "hidden", flops=2 * flops)(dyg_all, w_down, w_up, relu)
+        outs = (S((half, rows), F32), S((half, width), BF16), S((half, rows), BF16))
+        left = call(hidden, outs, [VMEM] * 4, "hidden", flops=flops)(x, dyg, up_turned, down_turned)
+        got_x, left = tie((got_x, left))
+        right = call(hidden_part, (*outs, S((half, width), BF16)), [VMEM] * 5, "hidden_part", flops=3 * flops // 2)(
+            got_x, got_dyg, up_turned, down_turned, w_up)
+        got = swap(right[3], core, members, devices)
+        ours = call(part_kernel, S((half, width), F32), [VMEM] * 2, "part", flops=flops // 2)(left[2], w_up)
+        x, relu, row_grad, pre_grad = (x, got_x), (left[0], right[0]), (left[1], right[1]), (left[2], right[2])
     else:
-        row_grad, act, pre_grad, part = plain(x, dyg_all, w_up, w_down)
-
-    half = tokens // 2
-    total = part[:half].astype(F32) + swap(part[half:], core, members, devices).astype(F32)
+        x, dyg = jnp.concatenate([x, got_x]), jnp.concatenate([dyg, got_dyg])
+        row_grad, act, pre_grad, part = plain(x, dyg, w_up, w_down)
+        ours = part[:half].astype(F32)
+        got = swap(part[half:], core, members, devices)
+
+    total = ours + got.astype(F32)
     for k, masks in enumerate(reversed(plan)):
         count = total.shape[0] // (len(masks) + 1)
         cut = [total[j * count : (j + 1) * count] for j in range(len(masks) + 1)]
         got = [swap(block.astype(BF16), mask, members, devices) for block, mask in zip(cut[1:], masks)]
         t = TIED[(2 + k) % 4]
         if small and k == 0:
-            up_grad = outer(pre_grad, x, "up", blocks)
+            up_grad = outer(pre_grad, x, "up")
             got[t], up_grad = tie((got[t], up_grad))
         if small and k == 1:
-            down_grad = outer(relu, row_grad, "down", blocks)
+            down_grad = outer(relu, row_grad, "down")
             got[t], down_grad = tie((got[t], down_grad))
         total = cut[0] + sum(block.astype(F32) for block in got)
     if not small:

time: 43.2 us -> 41.6 us (0.963)
  waiting for transfers between devices: 7.49 us -> 4.9 us
  Pallas kernels: 16.7 us -> 17.7 us
    ppermute x15, waiting for transfers between devices: 7.49 us -> 4.9 us  [swap(): lax.ppermute(value, AXES, [(i, i ^ (odd if i & core else even)) for i in...]
    pallas_call x6 -> x7, Pallas kernels: 15.8 us -> 16.9 us  [the longest x2 6.02 us: load(): call(kernel, out, [HBM], name, scratch, moved=2 * weight.size)]
  transfers between devices with their start and end apart: 15 -> 15, of which waited for: 7 -> 6; matrix products, arithmetic and copies ran while one was open for 0% -> 0% of each run, Pallas kernels for 29% -> 35%
where the time goes in v5:
time: 41.6 us; the launch traced here: 41.3 us
  Pallas kernels  17.7 us (43%)
  starting transfers between devices  17.1 us (41%)
  waiting for transfers between devices  4.9 us (12%)
  between operations  0.8 us (2%)
  other arithmetic  0.78 us (2%)
    ppermute x15, starting transfers between devices, swap(): lax.ppermute(value, AXES, [(i, i ^ (odd if i & core else even)) for i in...  17.1 us
    pallas_call x2, Pallas kernels, load(): call(kernel, out, [HBM], name, scratch, moved=2 * weight.size)  6.02 us
    pallas_call x2, Pallas kernels, outer(): call(kernel, S((1, n, width), BF16), [VMEM] * 4, name, (pltpu.VMEM((n, wi...  5.77 us
    ppermute x15, waiting for transfers between devices, swap(): lax.ppermute(value, AXES, [(i, i ^ (odd if i & core else even)) for i in...  4.9 us
    pallas_call x1, Pallas kernels, local(): call(hidden_part, (*outs, S((half, width), BF16)), [VMEM] * 5, 'hidden_pa...  2.46 us
    pallas_call x1, Pallas kernels, local(): call(hidden, outs, [VMEM] * 4, 'hidden', flops=flops)  1.69 us
    pallas_call x1, Pallas kernels, local(): call(part_kernel, S((half, width), F32), [VMEM] * 2, 'part', flops=flops...  0.92 us
    pallas_call x1, Pallas kernels, pack(): call(pack_kernel, S((rows, 2 * width + LANES), BF16), [HBM] * 4, 'pack',...  0.88 us
  transfers between devices with their start and end apart: 15, of which 6 were waited for; matrix products, arithmetic and copies ran while one was open for 0% of the time, Pallas kernels for 35%

profile of v5, /device:TPU:0, one launch (start us, length us, event | category | flops | bytes accessed | tf_op | source)
XLA Modules:
  0.0 41.3 jit_solution(2579680735746415983)
XLA Ops:
  0.6 0.9 %pack.1 = bf16[8,2176]{1,0:T(8,128)(2,1)S(1)} custom-call(bf16[8,1024]{1,0:T(8,128)(2,1)} %latent.1, bf16[8,1024]{1,0:T(8,128)(2,1)} %out_grad.1, bf16[8,22]{1,0:T(8,128)(2,1)} %gates.1, s32[8,22]{1,0:T(8,128)} %ids.1), custom_call_target="tpu_custom_call" | custom-call | tf_op jit(solution)/shard_map/pack/pallas_call | solution.py:83
  1.5 4.1 %collective-permute-start = (bf16[8,2176]{1,0:T(8,128)(2,1)S(1)}, bf16[8,2176]{1,0:T(8,128)(2,1)S(1)}, u32[]{:S(2)}, u32[]{:S(2)}) collective-permute-start(bf16[8,2176]{1,0:T(8,128)(2,1)S(1)} %pack.1), channel_id=1, source_target_pairs={{0,4},{1,5},{2,6},{3,7},{4,0},{5,1},{6,2},{7,3},{8,9},{9,8},{10,11... | collective-permute-start | bytes 104456 | tf_op jit(solution)/shard_map/ppermute | solution.py:32
  5.6 1.3 %collective-permute-start.2 = (bf16[8,2176]{1,0:T(8,128)(2,1)S(1)}, bf16[8,2176]{1,0:T(8,128)(2,1)S(1)}, u32[]{:S(2)}, u32[]{:S(2)}) collective-permute-start(bf16[8,2176]{1,0:T(8,128)(2,1)S(1)} %pack.1), channel_id=1, source_target_pairs={{0,6},{1,7},{2,4},{3,5},{4,2},{5,3},{6,0},{7,1},{8,25},{9,24},{10,... | collective-permute-start | bytes 104456 | tf_op jit(solution)/shard_map/ppermute | solution.py:32
  7.0 0.2 collective-permute-start.1
  7.2 3.0 %load_up.1 = (bf16[2688,1024]{1,0:T(8,128)(2,1)S(1)}, bf16[1024,2688]{1,0:T(8,128)(2,1)S(1)}) custom-call(bf16[2688,1024]{1,0:T(8,128)(2,1)} %bitcast.3), custom_call_target="tpu_custom_call" | custom-call | bytes 5505024 | tf_op jit(solution)/shard_map/load_up/pallas_call | solution.py:107
  10.2 0.0 collective-permute-done
  10.2 1.1 %collective-permute-done.2 = bf16[8,2176]{1,0:T(8,128)(2,1)S(1)} collective-permute-done((bf16[8,2176]{1,0:T(8,128)(2,1)S(1)}, bf16[8,2176]{1,0:T(8,128)(2,1)S(1)}, u32[]{:S(2)}, u32[]{:S(2)}) %collective-permute-start.2) | collective-permute-done | bytes 34848 | tf_op jit(solution)/shard_map/ppermute | solution.py:32
  11.4 0.0 collective-permute-done.1
  11.4 2.5 %collective-permute-start.5 = (bf16[32,2176]{1,0:T(8,128)(2,1)S(1)}, bf16[32,2176]{1,0:T(8,128)(2,1)S(1)}, u32[]{:S(2)}, u32[]{:S(2)}) collective-permute-start(bf16[32,2176]{1,0:T(8,128)(2,1)S(1)} %pad_maximum_fusion.1), channel_id=1, source_target_pairs={{0,17},{1,16},{2,19},{3,18},{4,21},{5,20},{6,23},{7,22},{8,14},{9,... | collective-permute-start | bytes 417800 | tf_op jit(solution)/shard_map/ppermute | solution.py:32
  13.9 0.5 %collective-permute-start.4 = (bf16[32,2176]{1,0:T(8,128)(2,1)S(1)}, bf16[32,2176]{1,0:T(8,128)(2,1)S(1)}, u32[]{:S(2)}, u32[]{:S(2)}) collective-permute-start(bf16[32,2176]{1,0:T(8,128)(2,1)S(1)} %pad_maximum_fusion.1), channel_id=1, source_target_pairs={{0,16},{1,17},{2,18},{3,19},{4,20},{5,21},{6,22},{7,23},{8,10},{9,... | collective-permute-start | bytes 417800 | tf_op jit(solution)/shard_map/ppermute | solution.py:32
  14.4 0.5 %collective-permute-start.3 = (bf16[32,2176]{1,0:T(8,128)(2,1)S(1)}, bf16[32,2176]{1,0:T(8,128)(2,1)S(1)}, u32[]{:S(2)}, u32[]{:S(2)}) collective-permute-start(bf16[32,2176]{1,0:T(8,128)(2,1)S(1)} %pad_maximum_fusion.1), channel_id=1, source_target_pairs={{0,1},{1,0},{2,3},{3,2},{4,5},{5,4},{6,7},{7,6},{8,12},{9,13},{10,... | collective-permute-start | bytes 417800 | tf_op jit(solution)/shard_map/ppermute | solution.py:32
  14.9 3.0 %load_down.1.down_turned = bf16[1024,2688]{1,0:T(8,128)(2,1)S(1)} custom-call(bf16[2688,1024]{1,0:T(8,128)(2,1)} %bitcast.2), custom_call_target="tpu_custom_call" | custom-call | bytes 5505024 | tf_op jit(solution)/shard_map/load_down/pallas_call | solution.py:107
  17.9 0.0 collective-permute-done.5
  18.0 1.0 %collective-permute-done.4 = bf16[32,2176]{1,0:T(8,128)(2,1)S(1)} collective-permute-done((bf16[32,2176]{1,0:T(8,128)(2,1)S(1)}, bf16[32,2176]{1,0:T(8,128)(2,1)S(1)}, u32[]{:S(2)}, u32[]{:S(2)}) %collective-permute-start.4) | collective-permute-done | bytes 139296 | tf_op jit(solution)/shard_map/ppermute | solution.py:32
  18.9 0.5 %collective-permute-done.3 = bf16[32,2176]{1,0:T(8,128)(2,1)S(1)} collective-permute-done((bf16[32,2176]{1,0:T(8,128)(2,1)S(1)}, bf16[32,2176]{1,0:T(8,128)(2,1)S(1)}, u32[]{:S(2)}, u32[]{:S(2)}) %collective-permute-start.3) | collective-permute-done | bytes 139296 | tf_op jit(solution)/shard_map/ppermute | solution.py:32
  19.6 0.1 collective-permute-start.7
  19.6 0.5 %collective-permute-start.6 = (bf16[128,1024]{1,0:T(8,128)(2,1)S(1)}, bf16[128,1024]{1,0:T(8,128)(2,1)S(1)}, u32[]{:S(2)}, u32[]{:S(2)}) collective-permute-start(bf16[128,1024]{1,0:T(8,128)(2,1)S(1)} %slice.46.x.b_0), channel_id=1, source_target_pairs={{0,8},{1,9},{2,10},{3,11},{4,12},{5,13},{6,14},{7,15},{8,0},{9,1},... | collective-permute-start | bytes 786440 | tf_op jit(solution)/shard_map/ppermute | solution.py:32
  20.1 1.7 %hidden.1 = (f32[128,2688]{1,0:T(8,128)S(1)}, bf16[128,1024]{1,0:T(8,128)(2,1)S(1)}, bf16[128,2688]{1,0:T(8,128)(2,1)S(1)}) custom-call(bf16[128,1024]{1,0:T(8,128)(2,1)S(1)} %slice.46.x.b_0, bf16[128,1152]{1,0:T(8,128)(2,1)S(1)} %slice.47.dyg, bf16[1024,2688]{1,0:T(8,128)(2,1)S(1)} %get-tuple-element.41.up_turned, bf16[1024,2688]{1,0:T(8,128)(2,1)S(1)} %load_down.1.down_turned), custom_call_target="tpu_custom_call" | custom-call | flops 1409286144 | tf_op jit(solution)/shard_map/hidden/pallas_call | solution.py:201
  21.8 0.0 collective-permute-done.6.x.b_1
  21.8 0.0 collective-permute-done.7.dyg
  21.8 2.5 %hidden_part.1 = (f32[128,2688]{1,0:T(8,128)S(1)}, bf16[128,1024]{1,0:T(8,128)(2,1)S(1)}, bf16[128,2688]{1,0:T(8,128)(2,1)S(1)}, bf16[128,1024]{1,0:T(8,128)(2,1)S(1)}) custom-call(bf16[128,1024]{1,0:T(8,128)(2,1)S(1)} %collective-permute-done.6.x.b_1, bf16[128,1152]{1,0:T(8,128)(2,1)S(1)} %collective-permute-done.7.dyg, ...), custom_call_target="tpu_custom_call" | custom-call | flops 2113929216 | tf_op jit(solution)/shard_map/hidden_part/pallas_call | solution.py:203
  24.3 0.1 collective-permute-start.8
  24.5 0.9 %part.1 = f32[128,1024]{1,0:T(8,128)S(1)} custom-call(bf16[128,2688]{1,0:T(8,128)(2,1)S(1)} %get-tuple-element.46.pre_grad.a_0, bf16[2688,1024]{1,0:T(8,128)(2,1)S(1)} %get-tuple-element.47.w_up), custom_call_target="tpu_custom_call" | custom-call | flops 704643072 | tf_op jit(solution)/shard_map/part/pallas_call | solution.py:206
  25.4 0.5 %collective-permute-done.8 = bf16[128,1024]{1,0:T(8,128)(2,1)S(1)} collective-permute-done((bf16[128,1024]{1,0:T(8,128)(2,1)S(1)}, bf16[128,1024]{1,0:T(8,128)(2,1)S(1)}, u32[]{:S(2)}, u32[]{:S(2)}) %collective-permute-start.8) | collective-permute-done | bytes 262176 | tf_op jit(solution)/shard_map/ppermute | solution.py:32
  25.9 0.1 fusion.1
  26.0 1.1 %collective-permute-start.9 = (bf16[32,1024]{1,0:T(8,128)(2,1)S(1)}, bf16[32,1024]{1,0:T(8,128)(2,1)S(1)}, u32[]{:S(2)}, u32[]{:S(2)}) collective-permute-start(bf16[32,1024]{1,0:T(8,128)(2,1)S(1)} %get-tuple-element.63), channel_id=1, source_target_pairs={{0,1},{1,0},{2,3},{3,2},{4,5},{5,4},{6,7},{7,6},{8,12},{9,13},{10,... | collective-permute-start | bytes 196616 | tf_op jit(solution)/shard_map/ppermute | solution.py:32
  27.1 1.9 %collective-permute-start.11 = (bf16[32,1024]{1,0:T(8,128)(2,1)S(1)}, bf16[32,1024]{1,0:T(8,128)(2,1)S(1)}, u32[]{:S(2)}, u32[]{:S(2)}) collective-permute-start(bf16[32,1024]{1,0:T(8,128)(2,1)S(1)} %get-tuple-element.64), channel_id=1, source_target_pairs={{0,17},{1,16},{2,19},{3,18},{4,21},{5,20},{6,23},{7,22},{8,14},{9,... | collective-permute-start | bytes 196616 | tf_op jit(solution)/shard_map/ppermute | solution.py:32
  29.1 0.5 %collective-permute-start.10 = (bf16[32,1024]{1,0:T(8,128)(2,1)S(1)}, bf16[32,1024]{1,0:T(8,128)(2,1)S(1)}, u32[]{:S(2)}, u32[]{:S(2)}) collective-permute-start(bf16[32,1024]{1,0:T(8,128)(2,1)S(1)} %get-tuple-element.65), channel_id=1, source_target_pairs={{0,16},{1,17},{2,18},{3,19},{4,20},{5,21},{6,22},{7,23},{8,10},{9,... | collective-permute-start | bytes 196616 | tf_op jit(solution)/shard_map/ppermute | solution.py:32
  29.6 2.9 %up.1 = bf16[1,2688,1024]{2,1,0:T(8,128)(2,1)} custom-call(bf16[128,2688]{1,0:T(8,128)(2,1)S(1)} %get-tuple-element.46.pre_grad.a_0, bf16[128,2688]{1,0:T(8,128)(2,1)S(1)} %get-tuple-element.50.a_1, bf16[128,1024]{1,0:T(8,128)(2,1)S(1)} %slice.46.x.b_0, bf16[128,1024]{1,0:T(8,128)(2,1)S(1)} %collective-permute-done.6.x.b_1), custom_call_target="tpu_custom_call" | custom-call | flops 1409286144 | bytes 5505024 | tf_op jit(solution)/shard_map/up/pallas_call | solution.py:162
  32.5 0.9 %collective-permute-done.10 = bf16[32,1024]{1,0:T(8,128)(2,1)S(1)} collective-permute-done((bf16[32,1024]{1,0:T(8,128)(2,1)S(1)}, bf16[32,1024]{1,0:T(8,128)(2,1)S(1)}, u32[]{:S(2)}, u32[]{:S(2)}) %collective-permute-start.10) | collective-permute-done | bytes 65568 | tf_op jit(solution)/shard_map/ppermute | solution.py:32
  33.3 0.0 collective-permute-done.9
  33.3 0.0 collective-permute-done.11
  33.4 1.8 %collective-permute-start.12 = (bf16[8,1024]{1,0:T(8,128)(2,1)S(1)}, bf16[8,1024]{1,0:T(8,128)(2,1)S(1)}, u32[]{:S(2)}, u32[]{:S(2)}) collective-permute-start(bf16[8,1024]{1,0:T(8,128)(2,1)S(1)} %get-tuple-element.66), channel_id=1, source_target_pairs={{0,4},{1,5},{2,6},{3,7},{4,0},{5,1},{6,2},{7,3},{8,9},{9,8},{10,11... | collective-permute-start | bytes 49160 | tf_op jit(solution)/shard_map/ppermute | solution.py:32
  35.2 1.3 %collective-permute-start.14 = (bf16[8,1024]{1,0:T(8,128)(2,1)S(1)}, bf16[8,1024]{1,0:T(8,128)(2,1)S(1)}, u32[]{:S(2)}, u32[]{:S(2)}) collective-permute-start(bf16[8,1024]{1,0:T(8,128)(2,1)S(1)} %get-tuple-element.67), channel_id=1, source_target_pairs={{0,6},{1,7},{2,4},{3,5},{4,2},{5,3},{6,0},{7,1},{8,25},{9,24},{10,... | collective-permute-start | bytes 49160 | tf_op jit(solution)/shard_map/ppermute | solution.py:32
  36.5 0.4 %collective-permute-start.13 = (bf16[8,1024]{1,0:T(8,128)(2,1)S(1)}, bf16[8,1024]{1,0:T(8,128)(2,1)S(1)}, u32[]{:S(2)}, u32[]{:S(2)}) collective-permute-start(bf16[8,1024]{1,0:T(8,128)(2,1)S(1)} %get-tuple-element.68), channel_id=1, source_target_pairs={{0,2},{1,3},{2,0},{3,1},{4,6},{5,7},{6,4},{7,5},{8,24},{9,25},{10,... | collective-permute-start | bytes 49160 | tf_op jit(solution)/shard_map/ppermute | solution.py:32
  36.9 2.9 %down.1 = bf16[1,2688,1024]{2,1,0:T(8,128)(2,1)} custom-call(f32[128,2688]{1,0:T(8,128)S(1)} %get-tuple-element.52.a_0, f32[128,2688]{1,0:T(8,128)S(1)} %get-tuple-element.53.a_1, bf16[128,1024]{1,0:T(8,128)(2,1)S(1)} %get-tuple-element.54.b_0, bf16[128,1024]{1,0:T(8,128)(2,1)S(1)} %get-tuple-element.55.b_1), custom_call_target="tpu_custom_call" | custom-call | flops 1409286144 | bytes 5505024 | tf_op jit(solution)/shard_map/down/pallas_call | solution.py:162
  39.8 0.9 %collective-permute-done.14 = bf16[8,1024]{1,0:T(8,128)(2,1)S(1)} collective-permute-done((bf16[8,1024]{1,0:T(8,128)(2,1)S(1)}, bf16[8,1024]{1,0:T(8,128)(2,1)S(1)}, u32[]{:S(2)}, u32[]{:S(2)}) %collective-permute-start.14) | collective-permute-done | bytes 16416 | tf_op jit(solution)/shard_map/ppermute | solution.py:32
  40.7 0.0 collective-permute-done.12
  40.7 0.0 collective-permute-done.13
  40.7 0.6 %slice_add_fusion.1 = f32[8,1024]{1,0:T(8,128)} fusion(f32[32,1024]{1,0:T(8,128)S(1)} %get-tuple-element.60, bf16[8,1024]{1,0:T(8,128)(2,1)S(1)} %collective-permute-done.14, bf16[8,1024]{1,0:T(8,128)(2,1)S(1)} %collective-permute-done.13, bf16[8,1024]{1,0:T(8,128)(2,1)S(1)} %collective-permute-done.12), kind=kLoop, calls=%fused_computation.4 | loop fusion | flops 49152 | bytes 114688 | tf_op jit(solution)/shard_map/add | solution.py:226
  (7 shorter events, 0.2 us)
Async XLA Ops:
  1.5 8.7 %collective-permute-start = (bf16[8,2176]{1,0:T(8,128)(2,1)S(1)}, bf16[8,2176]{1,0:T(8,128)(2,1)S(1)}, u32[]{:S(2)}, u32[]{:S(2)}) collective-permute-start(bf16[8,2176]{1,0:T(8,128)(2,1)S(1)} %pack.1), channel_id=1, source_target_pairs={{0,4},{1,5},{2,6},{3,7},{4,0},{5,1},{6,2},{7,3},{8,9},{9,8},{10,11... | collective-permute-start | bytes 104456 | tf_op jit(solution)/shard_map/ppermute | solution.py:32
  5.6 5.7 %collective-permute-start.2 = (bf16[8,2176]{1,0:T(8,128)(2,1)S(1)}, bf16[8,2176]{1,0:T(8,128)(2,1)S(1)}, u32[]{:S(2)}, u32[]{:S(2)}) collective-permute-start(bf16[8,2176]{1,0:T(8,128)(2,1)S(1)} %pack.1), channel_id=1, source_target_pairs={{0,6},{1,7},{2,4},{3,5},{4,2},{5,3},{6,0},{7,1},{8,25},{9,24},{10,... | collective-permute-start | bytes 104456 | tf_op jit(solution)/shard_map/ppermute | solution.py:32
  7.0 4.4 %collective-permute-start.1 = (bf16[8,2176]{1,0:T(8,128)(2,1)S(1)}, bf16[8,2176]{1,0:T(8,128)(2,1)S(1)}, u32[]{:S(2)}, u32[]{:S(2)}) collective-permute-start(bf16[8,2176]{1,0:T(8,128)(2,1)S(1)} %pack.1), channel_id=1, source_target_pairs={{0,2},{1,3},{2,0},{3,1},{4,6},{5,7},{6,4},{7,5},{8,24},{9,25},{10,... | collective-permute-start | bytes 104456 | tf_op jit(solution)/shard_map/ppermute | solution.py:32
  11.4 6.6 %collective-permute-start.5 = (bf16[32,2176]{1,0:T(8,128)(2,1)S(1)}, bf16[32,2176]{1,0:T(8,128)(2,1)S(1)}, u32[]{:S(2)}, u32[]{:S(2)}) collective-permute-start(bf16[32,2176]{1,0:T(8,128)(2,1)S(1)} %pad_maximum_fusion.1), channel_id=1, source_target_pairs={{0,17},{1,16},{2,19},{3,18},{4,21},{5,20},{6,23},{7,22},{8,14},{9,... | collective-permute-start | bytes 417800 | tf_op jit(solution)/shard_map/ppermute | solution.py:32
  13.9 5.1 %collective-permute-start.4 = (bf16[32,2176]{1,0:T(8,128)(2,1)S(1)}, bf16[32,2176]{1,0:T(8,128)(2,1)S(1)}, u32[]{:S(2)}, u32[]{:S(2)}) collective-permute-start(bf16[32,2176]{1,0:T(8,128)(2,1)S(1)} %pad_maximum_fusion.1), channel_id=1, source_target_pairs={{0,16},{1,17},{2,18},{3,19},{4,20},{5,21},{6,22},{7,23},{8,10},{9,... | collective-permute-start | bytes 417800 | tf_op jit(solution)/shard_map/ppermute | solution.py:32
  14.4 5.1 %collective-permute-start.3 = (bf16[32,2176]{1,0:T(8,128)(2,1)S(1)}, bf16[32,2176]{1,0:T(8,128)(2,1)S(1)}, u32[]{:S(2)}, u32[]{:S(2)}) collective-permute-start(bf16[32,2176]{1,0:T(8,128)(2,1)S(1)} %pad_maximum_fusion.1), channel_id=1, source_target_pairs={{0,1},{1,0},{2,3},{3,2},{4,5},{5,4},{6,7},{7,6},{8,12},{9,13},{10,... | collective-permute-start | bytes 417800 | tf_op jit(solution)/shard_map/ppermute | solution.py:32
  19.6 2.3 %collective-permute-start.7 = (bf16[128,1152]{1,0:T(8,128)(2,1)S(1)}, bf16[128,1152]{1,0:T(8,128)(2,1)S(1)}, u32[]{:S(2)}, u32[]{:S(2)}) collective-permute-start(bf16[128,1152]{1,0:T(8,128)(2,1)S(1)} %slice.47.dyg), channel_id=1, source_target_pairs={{0,8},{1,9},{2,10},{3,11},{4,12},{5,13},{6,14},{7,15},{8,0},{9,1},... | collective-permute-start | bytes 884744 | tf_op jit(solution)/shard_map/ppermute | solution.py:32
  19.6 2.2 %collective-permute-start.6 = (bf16[128,1024]{1,0:T(8,128)(2,1)S(1)}, bf16[128,1024]{1,0:T(8,128)(2,1)S(1)}, u32[]{:S(2)}, u32[]{:S(2)}) collective-permute-start(bf16[128,1024]{1,0:T(8,128)(2,1)S(1)} %slice.46.x.b_0), channel_id=1, source_target_pairs={{0,8},{1,9},{2,10},{3,11},{4,12},{5,13},{6,14},{7,15},{8,0},{9,1},... | collective-permute-start | bytes 786440 | tf_op jit(solution)/shard_map/ppermute | solution.py:32
  24.3 1.6 %collective-permute-start.8 = (bf16[128,1024]{1,0:T(8,128)(2,1)S(1)}, bf16[128,1024]{1,0:T(8,128)(2,1)S(1)}, u32[]{:S(2)}, u32[]{:S(2)}) collective-permute-start(bf16[128,1024]{1,0:T(8,128)(2,1)S(1)} %get-tuple-element.49), channel_id=1, source_target_pairs={{0,8},{1,9},{2,10},{3,11},{4,12},{5,13},{6,14},{7,15},{8,0},{9,1},... | collective-permute-start | bytes 786440 | tf_op jit(solution)/shard_map/ppermute | solution.py:32
  26.0 7.3 %collective-permute-start.9 = (bf16[32,1024]{1,0:T(8,128)(2,1)S(1)}, bf16[32,1024]{1,0:T(8,128)(2,1)S(1)}, u32[]{:S(2)}, u32[]{:S(2)}) collective-permute-start(bf16[32,1024]{1,0:T(8,128)(2,1)S(1)} %get-tuple-element.63), channel_id=1, source_target_pairs={{0,1},{1,0},{2,3},{3,2},{4,5},{5,4},{6,7},{7,6},{8,12},{9,13},{10,... | collective-permute-start | bytes 196616 | tf_op jit(solution)/shard_map/ppermute | solution.py:32
  27.1 6.2 %collective-permute-start.11 = (bf16[32,1024]{1,0:T(8,128)(2,1)S(1)}, bf16[32,1024]{1,0:T(8,128)(2,1)S(1)}, u32[]{:S(2)}, u32[]{:S(2)}) collective-permute-start(bf16[32,1024]{1,0:T(8,128)(2,1)S(1)} %get-tuple-element.64), channel_id=1, source_target_pairs={{0,17},{1,16},{2,19},{3,18},{4,21},{5,20},{6,23},{7,22},{8,14},{9,... | collective-permute-start | bytes 196616 | tf_op jit(solution)/shard_map/ppermute | solution.py:32
  29.1 4.3 %collective-permute-start.10 = (bf16[32,1024]{1,0:T(8,128)(2,1)S(1)}, bf16[32,1024]{1,0:T(8,128)(2,1)S(1)}, u32[]{:S(2)}, u32[]{:S(2)}) collective-permute-start(bf16[32,1024]{1,0:T(8,128)(2,1)S(1)} %get-tuple-element.65), channel_id=1, source_target_pairs={{0,16},{1,17},{2,18},{3,19},{4,20},{5,21},{6,22},{7,23},{8,10},{9,... | collective-permute-start | bytes 196616 | tf_op jit(solution)/shard_map/ppermute | solution.py:32
  33.4 7.3 %collective-permute-start.12 = (bf16[8,1024]{1,0:T(8,128)(2,1)S(1)}, bf16[8,1024]{1,0:T(8,128)(2,1)S(1)}, u32[]{:S(2)}, u32[]{:S(2)}) collective-permute-start(bf16[8,1024]{1,0:T(8,128)(2,1)S(1)} %get-tuple-element.66), channel_id=1, source_target_pairs={{0,4},{1,5},{2,6},{3,7},{4,0},{5,1},{6,2},{7,3},{8,9},{9,8},{10,11... | collective-permute-start | bytes 49160 | tf_op jit(solution)/shard_map/ppermute | solution.py:32
  35.2 5.5 %collective-permute-start.14 = (bf16[8,1024]{1,0:T(8,128)(2,1)S(1)}, bf16[8,1024]{1,0:T(8,128)(2,1)S(1)}, u32[]{:S(2)}, u32[]{:S(2)}) collective-permute-start(bf16[8,1024]{1,0:T(8,128)(2,1)S(1)} %get-tuple-element.67), channel_id=1, source_target_pairs={{0,6},{1,7},{2,4},{3,5},{4,2},{5,3},{6,0},{7,1},{8,25},{9,24},{10,... | collective-permute-start | bytes 49160 | tf_op jit(solution)/shard_map/ppermute | solution.py:32
  36.5 4.2 %collective-permute-start.13 = (bf16[8,1024]{1,0:T(8,128)(2,1)S(1)}, bf16[8,1024]{1,0:T(8,128)(2,1)S(1)}, u32[]{:S(2)}, u32[]{:S(2)}) collective-permute-start(bf16[8,1024]{1,0:T(8,128)(2,1)S(1)} %get-tuple-element.68), channel_id=1, source_target_pairs={{0,2},{1,3},{2,0},{3,1},{4,6},{5,7},{6,4},{7,5},{8,24},{9,25},{10,... | collective-permute-start | bytes 49160 | tf_op jit(solution)/shard_map/ppermute | solution.py:32

commit v6 on v5

--- a/solution.py
+++ b/solution.py
@@ -117,15 +117,16 @@
     return (gate * dyg[:, :width].astype(F32)).astype(BF16)
 
 
-def hidden(x, dyg, up_turned, down_turned, relu, row_grad, pre_grad):
-    row_grad[...] = gated(dyg[...], row_grad.shape[1], relu.shape[1])
-    relu[...] = jnp.maximum(dot(x[...], up_turned[...], 1, 0), 0.0)
+def hidden(rows, up_turned, down_turned, relu, row_grad, pre_grad):
+    width = row_grad.shape[1]
+    row_grad[...] = gated(rows[:, width:], width, relu.shape[1])
+    relu[...] = jnp.maximum(dot(rows[:, :width], up_turned[...], 1, 0), 0.0)
     hid_grad = dot(row_grad[...], down_turned[...], 1, 0)
     pre_grad[...] = (hid_grad * 2.0 * relu[...]).astype(BF16)
 
 
-def hidden_part(x, dyg, up_turned, down_turned, w_up, relu, row_grad, pre_grad, part):
-    hidden(x, dyg, up_turned, down_turned, relu, row_grad, pre_grad)
+def hidden_part(rows, up_turned, down_turned, w_up, relu, row_grad, pre_grad, part):
+    hidden(rows, up_turned, down_turned, relu, row_grad, pre_grad)
     part[...] = dot(pre_grad[...], w_up[...], 1, 0).astype(BF16)
 
 
@@ -141,17 +142,19 @@
     return row_grad, act, pre_grad, dot(pre_grad, w_up, 1, 0).astype(BF16)
 
 
-def outer(a, b, name):
-    n, width = a[0].shape[1], b[0].shape[1]
+def outer(lefts, rights, width, name):
+    n = lefts[0].shape[1]
     step = 384
     blocks = n // step
 
-    def kernel(a_0, a_1, b_0, b_1, out, buffer, sems):
+    def kernel(*refs):
+        left_refs, right_refs = refs[: len(lefts)], refs[len(lefts) : len(lefts) + len(rights)]
+        out, buffer, sems = refs[-3:]
         copies = []
-        right = jnp.concatenate([b_0[...], b_1[...]], axis=0)
+        right = jnp.concatenate([ref[:, :width] for ref in right_refs], axis=0)
         for k in range(blocks):
             rows = pl.ds(k * step, step)
-            left = jnp.concatenate([a_0[:, k * step : (k + 1) * step], a_1[:, k * step : (k + 1) * step]], axis=0)
+            left = jnp.concatenate([ref[:, k * step : (k + 1) * step] for ref in left_refs], axis=0)
             left = (left * left).astype(BF16) if left.dtype == F32 else left
             buffer[rows] = dot(left, right, 0, 0).astype(BF16)
             copies.append(pltpu.make_async_copy(buffer.at[rows], out.at[0, rows], sems.at[k]))
@@ -159,9 +162,9 @@
         for copy in copies:
             copy.wait()
 
-    return call(kernel, S((1, n, width), BF16), [VMEM] * 4, name,
+    return call(kernel, S((1, n, width), BF16), [VMEM] * (len(lefts) + len(rights)), name,
         (pltpu.VMEM((n, width), BF16), pltpu.SemaphoreType.DMA((blocks,))), ANY,
-        flops=4 * a[0].shape[0] * n * width, moved=2 * n * width)(*a, *b)
+        flops=2 * sum(left.shape[0] for left in lefts) * n * width, moved=2 * n * width)(*lefts, *rights)
 
 
 def local(latent, out_grad, gates, expert_ids, up_weight, down_weight):
@@ -174,42 +177,43 @@
     plan = stages(members, devices)
     tokens = latent.shape[0] * devices
     flops = 2 * tokens * rows * width
-    small = tokens <= 256 and rows % 384 == 0
+    small = tokens == 256 and rows % 384 == 0 and len(plan) == 2
     w_up, w_down = up_weight[0], down_weight[0]
 
+    half = tokens // 2
     rows_all = pack(latent, out_grad, gates, expert_ids)
-    for k, masks in enumerate(plan):
-        if small and k == 0:
-            rows_all, w_up = tie((rows_all, w_up))
-        if small and k == 1:
-            rows_all, w_down = tie((rows_all, w_down))
-        got = [swap(rows_all, mask, members, devices) for mask in masks]
-        t = TIED[k % 4]
-        if small and k == 0:
-            w_up, up_turned = load(w_up, "load_up", True)
-            got[t], w_up, up_turned = tie((got[t], w_up, up_turned))
-        if small and k == 1:
-            down_turned = load(w_down, "load_down", False)
-            got[t], down_turned = tie((got[t], down_turned))
-        rows_all = tie(jnp.concatenate([rows_all] + got, axis=0))
-    x, dyg = tie((rows_all[:, :width], rows_all[:, width:]))
-    got_x = swap(x, core, members, devices)
-    got_dyg = swap(dyg, core, members, devices)
-    half = tokens // 2
-    if small:
-        outs = (S((half, rows), F32), S((half, width), BF16), S((half, rows), BF16))
-        left = call(hidden, outs, [VMEM] * 4, "hidden", flops=flops)(x, dyg, up_turned, down_turned)
-        got_x, left = tie((got_x, left))
-        right = call(hidden_part, (*outs, S((half, width), BF16)), [VMEM] * 5, "hidden_part", flops=3 * flops // 2)(
-            got_x, got_dyg, up_turned, down_turned, w_up)
-        got = swap(right[3], core, members, devices)
-        ours = call(part_kernel, S((half, width), F32), [VMEM] * 2, "part", flops=flops // 2)(left[2], w_up)
-        x, relu, row_grad, pre_grad = (x, got_x), (left[0], right[0]), (left[1], right[1]), (left[2], right[2])
-    else:
-        x, dyg = jnp.concatenate([x, got_x]), jnp.concatenate([dyg, got_dyg])
-        row_grad, act, pre_grad, part = plain(x, dyg, w_up, w_down)
+    if not small:
+        for masks in plan:
+            got = [swap(rows_all, mask, members, devices) for mask in masks]
+            rows_all = jnp.concatenate([rows_all] + got, axis=0)
+        rows_all = jnp.concatenate([rows_all, swap(rows_all, core, members, devices)], axis=0)
+        x = rows_all[:, :width]
+        row_grad, act, pre_grad, part = plain(x, rows_all[:, width:], w_up, w_down)
         ours = part[:half].astype(F32)
         got = swap(part[half:], core, members, devices)
+    else:
+        outs = (S((half, rows), F32), S((half, width), BF16), S((half, rows), BF16))
+        rows_all, w_up = tie((rows_all, w_up))
+        got = [swap(rows_all, mask, members, devices) for mask in plan[0]]
+        w_up, up_turned = load(w_up, "load_up", True)
+        got[TIED[0]], w_up, up_turned = tie((got[TIED[0]], w_up, up_turned))
+        rows_all = tie(jnp.concatenate([rows_all] + got, axis=0))
+
+        rows_all, w_down = tie((rows_all, w_down))
+        got = [swap(rows_all, mask, members, devices) for mask in plan[1]]
+        down_turned = load(w_down, "load_down", False)
+        got[TIED[1]], down_turned = tie((got[TIED[1]], down_turned))
+        rows_all = tie(jnp.concatenate([rows_all] + got, axis=0))
+
+        theirs = swap(rows_all, core, members, devices)
+        first = call(hidden, outs, [VMEM] * 3, "hidden", flops=flops)(rows_all, up_turned, down_turned)
+        theirs, first = tie((theirs, first))
+        second = call(hidden_part, (*outs, S((half, width), BF16)), [VMEM] * 4, "hidden_part", flops=3 * flops // 2)(
+            theirs, up_turned, down_turned, w_up)
+        got = swap(second[3], core, members, devices)
+        ours = call(part_kernel, S((half, width), F32), [VMEM] * 2, "part", flops=flops // 2)(first[2], w_up)
+        x = (rows_all, theirs)
+        relu, row_grad, pre_grad = ((first[k], second[k]) for k in range(3))
 
     total = ours + got.astype(F32)
     for k, masks in enumerate(reversed(plan)):
@@ -218,10 +222,10 @@
         got = [swap(block.astype(BF16), mask, members, devices) for block, mask in zip(cut[1:], masks)]
         t = TIED[(2 + k) % 4]
         if small and k == 0:
-            up_grad = outer(pre_grad, x, "up")
+            up_grad = outer(pre_grad, x, width, "up")
             got[t], up_grad = tie((got[t], up_grad))
         if small and k == 1:
-            down_grad = outer(relu, row_grad, "down")
+            down_grad = outer(relu, row_grad, width, "down")
             got[t], down_grad = tie((got[t], down_grad))
         total = cut[0] + sum(block.astype(F32) for block in got)
     if not small:

time: 41.6 us -> 41.2 us (level)
    ppermute x15 -> x14, starting transfers between devices: 17.1 us -> 16.7 us  [swap(): lax.ppermute(value, AXES, [(i, i ^ (odd if i & core else even)) for i in...]
    ppermute x15 -> x14, waiting for transfers between devices: 4.9 us -> 4.97 us  [swap(): lax.ppermute(value, AXES, [(i, i ^ (odd if i & core else even)) for i in...]
  transfers between devices with their start and end apart: 15 -> 14, of which waited for: 6 -> 7; matrix products, arithmetic and copies ran while one was open for 0% -> 0% of each run, Pallas kernels for 35% -> 35%
where the time goes in v6:
time: 41.2 us; the launch traced here: 41 us
  Pallas kernels  17.7 us (43%)
  starting transfers between devices  16.7 us (41%)
  waiting for transfers between devices  4.97 us (12%)
  other arithmetic  0.78 us (2%)
  between operations  0.76 us (2%)
    ppermute x14, starting transfers between devices, swap(): lax.ppermute(value, AXES, [(i, i ^ (odd if i & core else even)) for i in...  16.7 us
    pallas_call x2, Pallas kernels, load(): call(kernel, out, [HBM], name, scratch, moved=2 * weight.size)  6.02 us
    pallas_call x2, Pallas kernels, outer(): call(kernel, S((1, n, width), BF16), [VMEM] * (len(lefts) + len(rights)),...  5.77 us
    ppermute x14, waiting for transfers between devices, swap(): lax.ppermute(value, AXES, [(i, i ^ (odd if i & core else even)) for i in...  4.97 us
    pallas_call x1, Pallas kernels, local(): call(hidden_part, (*outs, S((half, width), BF16)), [VMEM] * 4, 'hidden_pa...  2.44 us
    pallas_call x1, Pallas kernels, local(): call(hidden, outs, [VMEM] * 3, 'hidden', flops=flops)  1.69 us
    pallas_call x1, Pallas kernels, local(): call(part_kernel, S((half, width), F32), [VMEM] * 2, 'part', flops=flops...  0.92 us
    pallas_call x1, Pallas kernels, pack(): call(pack_kernel, S((rows, 2 * width + LANES), BF16), [HBM] * 4, 'pack',...  0.88 us
  transfers between devices with their start and end apart: 14, of which 7 were waited for; matrix products, arithmetic and copies ran while one was open for 0% of the time, Pallas kernels for 35%

profile of v6, /device:TPU:0, one launch (start us, length us, event | category | flops | bytes accessed | tf_op | source)
XLA Modules:
  0.0 41.0 jit_solution(2860769770931245853)
XLA Ops:
  0.6 0.9 %pack.1 = bf16[8,2176]{1,0:T(8,128)(2,1)S(1)} custom-call(bf16[8,1024]{1,0:T(8,128)(2,1)} %latent.1, bf16[8,1024]{1,0:T(8,128)(2,1)} %out_grad.1, bf16[8,22]{1,0:T(8,128)(2,1)} %gates.1, s32[8,22]{1,0:T(8,128)} %ids.1), custom_call_target="tpu_custom_call" | custom-call | tf_op jit(solution)/shard_map/pack/pallas_call | solution.py:83
  1.5 4.1 %collective-permute-start = (bf16[8,2176]{1,0:T(8,128)(2,1)S(1)}, bf16[8,2176]{1,0:T(8,128)(2,1)S(1)}, u32[]{:S(2)}, u32[]{:S(2)}) collective-permute-start(bf16[8,2176]{1,0:T(8,128)(2,1)S(1)} %pack.1), channel_id=1, source_target_pairs={{0,4},{1,5},{2,6},{3,7},{4,0},{5,1},{6,2},{7,3},{8,9},{9,8},{10,11... | collective-permute-start | bytes 104456 | tf_op jit(solution)/shard_map/ppermute | solution.py:32
  5.6 1.3 %collective-permute-start.2 = (bf16[8,2176]{1,0:T(8,128)(2,1)S(1)}, bf16[8,2176]{1,0:T(8,128)(2,1)S(1)}, u32[]{:S(2)}, u32[]{:S(2)}) collective-permute-start(bf16[8,2176]{1,0:T(8,128)(2,1)S(1)} %pack.1), channel_id=1, source_target_pairs={{0,6},{1,7},{2,4},{3,5},{4,2},{5,3},{6,0},{7,1},{8,25},{9,24},{10,... | collective-permute-start | bytes 104456 | tf_op jit(solution)/shard_map/ppermute | solution.py:32
  7.0 0.2 collective-permute-start.1
  7.2 3.0 %load_up.1 = (bf16[2688,1024]{1,0:T(8,128)(2,1)S(1)}, bf16[1024,2688]{1,0:T(8,128)(2,1)S(1)}) custom-call(bf16[2688,1024]{1,0:T(8,128)(2,1)} %bitcast.3), custom_call_target="tpu_custom_call" | custom-call | bytes 5505024 | tf_op jit(solution)/shard_map/load_up/pallas_call | solution.py:107
  10.2 0.0 collective-permute-done
  10.2 1.1 %collective-permute-done.2 = bf16[8,2176]{1,0:T(8,128)(2,1)S(1)} collective-permute-done((bf16[8,2176]{1,0:T(8,128)(2,1)S(1)}, bf16[8,2176]{1,0:T(8,128)(2,1)S(1)}, u32[]{:S(2)}, u32[]{:S(2)}) %collective-permute-start.2) | collective-permute-done | bytes 34848 | tf_op jit(solution)/shard_map/ppermute | solution.py:32
  11.4 0.0 collective-permute-done.1
  11.4 2.5 %collective-permute-start.5 = (bf16[32,2176]{1,0:T(8,128)(2,1)S(1)}, bf16[32,2176]{1,0:T(8,128)(2,1)S(1)}, u32[]{:S(2)}, u32[]{:S(2)}) collective-permute-start(bf16[32,2176]{1,0:T(8,128)(2,1)S(1)} %pad_maximum_fusion.1), channel_id=1, source_target_pairs={{0,17},{1,16},{2,19},{3,18},{4,21},{5,20},{6,23},{7,22},{8,14},{9,... | collective-permute-start | bytes 417800 | tf_op jit(solution)/shard_map/ppermute | solution.py:32
  13.9 0.5 %collective-permute-start.4 = (bf16[32,2176]{1,0:T(8,128)(2,1)S(1)}, bf16[32,2176]{1,0:T(8,128)(2,1)S(1)}, u32[]{:S(2)}, u32[]{:S(2)}) collective-permute-start(bf16[32,2176]{1,0:T(8,128)(2,1)S(1)} %pad_maximum_fusion.1), channel_id=1, source_target_pairs={{0,16},{1,17},{2,18},{3,19},{4,20},{5,21},{6,22},{7,23},{8,10},{9,... | collective-permute-start | bytes 417800 | tf_op jit(solution)/shard_map/ppermute | solution.py:32
  14.4 0.5 %collective-permute-start.3 = (bf16[32,2176]{1,0:T(8,128)(2,1)S(1)}, bf16[32,2176]{1,0:T(8,128)(2,1)S(1)}, u32[]{:S(2)}, u32[]{:S(2)}) collective-permute-start(bf16[32,2176]{1,0:T(8,128)(2,1)S(1)} %pad_maximum_fusion.1), channel_id=1, source_target_pairs={{0,1},{1,0},{2,3},{3,2},{4,5},{5,4},{6,7},{7,6},{8,12},{9,13},{10,... | collective-permute-start | bytes 417800 | tf_op jit(solution)/shard_map/ppermute | solution.py:32
  14.9 3.0 %load_down.1.down_turned = bf16[1024,2688]{1,0:T(8,128)(2,1)S(1)} custom-call(bf16[2688,1024]{1,0:T(8,128)(2,1)} %bitcast.2), custom_call_target="tpu_custom_call" | custom-call | bytes 5505024 | tf_op jit(solution)/shard_map/load_down/pallas_call | solution.py:107
  17.9 0.0 collective-permute-done.5
  18.0 1.0 %collective-permute-done.4 = bf16[32,2176]{1,0:T(8,128)(2,1)S(1)} collective-permute-done((bf16[32,2176]{1,0:T(8,128)(2,1)S(1)}, bf16[32,2176]{1,0:T(8,128)(2,1)S(1)}, u32[]{:S(2)}, u32[]{:S(2)}) %collective-permute-start.4) | collective-permute-done | bytes 139296 | tf_op jit(solution)/shard_map/ppermute | solution.py:32
  18.9 0.5 %collective-permute-done.3 = bf16[32,2176]{1,0:T(8,128)(2,1)S(1)} collective-permute-done((bf16[32,2176]{1,0:T(8,128)(2,1)S(1)}, bf16[32,2176]{1,0:T(8,128)(2,1)S(1)}, u32[]{:S(2)}, u32[]{:S(2)}) %collective-permute-start.3) | collective-permute-done | bytes 139296 | tf_op jit(solution)/shard_map/ppermute | solution.py:32
  19.5 0.1 collective-permute-start.6
  19.6 1.7 %hidden.1 = (f32[128,2688]{1,0:T(8,128)S(1)}, bf16[128,1024]{1,0:T(8,128)(2,1)S(1)}, bf16[128,2688]{1,0:T(8,128)(2,1)S(1)}) custom-call(bf16[128,2176]{1,0:T(8,128)(2,1)S(1)} %pad_maximum_fusion.rows.refs_2_, bf16[1024,2688]{1,0:T(8,128)(2,1)S(1)} %get-tuple-element.37.up_turned, bf16[1024,2688]{1,0:T(8,128)(2,1)S(1)} %load_down.1.down_turned), custom_call_target="tpu_custom_call" | custom-call | flops 1409286144 | tf_op jit(solution)/shard_map/hidden/pallas_call | solution.py:209
  21.3 0.3 collective-permute-done.6.rows.refs_3_
  21.5 2.4 %hidden_part.1 = (f32[128,2688]{1,0:T(8,128)S(1)}, bf16[128,1024]{1,0:T(8,128)(2,1)S(1)}, bf16[128,2688]{1,0:T(8,128)(2,1)S(1)}, bf16[128,1024]{1,0:T(8,128)(2,1)S(1)}) custom-call(bf16[128,2176]{1,0:T(8,128)(2,1)S(1)} %collective-permute-done.6.rows.refs_3_, bf16[1024,2688]{1,0:T(8,128)(2,1)S(1)} %get-tuple-element.37.up_turned, ...), custom_call_target="tpu_custom_call" | custom-call | flops 2113929216 | tf_op jit(solution)/shard_map/hidden_part/pallas_call | solution.py:211
  24.0 0.3 collective-permute-start.7
  24.3 0.9 %part.1 = f32[128,1024]{1,0:T(8,128)S(1)} custom-call(bf16[128,2688]{1,0:T(8,128)(2,1)S(1)} %get-tuple-element.42.pre_grad.refs_0_, bf16[2688,1024]{1,0:T(8,128)(2,1)S(1)} %get-tuple-element.43.w_up), custom_call_target="tpu_custom_call" | custom-call | flops 704643072 | tf_op jit(solution)/shard_map/part/pallas_call | solution.py:214
  25.2 0.4 collective-permute-done.7
  25.6 0.1 fusion.1
  25.7 1.1 %collective-permute-start.8 = (bf16[32,1024]{1,0:T(8,128)(2,1)S(1)}, bf16[32,1024]{1,0:T(8,128)(2,1)S(1)}, u32[]{:S(2)}, u32[]{:S(2)}) collective-permute-start(bf16[32,1024]{1,0:T(8,128)(2,1)S(1)} %get-tuple-element.59), channel_id=1, source_target_pairs={{0,1},{1,0},{2,3},{3,2},{4,5},{5,4},{6,7},{7,6},{8,12},{9,13},{10,... | collective-permute-start | bytes 196616 | tf_op jit(solution)/shard_map/ppermute | solution.py:32
  26.8 2.0 %collective-permute-start.10 = (bf16[32,1024]{1,0:T(8,128)(2,1)S(1)}, bf16[32,1024]{1,0:T(8,128)(2,1)S(1)}, u32[]{:S(2)}, u32[]{:S(2)}) collective-permute-start(bf16[32,1024]{1,0:T(8,128)(2,1)S(1)} %get-tuple-element.60), channel_id=1, source_target_pairs={{0,17},{1,16},{2,19},{3,18},{4,21},{5,20},{6,23},{7,22},{8,14},{9,... | collective-permute-start | bytes 196616 | tf_op jit(solution)/shard_map/ppermute | solution.py:32
  28.7 0.5 %collective-permute-start.9 = (bf16[32,1024]{1,0:T(8,128)(2,1)S(1)}, bf16[32,1024]{1,0:T(8,128)(2,1)S(1)}, u32[]{:S(2)}, u32[]{:S(2)}) collective-permute-start(bf16[32,1024]{1,0:T(8,128)(2,1)S(1)} %get-tuple-element.61), channel_id=1, source_target_pairs={{0,16},{1,17},{2,18},{3,19},{4,20},{5,21},{6,22},{7,23},{8,10},{9,... | collective-permute-start | bytes 196616 | tf_op jit(solution)/shard_map/ppermute | solution.py:32
  29.2 2.9 %up.1 = bf16[1,2688,1024]{2,1,0:T(8,128)(2,1)} custom-call(bf16[128,2688]{1,0:T(8,128)(2,1)S(1)} %get-tuple-element.42.pre_grad.refs_0_, bf16[128,2688]{1,0:T(8,128)(2,1)S(1)} %get-tuple-element.46.refs_1_, bf16[128,2176]{1,0:T(8,128)(2,1)S(1)} %pad_maximum_fusion.rows.refs_2_, bf16[128,2176]{1,0:T(8,128)(2,1)S(1)} %collective-permute-done.6.rows.refs_3_), custom_call_target="tpu_custom_call" | custom-call | flops 1409286144 | bytes 5505024 | tf_op jit(solution)/shard_map/up/pallas_call | solution.py:165
  32.1 0.9 %collective-permute-done.9 = bf16[32,1024]{1,0:T(8,128)(2,1)S(1)} collective-permute-done((bf16[32,1024]{1,0:T(8,128)(2,1)S(1)}, bf16[32,1024]{1,0:T(8,128)(2,1)S(1)}, u32[]{:S(2)}, u32[]{:S(2)}) %collective-permute-start.9) | collective-permute-done | bytes 65568 | tf_op jit(solution)/shard_map/ppermute | solution.py:32
  33.0 0.0 collective-permute-done.8
  33.0 0.0 collective-permute-done.10
  33.0 1.8 %collective-permute-start.11 = (bf16[8,1024]{1,0:T(8,128)(2,1)S(1)}, bf16[8,1024]{1,0:T(8,128)(2,1)S(1)}, u32[]{:S(2)}, u32[]{:S(2)}) collective-permute-start(bf16[8,1024]{1,0:T(8,128)(2,1)S(1)} %get-tuple-element.62), channel_id=1, source_target_pairs={{0,4},{1,5},{2,6},{3,7},{4,0},{5,1},{6,2},{7,3},{8,9},{9,8},{10,11... | collective-permute-start | bytes 49160 | tf_op jit(solution)/shard_map/ppermute | solution.py:32
  34.8 1.4 %collective-permute-start.13 = (bf16[8,1024]{1,0:T(8,128)(2,1)S(1)}, bf16[8,1024]{1,0:T(8,128)(2,1)S(1)}, u32[]{:S(2)}, u32[]{:S(2)}) collective-permute-start(bf16[8,1024]{1,0:T(8,128)(2,1)S(1)} %get-tuple-element.63), channel_id=1, source_target_pairs={{0,6},{1,7},{2,4},{3,5},{4,2},{5,3},{6,0},{7,1},{8,25},{9,24},{10,... | collective-permute-start | bytes 49160 | tf_op jit(solution)/shard_map/ppermute | solution.py:32
  36.2 0.4 %collective-permute-start.12 = (bf16[8,1024]{1,0:T(8,128)(2,1)S(1)}, bf16[8,1024]{1,0:T(8,128)(2,1)S(1)}, u32[]{:S(2)}, u32[]{:S(2)}) collective-permute-start(bf16[8,1024]{1,0:T(8,128)(2,1)S(1)} %get-tuple-element.64), channel_id=1, source_target_pairs={{0,2},{1,3},{2,0},{3,1},{4,6},{5,7},{6,4},{7,5},{8,24},{9,25},{10,... | collective-permute-start | bytes 49160 | tf_op jit(solution)/shard_map/ppermute | solution.py:32
  36.6 2.9 %down.1 = bf16[1,2688,1024]{2,1,0:T(8,128)(2,1)} custom-call(f32[128,2688]{1,0:T(8,128)S(1)} %get-tuple-element.48.refs_0_, f32[128,2688]{1,0:T(8,128)S(1)} %get-tuple-element.49.refs_1_, bf16[128,1024]{1,0:T(8,128)(2,1)S(1)} %get-tuple-element.50.refs_2_, bf16[128,1024]{1,0:T(8,128)(2,1)S(1)} %get-tuple-element.51.refs_3_), custom_call_target="tpu_custom_call" | custom-call | flops 1409286144 | bytes 5505024 | tf_op jit(solution)/shard_map/down/pallas_call | solution.py:165
  39.5 0.9 %collective-permute-done.13 = bf16[8,1024]{1,0:T(8,128)(2,1)S(1)} collective-permute-done((bf16[8,1024]{1,0:T(8,128)(2,1)S(1)}, bf16[8,1024]{1,0:T(8,128)(2,1)S(1)}, u32[]{:S(2)}, u32[]{:S(2)}) %collective-permute-start.13) | collective-permute-done | bytes 16416 | tf_op jit(solution)/shard_map/ppermute | solution.py:32
  40.3 0.0 collective-permute-done.11
  40.4 0.0 collective-permute-done.12
  40.4 0.6 %slice_add_fusion.1 = f32[8,1024]{1,0:T(8,128)} fusion(f32[32,1024]{1,0:T(8,128)S(1)} %get-tuple-element.56, bf16[8,1024]{1,0:T(8,128)(2,1)S(1)} %collective-permute-done.13, bf16[8,1024]{1,0:T(8,128)(2,1)S(1)} %collective-permute-done.12, bf16[8,1024]{1,0:T(8,128)(2,1)S(1)} %collective-permute-done.11), kind=kLoop, calls=%fused_computation.4 | loop fusion | flops 49152 | bytes 114688 | tf_op jit(solution)/shard_map/add | solution.py:230
  (5 shorter events, 0.1 us)
Async XLA Ops:
  1.5 8.7 %collective-permute-start = (bf16[8,2176]{1,0:T(8,128)(2,1)S(1)}, bf16[8,2176]{1,0:T(8,128)(2,1)S(1)}, u32[]{:S(2)}, u32[]{:S(2)}) collective-permute-start(bf16[8,2176]{1,0:T(8,128)(2,1)S(1)} %pack.1), channel_id=1, source_target_pairs={{0,4},{1,5},{2,6},{3,7},{4,0},{5,1},{6,2},{7,3},{8,9},{9,8},{10,11... | collective-permute-start | bytes 104456 | tf_op jit(solution)/shard_map/ppermute | solution.py:32
  5.6 5.7 %collective-permute-start.2 = (bf16[8,2176]{1,0:T(8,128)(2,1)S(1)}, bf16[8,2176]{1,0:T(8,128)(2,1)S(1)}, u32[]{:S(2)}, u32[]{:S(2)}) collective-permute-start(bf16[8,2176]{1,0:T(8,128)(2,1)S(1)} %pack.1), channel_id=1, source_target_pairs={{0,6},{1,7},{2,4},{3,5},{4,2},{5,3},{6,0},{7,1},{8,25},{9,24},{10,... | collective-permute-start | bytes 104456 | tf_op jit(solution)/shard_map/ppermute | solution.py:32
  7.0 4.4 %collective-permute-start.1 = (bf16[8,2176]{1,0:T(8,128)(2,1)S(1)}, bf16[8,2176]{1,0:T(8,128)(2,1)S(1)}, u32[]{:S(2)}, u32[]{:S(2)}) collective-permute-start(bf16[8,2176]{1,0:T(8,128)(2,1)S(1)} %pack.1), channel_id=1, source_target_pairs={{0,2},{1,3},{2,0},{3,1},{4,6},{5,7},{6,4},{7,5},{8,24},{9,25},{10,... | collective-permute-start | bytes 104456 | tf_op jit(solution)/shard_map/ppermute | solution.py:32
  11.4 6.6 %collective-permute-start.5 = (bf16[32,2176]{1,0:T(8,128)(2,1)S(1)}, bf16[32,2176]{1,0:T(8,128)(2,1)S(1)}, u32[]{:S(2)}, u32[]{:S(2)}) collective-permute-start(bf16[32,2176]{1,0:T(8,128)(2,1)S(1)} %pad_maximum_fusion.1), channel_id=1, source_target_pairs={{0,17},{1,16},{2,19},{3,18},{4,21},{5,20},{6,23},{7,22},{8,14},{9,... | collective-permute-start | bytes 417800 | tf_op jit(solution)/shard_map/ppermute | solution.py:32
  13.9 5.1 %collective-permute-start.4 = (bf16[32,2176]{1,0:T(8,128)(2,1)S(1)}, bf16[32,2176]{1,0:T(8,128)(2,1)S(1)}, u32[]{:S(2)}, u32[]{:S(2)}) collective-permute-start(bf16[32,2176]{1,0:T(8,128)(2,1)S(1)} %pad_maximum_fusion.1), channel_id=1, source_target_pairs={{0,16},{1,17},{2,18},{3,19},{4,20},{5,21},{6,22},{7,23},{8,10},{9,... | collective-permute-start | bytes 417800 | tf_op jit(solution)/shard_map/ppermute | solution.py:32
  14.4 5.1 %collective-permute-start.3 = (bf16[32,2176]{1,0:T(8,128)(2,1)S(1)}, bf16[32,2176]{1,0:T(8,128)(2,1)S(1)}, u32[]{:S(2)}, u32[]{:S(2)}) collective-permute-start(bf16[32,2176]{1,0:T(8,128)(2,1)S(1)} %pad_maximum_fusion.1), channel_id=1, source_target_pairs={{0,1},{1,0},{2,3},{3,2},{4,5},{5,4},{6,7},{7,6},{8,12},{9,13},{10,... | collective-permute-start | bytes 417800 | tf_op jit(solution)/shard_map/ppermute | solution.py:32
  19.5 2.0 %collective-permute-start.6 = (bf16[128,2176]{1,0:T(8,128)(2,1)S(1)}, bf16[128,2176]{1,0:T(8,128)(2,1)S(1)}, u32[]{:S(2)}, u32[]{:S(2)}) collective-permute-start(bf16[128,2176]{1,0:T(8,128)(2,1)S(1)} %pad_maximum_fusion.rows.refs_2_), channel_id=1, source_target_pairs={{0,8},{1,9},{2,10},{3,11},{4,12},{5,13},{6,14},{7,15},{8,0},{9,1},... | collective-permute-start | bytes 1671176 | tf_op jit(solution)/shard_map/ppermute | solution.py:32
  24.0 1.6 %collective-permute-start.7 = (bf16[128,1024]{1,0:T(8,128)(2,1)S(1)}, bf16[128,1024]{1,0:T(8,128)(2,1)S(1)}, u32[]{:S(2)}, u32[]{:S(2)}) collective-permute-start(bf16[128,1024]{1,0:T(8,128)(2,1)S(1)} %get-tuple-element.45), channel_id=1, source_target_pairs={{0,8},{1,9},{2,10},{3,11},{4,12},{5,13},{6,14},{7,15},{8,0},{9,1},... | collective-permute-start | bytes 786440 | tf_op jit(solution)/shard_map/ppermute | solution.py:32
  25.7 7.3 %collective-permute-start.8 = (bf16[32,1024]{1,0:T(8,128)(2,1)S(1)}, bf16[32,1024]{1,0:T(8,128)(2,1)S(1)}, u32[]{:S(2)}, u32[]{:S(2)}) collective-permute-start(bf16[32,1024]{1,0:T(8,128)(2,1)S(1)} %get-tuple-element.59), channel_id=1, source_target_pairs={{0,1},{1,0},{2,3},{3,2},{4,5},{5,4},{6,7},{7,6},{8,12},{9,13},{10,... | collective-permute-start | bytes 196616 | tf_op jit(solution)/shard_map/ppermute | solution.py:32
  26.8 6.2 %collective-permute-start.10 = (bf16[32,1024]{1,0:T(8,128)(2,1)S(1)}, bf16[32,1024]{1,0:T(8,128)(2,1)S(1)}, u32[]{:S(2)}, u32[]{:S(2)}) collective-permute-start(bf16[32,1024]{1,0:T(8,128)(2,1)S(1)} %get-tuple-element.60), channel_id=1, source_target_pairs={{0,17},{1,16},{2,19},{3,18},{4,21},{5,20},{6,23},{7,22},{8,14},{9,... | collective-permute-start | bytes 196616 | tf_op jit(solution)/shard_map/ppermute | solution.py:32
  28.7 4.3 %collective-permute-start.9 = (bf16[32,1024]{1,0:T(8,128)(2,1)S(1)}, bf16[32,1024]{1,0:T(8,128)(2,1)S(1)}, u32[]{:S(2)}, u32[]{:S(2)}) collective-permute-start(bf16[32,1024]{1,0:T(8,128)(2,1)S(1)} %get-tuple-element.61), channel_id=1, source_target_pairs={{0,16},{1,17},{2,18},{3,19},{4,20},{5,21},{6,22},{7,23},{8,10},{9,... | collective-permute-start | bytes 196616 | tf_op jit(solution)/shard_map/ppermute | solution.py:32
  33.0 7.3 %collective-permute-start.11 = (bf16[8,1024]{1,0:T(8,128)(2,1)S(1)}, bf16[8,1024]{1,0:T(8,128)(2,1)S(1)}, u32[]{:S(2)}, u32[]{:S(2)}) collective-permute-start(bf16[8,1024]{1,0:T(8,128)(2,1)S(1)} %get-tuple-element.62), channel_id=1, source_target_pairs={{0,4},{1,5},{2,6},{3,7},{4,0},{5,1},{6,2},{7,3},{8,9},{9,8},{10,11... | collective-permute-start | bytes 49160 | tf_op jit(solution)/shard_map/ppermute | solution.py:32
  34.8 5.5 %collective-permute-start.13 = (bf16[8,1024]{1,0:T(8,128)(2,1)S(1)}, bf16[8,1024]{1,0:T(8,128)(2,1)S(1)}, u32[]{:S(2)}, u32[]{:S(2)}) collective-permute-start(bf16[8,1024]{1,0:T(8,128)(2,1)S(1)} %get-tuple-element.63), channel_id=1, source_target_pairs={{0,6},{1,7},{2,4},{3,5},{4,2},{5,3},{6,0},{7,1},{8,25},{9,24},{10,... | collective-permute-start | bytes 49160 | tf_op jit(solution)/shard_map/ppermute | solution.py:32
  36.2 4.2 %collective-permute-start.12 = (bf16[8,1024]{1,0:T(8,128)(2,1)S(1)}, bf16[8,1024]{1,0:T(8,128)(2,1)S(1)}, u32[]{:S(2)}, u32[]{:S(2)}) collective-permute-start(bf16[8,1024]{1,0:T(8,128)(2,1)S(1)} %get-tuple-element.64), channel_id=1, source_target_pairs={{0,2},{1,3},{2,0},{3,1},{4,6},{5,7},{6,4},{7,5},{8,24},{9,25},{10,... | collective-permute-start | bytes 49160 | tf_op jit(solution)/shard_map/ppermute | solution.py:32

commit v7 on v6

--- a/solution.py
+++ b/solution.py
@@ -49,7 +49,7 @@
     )
 
 
-def pack_kernel(latent, out_grad, gates, ids, packed, latent_in, out_grad_in, gates_in, ids_in, sems):
+def pack_kernel(latent, out_grad, gates, ids, packed, latent_in, out_grad_in, gates_in, ids_in, lists, sems):
     copies = [
         pltpu.make_async_copy(source, target, sems.at[k])
         for k, (source, target) in enumerate(
@@ -61,13 +61,11 @@
     copies[0].wait()
     copies[1].wait()
     rows, width = latent.shape
-    lane = lax.broadcasted_iota(jnp.int32, (rows, LANES), 1)
-    weight = gates_in[...].astype(F32)
-    chosen = ids_in[...]
-    dense = jnp.zeros(lane.shape, F32)
-    for k in range(gates.shape[1]):
-        dense += jnp.where(chosen[:, k : k + 1] == lane, weight[:, k : k + 1], 0.0)
-    packed[:, 2 * width :] = dense.astype(BF16)
+    top = gates.shape[1]
+    lists[...] = jnp.zeros_like(lists)
+    lists[:, :top] = gates_in[...].astype(F32)
+    lists[:, LANES // 2 : LANES // 2 + top] = (ids_in[...] + 1).astype(F32)
+    packed[:, 2 * width :] = lists[...].astype(BF16)
     copies[2].wait()
     packed[:, :width] = latent_in[...]
     copies[3].wait()
@@ -82,7 +80,7 @@
     rows, width = latent.shape
     return call(pack_kernel, S((rows, 2 * width + LANES), BF16), [HBM] * 4, "pack",
         (pltpu.VMEM(latent.shape, BF16), pltpu.VMEM(out_grad.shape, BF16), pltpu.VMEM(gates.shape, BF16), pltpu.VMEM(ids.shape, jnp.int32),
-         pltpu.SemaphoreType.DMA((4,))), limit=4)(*in_hbm(latent, out_grad, gates, ids))
+         pltpu.VMEM((rows, LANES), F32), pltpu.SemaphoreType.DMA((4,))), limit=4)(*in_hbm(latent, out_grad, gates, ids))
 
 
 def load(weight, name, keep):
@@ -111,9 +109,9 @@
     groups = lax.axis_size("group")
     local_experts = groups * rows // HID
     mine = lax.axis_index("member") * local_experts + lax.axis_index("group") // (groups // local_experts)
-    gates = dyg[:, width:].astype(F32)
-    lane = lax.broadcasted_iota(jnp.int32, gates.shape, 1)
-    gate = jnp.sum(jnp.where(lane == mine, gates, 0.0), axis=1, keepdims=True)
+    lists = dyg[:, width:].astype(F32)
+    named = lists[:, LANES // 2 :] == (mine + 1).astype(F32)
+    gate = jnp.sum(jnp.where(named, lists[:, : LANES // 2], 0.0), axis=1, keepdims=True)
     return (gate * dyg[:, :width].astype(F32)).astype(BF16)
 
 

time: 41.2 us -> 41.2 us (level)
  no operation moved by 1% of the time
where the time goes in v7:
time: 41.2 us; the launch traced here: 40.9 us
  Pallas kernels  17.6 us (43%)
  starting transfers between devices  16.7 us (41%)
  waiting for transfers between devices  4.98 us (12%)
  other arithmetic  0.78 us (2%)
  between operations  0.76 us (2%)
    ppermute x14, starting transfers between devices, swap(): lax.ppermute(value, AXES, [(i, i ^ (odd if i & core else even)) for i in...  16.7 us
    pallas_call x2, Pallas kernels, load(): call(kernel, out, [HBM], name, scratch, moved=2 * weight.size)  6.02 us
    pallas_call x2, Pallas kernels, outer(): call(kernel, S((1, n, width), BF16), [VMEM] * (len(lefts) + len(rights)),...  5.77 us
    ppermute x14, waiting for transfers between devices, swap(): lax.ppermute(value, AXES, [(i, i ^ (odd if i & core else even)) for i in...  4.98 us
    pallas_call x1, Pallas kernels, local(): call(hidden_part, (*outs, S((half, width), BF16)), [VMEM] * 4, 'hidden_pa...  2.44 us
    pallas_call x1, Pallas kernels, local(): call(hidden, outs, [VMEM] * 3, 'hidden', flops=flops)  1.69 us
    pallas_call x1, Pallas kernels, local(): call(part_kernel, S((half, width), F32), [VMEM] * 2, 'part', flops=flops...  0.92 us
  transfers between devices with their start and end apart: 14, of which 7 were waited for; matrix products, arithmetic and copies ran while one was open for 0% of the time, Pallas kernels for 35%

profile of v7, /device:TPU:0, one launch (start us, length us, event | category | flops | bytes accessed | tf_op | source)
XLA Modules:
  0.0 40.9 jit_solution(5446108404270492266)
XLA Ops:
  0.6 0.8 %pack.1 = bf16[8,2176]{1,0:T(8,128)(2,1)S(1)} custom-call(bf16[8,1024]{1,0:T(8,128)(2,1)} %latent.1, bf16[8,1024]{1,0:T(8,128)(2,1)} %out_grad.1, bf16[8,22]{1,0:T(8,128)(2,1)} %gates.1, s32[8,22]{1,0:T(8,128)} %ids.1), custom_call_target="tpu_custom_call" | custom-call | tf_op jit(solution)/shard_map/pack/pallas_call | solution.py:81
  1.5 4.1 %collective-permute-start = (bf16[8,2176]{1,0:T(8,128)(2,1)S(1)}, bf16[8,2176]{1,0:T(8,128)(2,1)S(1)}, u32[]{:S(2)}, u32[]{:S(2)}) collective-permute-start(bf16[8,2176]{1,0:T(8,128)(2,1)S(1)} %pack.1), channel_id=1, source_target_pairs={{0,4},{1,5},{2,6},{3,7},{4,0},{5,1},{6,2},{7,3},{8,9},{9,8},{10,11... | collective-permute-start | bytes 104456 | tf_op jit(solution)/shard_map/ppermute | solution.py:32
  5.6 1.3 %collective-permute-start.2 = (bf16[8,2176]{1,0:T(8,128)(2,1)S(1)}, bf16[8,2176]{1,0:T(8,128)(2,1)S(1)}, u32[]{:S(2)}, u32[]{:S(2)}) collective-permute-start(bf16[8,2176]{1,0:T(8,128)(2,1)S(1)} %pack.1), channel_id=1, source_target_pairs={{0,6},{1,7},{2,4},{3,5},{4,2},{5,3},{6,0},{7,1},{8,25},{9,24},{10,... | collective-permute-start | bytes 104456 | tf_op jit(solution)/shard_map/ppermute | solution.py:32
  6.9 0.2 collective-permute-start.1
  7.1 3.0 %load_up.1 = (bf16[2688,1024]{1,0:T(8,128)(2,1)S(1)}, bf16[1024,2688]{1,0:T(8,128)(2,1)S(1)}) custom-call(bf16[2688,1024]{1,0:T(8,128)(2,1)} %bitcast.3), custom_call_target="tpu_custom_call" | custom-call | bytes 5505024 | tf_op jit(solution)/shard_map/load_up/pallas_call | solution.py:105
  10.2 0.0 collective-permute-done
  10.2 1.1 %collective-permute-done.2 = bf16[8,2176]{1,0:T(8,128)(2,1)S(1)} collective-permute-done((bf16[8,2176]{1,0:T(8,128)(2,1)S(1)}, bf16[8,2176]{1,0:T(8,128)(2,1)S(1)}, u32[]{:S(2)}, u32[]{:S(2)}) %collective-permute-start.2) | collective-permute-done | bytes 34848 | tf_op jit(solution)/shard_map/ppermute | solution.py:32
  11.3 0.0 collective-permute-done.1
  11.3 2.5 %collective-permute-start.5 = (bf16[32,2176]{1,0:T(8,128)(2,1)S(1)}, bf16[32,2176]{1,0:T(8,128)(2,1)S(1)}, u32[]{:S(2)}, u32[]{:S(2)}) collective-permute-start(bf16[32,2176]{1,0:T(8,128)(2,1)S(1)} %pad_maximum_fusion.1), channel_id=1, source_target_pairs={{0,17},{1,16},{2,19},{3,18},{4,21},{5,20},{6,23},{7,22},{8,14},{9,... | collective-permute-start | bytes 417800 | tf_op jit(solution)/shard_map/ppermute | solution.py:32
  13.8 0.5 %collective-permute-start.4 = (bf16[32,2176]{1,0:T(8,128)(2,1)S(1)}, bf16[32,2176]{1,0:T(8,128)(2,1)S(1)}, u32[]{:S(2)}, u32[]{:S(2)}) collective-permute-start(bf16[32,2176]{1,0:T(8,128)(2,1)S(1)} %pad_maximum_fusion.1), channel_id=1, source_target_pairs={{0,16},{1,17},{2,18},{3,19},{4,20},{5,21},{6,22},{7,23},{8,10},{9,... | collective-permute-start | bytes 417800 | tf_op jit(solution)/shard_map/ppermute | solution.py:32
  14.3 0.5 %collective-permute-start.3 = (bf16[32,2176]{1,0:T(8,128)(2,1)S(1)}, bf16[32,2176]{1,0:T(8,128)(2,1)S(1)}, u32[]{:S(2)}, u32[]{:S(2)}) collective-permute-start(bf16[32,2176]{1,0:T(8,128)(2,1)S(1)} %pad_maximum_fusion.1), channel_id=1, source_target_pairs={{0,1},{1,0},{2,3},{3,2},{4,5},{5,4},{6,7},{7,6},{8,12},{9,13},{10,... | collective-permute-start | bytes 417800 | tf_op jit(solution)/shard_map/ppermute | solution.py:32
  14.9 3.0 %load_down.1.down_turned = bf16[1024,2688]{1,0:T(8,128)(2,1)S(1)} custom-call(bf16[2688,1024]{1,0:T(8,128)(2,1)} %bitcast.2), custom_call_target="tpu_custom_call" | custom-call | bytes 5505024 | tf_op jit(solution)/shard_map/load_down/pallas_call | solution.py:105
  17.9 0.0 collective-permute-done.5
  17.9 1.0 %collective-permute-done.4 = bf16[32,2176]{1,0:T(8,128)(2,1)S(1)} collective-permute-done((bf16[32,2176]{1,0:T(8,128)(2,1)S(1)}, bf16[32,2176]{1,0:T(8,128)(2,1)S(1)}, u32[]{:S(2)}, u32[]{:S(2)}) %collective-permute-start.4) | collective-permute-done | bytes 139296 | tf_op jit(solution)/shard_map/ppermute | solution.py:32
  18.9 0.5 %collective-permute-done.3 = bf16[32,2176]{1,0:T(8,128)(2,1)S(1)} collective-permute-done((bf16[32,2176]{1,0:T(8,128)(2,1)S(1)}, bf16[32,2176]{1,0:T(8,128)(2,1)S(1)}, u32[]{:S(2)}, u32[]{:S(2)}) %collective-permute-start.3) | collective-permute-done | bytes 139296 | tf_op jit(solution)/shard_map/ppermute | solution.py:32
  19.4 0.1 collective-permute-start.6
  19.5 1.7 %hidden.1 = (f32[128,2688]{1,0:T(8,128)S(1)}, bf16[128,1024]{1,0:T(8,128)(2,1)S(1)}, bf16[128,2688]{1,0:T(8,128)(2,1)S(1)}) custom-call(bf16[128,2176]{1,0:T(8,128)(2,1)S(1)} %pad_maximum_fusion.rows.refs_2_, bf16[1024,2688]{1,0:T(8,128)(2,1)S(1)} %get-tuple-element.37.up_turned, bf16[1024,2688]{1,0:T(8,128)(2,1)S(1)} %load_down.1.down_turned), custom_call_target="tpu_custom_call" | custom-call | flops 1409286144 | tf_op jit(solution)/shard_map/hidden/pallas_call | solution.py:207
  21.2 0.3 collective-permute-done.6.rows.refs_3_
  21.5 2.4 %hidden_part.1 = (f32[128,2688]{1,0:T(8,128)S(1)}, bf16[128,1024]{1,0:T(8,128)(2,1)S(1)}, bf16[128,2688]{1,0:T(8,128)(2,1)S(1)}, bf16[128,1024]{1,0:T(8,128)(2,1)S(1)}) custom-call(bf16[128,2176]{1,0:T(8,128)(2,1)S(1)} %collective-permute-done.6.rows.refs_3_, bf16[1024,2688]{1,0:T(8,128)(2,1)S(1)} %get-tuple-element.37.up_turned, ...), custom_call_target="tpu_custom_call" | custom-call | flops 2113929216 | tf_op jit(solution)/shard_map/hidden_part/pallas_call | solution.py:209
  23.9 0.3 collective-permute-start.7
  24.2 0.9 %part.1 = f32[128,1024]{1,0:T(8,128)S(1)} custom-call(bf16[128,2688]{1,0:T(8,128)(2,1)S(1)} %get-tuple-element.42.pre_grad.refs_0_, bf16[2688,1024]{1,0:T(8,128)(2,1)S(1)} %get-tuple-element.43.w_up), custom_call_target="tpu_custom_call" | custom-call | flops 704643072 | tf_op jit(solution)/shard_map/part/pallas_call | solution.py:212
  25.2 0.4 collective-permute-done.7
  25.5 0.1 fusion.1
  25.6 1.1 %collective-permute-start.8 = (bf16[32,1024]{1,0:T(8,128)(2,1)S(1)}, bf16[32,1024]{1,0:T(8,128)(2,1)S(1)}, u32[]{:S(2)}, u32[]{:S(2)}) collective-permute-start(bf16[32,1024]{1,0:T(8,128)(2,1)S(1)} %get-tuple-element.59), channel_id=1, source_target_pairs={{0,1},{1,0},{2,3},{3,2},{4,5},{5,4},{6,7},{7,6},{8,12},{9,13},{10,... | collective-permute-start | bytes 196616 | tf_op jit(solution)/shard_map/ppermute | solution.py:32
  26.7 1.9 %collective-permute-start.10 = (bf16[32,1024]{1,0:T(8,128)(2,1)S(1)}, bf16[32,1024]{1,0:T(8,128)(2,1)S(1)}, u32[]{:S(2)}, u32[]{:S(2)}) collective-permute-start(bf16[32,1024]{1,0:T(8,128)(2,1)S(1)} %get-tuple-element.60), channel_id=1, source_target_pairs={{0,17},{1,16},{2,19},{3,18},{4,21},{5,20},{6,23},{7,22},{8,14},{9,... | collective-permute-start | bytes 196616 | tf_op jit(solution)/shard_map/ppermute | solution.py:32
  28.7 0.5 %collective-permute-start.9 = (bf16[32,1024]{1,0:T(8,128)(2,1)S(1)}, bf16[32,1024]{1,0:T(8,128)(2,1)S(1)}, u32[]{:S(2)}, u32[]{:S(2)}) collective-permute-start(bf16[32,1024]{1,0:T(8,128)(2,1)S(1)} %get-tuple-element.61), channel_id=1, source_target_pairs={{0,16},{1,17},{2,18},{3,19},{4,20},{5,21},{6,22},{7,23},{8,10},{9,... | collective-permute-start | bytes 196616 | tf_op jit(solution)/shard_map/ppermute | solution.py:32
  29.2 2.9 %up.1 = bf16[1,2688,1024]{2,1,0:T(8,128)(2,1)} custom-call(bf16[128,2688]{1,0:T(8,128)(2,1)S(1)} %get-tuple-element.42.pre_grad.refs_0_, bf16[128,2688]{1,0:T(8,128)(2,1)S(1)} %get-tuple-element.46.refs_1_, bf16[128,2176]{1,0:T(8,128)(2,1)S(1)} %pad_maximum_fusion.rows.refs_2_, bf16[128,2176]{1,0:T(8,128)(2,1)S(1)} %collective-permute-done.6.rows.refs_3_), custom_call_target="tpu_custom_call" | custom-call | flops 1409286144 | bytes 5505024 | tf_op jit(solution)/shard_map/up/pallas_call | solution.py:163
  32.1 0.9 %collective-permute-done.9 = bf16[32,1024]{1,0:T(8,128)(2,1)S(1)} collective-permute-done((bf16[32,1024]{1,0:T(8,128)(2,1)S(1)}, bf16[32,1024]{1,0:T(8,128)(2,1)S(1)}, u32[]{:S(2)}, u32[]{:S(2)}) %collective-permute-start.9) | collective-permute-done | bytes 65568 | tf_op jit(solution)/shard_map/ppermute | solution.py:32
  32.9 0.0 collective-permute-done.8
  32.9 0.0 collective-permute-done.10
  33.0 1.8 %collective-permute-start.11 = (bf16[8,1024]{1,0:T(8,128)(2,1)S(1)}, bf16[8,1024]{1,0:T(8,128)(2,1)S(1)}, u32[]{:S(2)}, u32[]{:S(2)}) collective-permute-start(bf16[8,1024]{1,0:T(8,128)(2,1)S(1)} %get-tuple-element.62), channel_id=1, source_target_pairs={{0,4},{1,5},{2,6},{3,7},{4,0},{5,1},{6,2},{7,3},{8,9},{9,8},{10,11... | collective-permute-start | bytes 49160 | tf_op jit(solution)/shard_map/ppermute | solution.py:32
  34.8 1.3 %collective-permute-start.13 = (bf16[8,1024]{1,0:T(8,128)(2,1)S(1)}, bf16[8,1024]{1,0:T(8,128)(2,1)S(1)}, u32[]{:S(2)}, u32[]{:S(2)}) collective-permute-start(bf16[8,1024]{1,0:T(8,128)(2,1)S(1)} %get-tuple-element.63), channel_id=1, source_target_pairs={{0,6},{1,7},{2,4},{3,5},{4,2},{5,3},{6,0},{7,1},{8,25},{9,24},{10,... | collective-permute-start | bytes 49160 | tf_op jit(solution)/shard_map/ppermute | solution.py:32
  36.1 0.4 %collective-permute-start.12 = (bf16[8,1024]{1,0:T(8,128)(2,1)S(1)}, bf16[8,1024]{1,0:T(8,128)(2,1)S(1)}, u32[]{:S(2)}, u32[]{:S(2)}) collective-permute-start(bf16[8,1024]{1,0:T(8,128)(2,1)S(1)} %get-tuple-element.64), channel_id=1, source_target_pairs={{0,2},{1,3},{2,0},{3,1},{4,6},{5,7},{6,4},{7,5},{8,24},{9,25},{10,... | collective-permute-start | bytes 49160 | tf_op jit(solution)/shard_map/ppermute | solution.py:32
  36.5 2.9 %down.1 = bf16[1,2688,1024]{2,1,0:T(8,128)(2,1)} custom-call(f32[128,2688]{1,0:T(8,128)S(1)} %get-tuple-element.48.refs_0_, f32[128,2688]{1,0:T(8,128)S(1)} %get-tuple-element.49.refs_1_, bf16[128,1024]{1,0:T(8,128)(2,1)S(1)} %get-tuple-element.50.refs_2_, bf16[128,1024]{1,0:T(8,128)(2,1)S(1)} %get-tuple-element.51.refs_3_), custom_call_target="tpu_custom_call" | custom-call | flops 1409286144 | bytes 5505024 | tf_op jit(solution)/shard_map/down/pallas_call | solution.py:163
  39.4 0.9 %collective-permute-done.13 = bf16[8,1024]{1,0:T(8,128)(2,1)S(1)} collective-permute-done((bf16[8,1024]{1,0:T(8,128)(2,1)S(1)}, bf16[8,1024]{1,0:T(8,128)(2,1)S(1)}, u32[]{:S(2)}, u32[]{:S(2)}) %collective-permute-start.13) | collective-permute-done | bytes 16416 | tf_op jit(solution)/shard_map/ppermute | solution.py:32
  40.3 0.0 collective-permute-done.11
  40.3 0.0 collective-permute-done.12
  40.3 0.6 %slice_add_fusion.1 = f32[8,1024]{1,0:T(8,128)} fusion(f32[32,1024]{1,0:T(8,128)S(1)} %get-tuple-element.56, bf16[8,1024]{1,0:T(8,128)(2,1)S(1)} %collective-permute-done.13, bf16[8,1024]{1,0:T(8,128)(2,1)S(1)} %collective-permute-done.12, bf16[8,1024]{1,0:T(8,128)(2,1)S(1)} %collective-permute-done.11), kind=kLoop, calls=%fused_computation.4 | loop fusion | flops 49152 | bytes 114688 | tf_op jit(solution)/shard_map/add | solution.py:228
  (5 shorter events, 0.1 us)
Async XLA Ops:
  1.5 8.7 %collective-permute-start = (bf16[8,2176]{1,0:T(8,128)(2,1)S(1)}, bf16[8,2176]{1,0:T(8,128)(2,1)S(1)}, u32[]{:S(2)}, u32[]{:S(2)}) collective-permute-start(bf16[8,2176]{1,0:T(8,128)(2,1)S(1)} %pack.1), channel_id=1, source_target_pairs={{0,4},{1,5},{2,6},{3,7},{4,0},{5,1},{6,2},{7,3},{8,9},{9,8},{10,11... | collective-permute-start | bytes 104456 | tf_op jit(solution)/shard_map/ppermute | solution.py:32
  5.6 5.7 %collective-permute-start.2 = (bf16[8,2176]{1,0:T(8,128)(2,1)S(1)}, bf16[8,2176]{1,0:T(8,128)(2,1)S(1)}, u32[]{:S(2)}, u32[]{:S(2)}) collective-permute-start(bf16[8,2176]{1,0:T(8,128)(2,1)S(1)} %pack.1), channel_id=1, source_target_pairs={{0,6},{1,7},{2,4},{3,5},{4,2},{5,3},{6,0},{7,1},{8,25},{9,24},{10,... | collective-permute-start | bytes 104456 | tf_op jit(solution)/shard_map/ppermute | solution.py:32
  6.9 4.4 %collective-permute-start.1 = (bf16[8,2176]{1,0:T(8,128)(2,1)S(1)}, bf16[8,2176]{1,0:T(8,128)(2,1)S(1)}, u32[]{:S(2)}, u32[]{:S(2)}) collective-permute-start(bf16[8,2176]{1,0:T(8,128)(2,1)S(1)} %pack.1), channel_id=1, source_target_pairs={{0,2},{1,3},{2,0},{3,1},{4,6},{5,7},{6,4},{7,5},{8,24},{9,25},{10,... | collective-permute-start | bytes 104456 | tf_op jit(solution)/shard_map/ppermute | solution.py:32
  11.3 6.6 %collective-permute-start.5 = (bf16[32,2176]{1,0:T(8,128)(2,1)S(1)}, bf16[32,2176]{1,0:T(8,128)(2,1)S(1)}, u32[]{:S(2)}, u32[]{:S(2)}) collective-permute-start(bf16[32,2176]{1,0:T(8,128)(2,1)S(1)} %pad_maximum_fusion.1), channel_id=1, source_target_pairs={{0,17},{1,16},{2,19},{3,18},{4,21},{5,20},{6,23},{7,22},{8,14},{9,... | collective-permute-start | bytes 417800 | tf_op jit(solution)/shard_map/ppermute | solution.py:32
  13.8 5.1 %collective-permute-start.4 = (bf16[32,2176]{1,0:T(8,128)(2,1)S(1)}, bf16[32,2176]{1,0:T(8,128)(2,1)S(1)}, u32[]{:S(2)}, u32[]{:S(2)}) collective-permute-start(bf16[32,2176]{1,0:T(8,128)(2,1)S(1)} %pad_maximum_fusion.1), channel_id=1, source_target_pairs={{0,16},{1,17},{2,18},{3,19},{4,20},{5,21},{6,22},{7,23},{8,10},{9,... | collective-permute-start | bytes 417800 | tf_op jit(solution)/shard_map/ppermute | solution.py:32
  14.3 5.1 %collective-permute-start.3 = (bf16[32,2176]{1,0:T(8,128)(2,1)S(1)}, bf16[32,2176]{1,0:T(8,128)(2,1)S(1)}, u32[]{:S(2)}, u32[]{:S(2)}) collective-permute-start(bf16[32,2176]{1,0:T(8,128)(2,1)S(1)} %pad_maximum_fusion.1), channel_id=1, source_target_pairs={{0,1},{1,0},{2,3},{3,2},{4,5},{5,4},{6,7},{7,6},{8,12},{9,13},{10,... | collective-permute-start | bytes 417800 | tf_op jit(solution)/shard_map/ppermute | solution.py:32
  19.4 2.0 %collective-permute-start.6 = (bf16[128,2176]{1,0:T(8,128)(2,1)S(1)}, bf16[128,2176]{1,0:T(8,128)(2,1)S(1)}, u32[]{:S(2)}, u32[]{:S(2)}) collective-permute-start(bf16[128,2176]{1,0:T(8,128)(2,1)S(1)} %pad_maximum_fusion.rows.refs_2_), channel_id=1, source_target_pairs={{0,8},{1,9},{2,10},{3,11},{4,12},{5,13},{6,14},{7,15},{8,0},{9,1},... | collective-permute-start | bytes 1671176 | tf_op jit(solution)/shard_map/ppermute | solution.py:32
  23.9 1.6 %collective-permute-start.7 = (bf16[128,1024]{1,0:T(8,128)(2,1)S(1)}, bf16[128,1024]{1,0:T(8,128)(2,1)S(1)}, u32[]{:S(2)}, u32[]{:S(2)}) collective-permute-start(bf16[128,1024]{1,0:T(8,128)(2,1)S(1)} %get-tuple-element.45), channel_id=1, source_target_pairs={{0,8},{1,9},{2,10},{3,11},{4,12},{5,13},{6,14},{7,15},{8,0},{9,1},... | collective-permute-start | bytes 786440 | tf_op jit(solution)/shard_map/ppermute | solution.py:32
  25.6 7.3 %collective-permute-start.8 = (bf16[32,1024]{1,0:T(8,128)(2,1)S(1)}, bf16[32,1024]{1,0:T(8,128)(2,1)S(1)}, u32[]{:S(2)}, u32[]{:S(2)}) collective-permute-start(bf16[32,1024]{1,0:T(8,128)(2,1)S(1)} %get-tuple-element.59), channel_id=1, source_target_pairs={{0,1},{1,0},{2,3},{3,2},{4,5},{5,4},{6,7},{7,6},{8,12},{9,13},{10,... | collective-permute-start | bytes 196616 | tf_op jit(solution)/shard_map/ppermute | solution.py:32
  26.7 6.2 %collective-permute-start.10 = (bf16[32,1024]{1,0:T(8,128)(2,1)S(1)}, bf16[32,1024]{1,0:T(8,128)(2,1)S(1)}, u32[]{:S(2)}, u32[]{:S(2)}) collective-permute-start(bf16[32,1024]{1,0:T(8,128)(2,1)S(1)} %get-tuple-element.60), channel_id=1, source_target_pairs={{0,17},{1,16},{2,19},{3,18},{4,21},{5,20},{6,23},{7,22},{8,14},{9,... | collective-permute-start | bytes 196616 | tf_op jit(solution)/shard_map/ppermute | solution.py:32
  28.7 4.3 %collective-permute-start.9 = (bf16[32,1024]{1,0:T(8,128)(2,1)S(1)}, bf16[32,1024]{1,0:T(8,128)(2,1)S(1)}, u32[]{:S(2)}, u32[]{:S(2)}) collective-permute-start(bf16[32,1024]{1,0:T(8,128)(2,1)S(1)} %get-tuple-element.61), channel_id=1, source_target_pairs={{0,16},{1,17},{2,18},{3,19},{4,20},{5,21},{6,22},{7,23},{8,10},{9,... | collective-permute-start | bytes 196616 | tf_op jit(solution)/shard_map/ppermute | solution.py:32
  33.0 7.3 %collective-permute-start.11 = (bf16[8,1024]{1,0:T(8,128)(2,1)S(1)}, bf16[8,1024]{1,0:T(8,128)(2,1)S(1)}, u32[]{:S(2)}, u32[]{:S(2)}) collective-permute-start(bf16[8,1024]{1,0:T(8,128)(2,1)S(1)} %get-tuple-element.62), channel_id=1, source_target_pairs={{0,4},{1,5},{2,6},{3,7},{4,0},{5,1},{6,2},{7,3},{8,9},{9,8},{10,11... | collective-permute-start | bytes 49160 | tf_op jit(solution)/shard_map/ppermute | solution.py:32
  34.8 5.5 %collective-permute-start.13 = (bf16[8,1024]{1,0:T(8,128)(2,1)S(1)}, bf16[8,1024]{1,0:T(8,128)(2,1)S(1)}, u32[]{:S(2)}, u32[]{:S(2)}) collective-permute-start(bf16[8,1024]{1,0:T(8,128)(2,1)S(1)} %get-tuple-element.63), channel_id=1, source_target_pairs={{0,6},{1,7},{2,4},{3,5},{4,2},{5,3},{6,0},{7,1},{8,25},{9,24},{10,... | collective-permute-start | bytes 49160 | tf_op jit(solution)/shard_map/ppermute | solution.py:32
  36.1 4.2 %collective-permute-start.12 = (bf16[8,1024]{1,0:T(8,128)(2,1)S(1)}, bf16[8,1024]{1,0:T(8,128)(2,1)S(1)}, u32[]{:S(2)}, u32[]{:S(2)}) collective-permute-start(bf16[8,1024]{1,0:T(8,128)(2,1)S(1)} %get-tuple-element.64), channel_id=1, source_target_pairs={{0,2},{1,3},{2,0},{3,1},{4,6},{5,7},{6,4},{7,5},{8,24},{9,25},{10,... | collective-permute-start | bytes 49160 | tf_op jit(solution)/shard_map/ppermute | solution.py:32

commit v8 on v6

--- a/solution.py
+++ b/solution.py
@@ -8,7 +8,7 @@
 HID = 2688
 LANES = 128
 AXES = ("group", "member")
-TIED = (0, 2, 1, 2)
+TIED = (0, 2, 1, 1)
 BF16 = jnp.bfloat16
 F32 = jnp.float32
 VMEM = pl.BlockSpec(memory_space=pltpu.VMEM)

time: 41.2 us -> 41.2 us (level)
  transfers between devices with their start and end apart: 14 -> 14, of which waited for: 7 -> 8; matrix products, arithmetic and copies ran while one was open for 0% -> 0% of each run, Pallas kernels for 35% -> 35%
where the time goes in v8:
time: 41.2 us; the launch traced here: 41 us
  Pallas kernels  17.7 us (43%)
  starting transfers between devices  16.7 us (41%)
  waiting for transfers between devices  4.96 us (12%)
  other arithmetic  0.78 us (2%)
  between operations  0.76 us (2%)
    ppermute x14, starting transfers between devices, swap(): lax.ppermute(value, AXES, [(i, i ^ (odd if i & core else even)) for i in...  16.7 us
    pallas_call x2, Pallas kernels, load(): call(kernel, out, [HBM], name, scratch, moved=2 * weight.size)  6.02 us
    pallas_call x2, Pallas kernels, outer(): call(kernel, S((1, n, width), BF16), [VMEM] * (len(lefts) + len(rights)),...  5.77 us
    ppermute x14, waiting for transfers between devices, swap(): lax.ppermute(value, AXES, [(i, i ^ (odd if i & core else even)) for i in...  4.96 us
    pallas_call x1, Pallas kernels, local(): call(hidden_part, (*outs, S((half, width), BF16)), [VMEM] * 4, 'hidden_pa...  2.44 us
    pallas_call x1, Pallas kernels, local(): call(hidden, outs, [VMEM] * 3, 'hidden', flops=flops)  1.69 us
    pallas_call x1, Pallas kernels, local(): call(part_kernel, S((half, width), F32), [VMEM] * 2, 'part', flops=flops...  0.92 us
    pallas_call x1, Pallas kernels, pack(): call(pack_kernel, S((rows, 2 * width + LANES), BF16), [HBM] * 4, 'pack',...  0.88 us
  transfers between devices with their start and end apart: 14, of which 8 were waited for; matrix products, arithmetic and copies ran while one was open for 0% of the time, Pallas kernels for 35%

profile of v8, /device:TPU:0, one launch (start us, length us, event | category | flops | bytes accessed | tf_op | source)
XLA Modules:
  0.0 41.0 jit_solution(3103404639733532843)
XLA Ops:
  0.6 0.9 %pack.1 = bf16[8,2176]{1,0:T(8,128)(2,1)S(1)} custom-call(bf16[8,1024]{1,0:T(8,128)(2,1)} %latent.1, bf16[8,1024]{1,0:T(8,128)(2,1)} %out_grad.1, bf16[8,22]{1,0:T(8,128)(2,1)} %gates.1, s32[8,22]{1,0:T(8,128)} %ids.1), custom_call_target="tpu_custom_call" | custom-call | tf_op jit(solution)/shard_map/pack/pallas_call | solution.py:83
  1.5 4.1 %collective-permute-start = (bf16[8,2176]{1,0:T(8,128)(2,1)S(1)}, bf16[8,2176]{1,0:T(8,128)(2,1)S(1)}, u32[]{:S(2)}, u32[]{:S(2)}) collective-permute-start(bf16[8,2176]{1,0:T(8,128)(2,1)S(1)} %pack.1), channel_id=1, source_target_pairs={{0,4},{1,5},{2,6},{3,7},{4,0},{5,1},{6,2},{7,3},{8,9},{9,8},{10,11... | collective-permute-start | bytes 104456 | tf_op jit(solution)/shard_map/ppermute | solution.py:32
  5.6 1.3 %collective-permute-start.2 = (bf16[8,2176]{1,0:T(8,128)(2,1)S(1)}, bf16[8,2176]{1,0:T(8,128)(2,1)S(1)}, u32[]{:S(2)}, u32[]{:S(2)}) collective-permute-start(bf16[8,2176]{1,0:T(8,128)(2,1)S(1)} %pack.1), channel_id=1, source_target_pairs={{0,6},{1,7},{2,4},{3,5},{4,2},{5,3},{6,0},{7,1},{8,25},{9,24},{10,... | collective-permute-start | bytes 104456 | tf_op jit(solution)/shard_map/ppermute | solution.py:32
  7.0 0.2 collective-permute-start.1
  7.2 3.0 %load_up.1 = (bf16[2688,1024]{1,0:T(8,128)(2,1)S(1)}, bf16[1024,2688]{1,0:T(8,128)(2,1)S(1)}) custom-call(bf16[2688,1024]{1,0:T(8,128)(2,1)} %bitcast.3), custom_call_target="tpu_custom_call" | custom-call | bytes 5505024 | tf_op jit(solution)/shard_map/load_up/pallas_call | solution.py:107
  10.2 0.0 collective-permute-done
  10.2 1.1 %collective-permute-done.2 = bf16[8,2176]{1,0:T(8,128)(2,1)S(1)} collective-permute-done((bf16[8,2176]{1,0:T(8,128)(2,1)S(1)}, bf16[8,2176]{1,0:T(8,128)(2,1)S(1)}, u32[]{:S(2)}, u32[]{:S(2)}) %collective-permute-start.2) | collective-permute-done | bytes 34848 | tf_op jit(solution)/shard_map/ppermute | solution.py:32
  11.4 0.0 collective-permute-done.1
  11.4 2.5 %collective-permute-start.5 = (bf16[32,2176]{1,0:T(8,128)(2,1)S(1)}, bf16[32,2176]{1,0:T(8,128)(2,1)S(1)}, u32[]{:S(2)}, u32[]{:S(2)}) collective-permute-start(bf16[32,2176]{1,0:T(8,128)(2,1)S(1)} %pad_maximum_fusion.1), channel_id=1, source_target_pairs={{0,17},{1,16},{2,19},{3,18},{4,21},{5,20},{6,23},{7,22},{8,14},{9,... | collective-permute-start | bytes 417800 | tf_op jit(solution)/shard_map/ppermute | solution.py:32
  13.9 0.5 %collective-permute-start.4 = (bf16[32,2176]{1,0:T(8,128)(2,1)S(1)}, bf16[32,2176]{1,0:T(8,128)(2,1)S(1)}, u32[]{:S(2)}, u32[]{:S(2)}) collective-permute-start(bf16[32,2176]{1,0:T(8,128)(2,1)S(1)} %pad_maximum_fusion.1), channel_id=1, source_target_pairs={{0,16},{1,17},{2,18},{3,19},{4,20},{5,21},{6,22},{7,23},{8,10},{9,... | collective-permute-start | bytes 417800 | tf_op jit(solution)/shard_map/ppermute | solution.py:32
  14.4 0.5 %collective-permute-start.3 = (bf16[32,2176]{1,0:T(8,128)(2,1)S(1)}, bf16[32,2176]{1,0:T(8,128)(2,1)S(1)}, u32[]{:S(2)}, u32[]{:S(2)}) collective-permute-start(bf16[32,2176]{1,0:T(8,128)(2,1)S(1)} %pad_maximum_fusion.1), channel_id=1, source_target_pairs={{0,1},{1,0},{2,3},{3,2},{4,5},{5,4},{6,7},{7,6},{8,12},{9,13},{10,... | collective-permute-start | bytes 417800 | tf_op jit(solution)/shard_map/ppermute | solution.py:32
  14.9 3.0 %load_down.1.down_turned = bf16[1024,2688]{1,0:T(8,128)(2,1)S(1)} custom-call(bf16[2688,1024]{1,0:T(8,128)(2,1)} %bitcast.2), custom_call_target="tpu_custom_call" | custom-call | bytes 5505024 | tf_op jit(solution)/shard_map/load_down/pallas_call | solution.py:107
  17.9 0.0 collective-permute-done.5
  18.0 1.0 %collective-permute-done.4 = bf16[32,2176]{1,0:T(8,128)(2,1)S(1)} collective-permute-done((bf16[32,2176]{1,0:T(8,128)(2,1)S(1)}, bf16[32,2176]{1,0:T(8,128)(2,1)S(1)}, u32[]{:S(2)}, u32[]{:S(2)}) %collective-permute-start.4) | collective-permute-done | bytes 139296 | tf_op jit(solution)/shard_map/ppermute | solution.py:32
  18.9 0.5 %collective-permute-done.3 = bf16[32,2176]{1,0:T(8,128)(2,1)S(1)} collective-permute-done((bf16[32,2176]{1,0:T(8,128)(2,1)S(1)}, bf16[32,2176]{1,0:T(8,128)(2,1)S(1)}, u32[]{:S(2)}, u32[]{:S(2)}) %collective-permute-start.3) | collective-permute-done | bytes 139296 | tf_op jit(solution)/shard_map/ppermute | solution.py:32
  19.5 0.1 collective-permute-start.6
  19.6 1.7 %hidden.1 = (f32[128,2688]{1,0:T(8,128)S(1)}, bf16[128,1024]{1,0:T(8,128)(2,1)S(1)}, bf16[128,2688]{1,0:T(8,128)(2,1)S(1)}) custom-call(bf16[128,2176]{1,0:T(8,128)(2,1)S(1)} %pad_maximum_fusion.rows.refs_2_, bf16[1024,2688]{1,0:T(8,128)(2,1)S(1)} %get-tuple-element.37.up_turned, bf16[1024,2688]{1,0:T(8,128)(2,1)S(1)} %load_down.1.down_turned), custom_call_target="tpu_custom_call" | custom-call | flops 1409286144 | tf_op jit(solution)/shard_map/hidden/pallas_call | solution.py:209
  21.3 0.3 collective-permute-done.6.rows.refs_3_
  21.5 2.4 %hidden_part.1 = (f32[128,2688]{1,0:T(8,128)S(1)}, bf16[128,1024]{1,0:T(8,128)(2,1)S(1)}, bf16[128,2688]{1,0:T(8,128)(2,1)S(1)}, bf16[128,1024]{1,0:T(8,128)(2,1)S(1)}) custom-call(bf16[128,2176]{1,0:T(8,128)(2,1)S(1)} %collective-permute-done.6.rows.refs_3_, bf16[1024,2688]{1,0:T(8,128)(2,1)S(1)} %get-tuple-element.37.up_turned, ...), custom_call_target="tpu_custom_call" | custom-call | flops 2113929216 | tf_op jit(solution)/shard_map/hidden_part/pallas_call | solution.py:211
  24.0 0.3 collective-permute-start.7
  24.3 0.9 %part.1 = f32[128,1024]{1,0:T(8,128)S(1)} custom-call(bf16[128,2688]{1,0:T(8,128)(2,1)S(1)} %get-tuple-element.42.pre_grad.refs_0_, bf16[2688,1024]{1,0:T(8,128)(2,1)S(1)} %get-tuple-element.43.w_up), custom_call_target="tpu_custom_call" | custom-call | flops 704643072 | tf_op jit(solution)/shard_map/part/pallas_call | solution.py:214
  25.2 0.4 collective-permute-done.7
  25.6 0.1 fusion.1
  25.7 1.1 %collective-permute-start.8 = (bf16[32,1024]{1,0:T(8,128)(2,1)S(1)}, bf16[32,1024]{1,0:T(8,128)(2,1)S(1)}, u32[]{:S(2)}, u32[]{:S(2)}) collective-permute-start(bf16[32,1024]{1,0:T(8,128)(2,1)S(1)} %get-tuple-element.59), channel_id=1, source_target_pairs={{0,1},{1,0},{2,3},{3,2},{4,5},{5,4},{6,7},{7,6},{8,12},{9,13},{10,... | collective-permute-start | bytes 196616 | tf_op jit(solution)/shard_map/ppermute | solution.py:32
  26.8 2.0 %collective-permute-start.10 = (bf16[32,1024]{1,0:T(8,128)(2,1)S(1)}, bf16[32,1024]{1,0:T(8,128)(2,1)S(1)}, u32[]{:S(2)}, u32[]{:S(2)}) collective-permute-start(bf16[32,1024]{1,0:T(8,128)(2,1)S(1)} %get-tuple-element.60), channel_id=1, source_target_pairs={{0,17},{1,16},{2,19},{3,18},{4,21},{5,20},{6,23},{7,22},{8,14},{9,... | collective-permute-start | bytes 196616 | tf_op jit(solution)/shard_map/ppermute | solution.py:32
  28.7 0.5 %collective-permute-start.9 = (bf16[32,1024]{1,0:T(8,128)(2,1)S(1)}, bf16[32,1024]{1,0:T(8,128)(2,1)S(1)}, u32[]{:S(2)}, u32[]{:S(2)}) collective-permute-start(bf16[32,1024]{1,0:T(8,128)(2,1)S(1)} %get-tuple-element.61), channel_id=1, source_target_pairs={{0,16},{1,17},{2,18},{3,19},{4,20},{5,21},{6,22},{7,23},{8,10},{9,... | collective-permute-start | bytes 196616 | tf_op jit(solution)/shard_map/ppermute | solution.py:32
  29.2 2.9 %up.1 = bf16[1,2688,1024]{2,1,0:T(8,128)(2,1)} custom-call(bf16[128,2688]{1,0:T(8,128)(2,1)S(1)} %get-tuple-element.42.pre_grad.refs_0_, bf16[128,2688]{1,0:T(8,128)(2,1)S(1)} %get-tuple-element.46.refs_1_, bf16[128,2176]{1,0:T(8,128)(2,1)S(1)} %pad_maximum_fusion.rows.refs_2_, bf16[128,2176]{1,0:T(8,128)(2,1)S(1)} %collective-permute-done.6.rows.refs_3_), custom_call_target="tpu_custom_call" | custom-call | flops 1409286144 | bytes 5505024 | tf_op jit(solution)/shard_map/up/pallas_call | solution.py:165
  32.1 0.9 %collective-permute-done.9 = bf16[32,1024]{1,0:T(8,128)(2,1)S(1)} collective-permute-done((bf16[32,1024]{1,0:T(8,128)(2,1)S(1)}, bf16[32,1024]{1,0:T(8,128)(2,1)S(1)}, u32[]{:S(2)}, u32[]{:S(2)}) %collective-permute-start.9) | collective-permute-done | bytes 65568 | tf_op jit(solution)/shard_map/ppermute | solution.py:32
  33.0 0.0 collective-permute-done.8
  33.0 0.0 collective-permute-done.10
  33.0 1.8 %collective-permute-start.11 = (bf16[8,1024]{1,0:T(8,128)(2,1)S(1)}, bf16[8,1024]{1,0:T(8,128)(2,1)S(1)}, u32[]{:S(2)}, u32[]{:S(2)}) collective-permute-start(bf16[8,1024]{1,0:T(8,128)(2,1)S(1)} %get-tuple-element.62), channel_id=1, source_target_pairs={{0,4},{1,5},{2,6},{3,7},{4,0},{5,1},{6,2},{7,3},{8,9},{9,8},{10,11... | collective-permute-start | bytes 49160 | tf_op jit(solution)/shard_map/ppermute | solution.py:32
  34.8 1.4 %collective-permute-start.13 = (bf16[8,1024]{1,0:T(8,128)(2,1)S(1)}, bf16[8,1024]{1,0:T(8,128)(2,1)S(1)}, u32[]{:S(2)}, u32[]{:S(2)}) collective-permute-start(bf16[8,1024]{1,0:T(8,128)(2,1)S(1)} %get-tuple-element.63), channel_id=1, source_target_pairs={{0,6},{1,7},{2,4},{3,5},{4,2},{5,3},{6,0},{7,1},{8,25},{9,24},{10,... | collective-permute-start | bytes 49160 | tf_op jit(solution)/shard_map/ppermute | solution.py:32
  36.2 0.4 %collective-permute-start.12 = (bf16[8,1024]{1,0:T(8,128)(2,1)S(1)}, bf16[8,1024]{1,0:T(8,128)(2,1)S(1)}, u32[]{:S(2)}, u32[]{:S(2)}) collective-permute-start(bf16[8,1024]{1,0:T(8,128)(2,1)S(1)} %get-tuple-element.64), channel_id=1, source_target_pairs={{0,2},{1,3},{2,0},{3,1},{4,6},{5,7},{6,4},{7,5},{8,24},{9,25},{10,... | collective-permute-start | bytes 49160 | tf_op jit(solution)/shard_map/ppermute | solution.py:32
  36.6 2.9 %down.1 = bf16[1,2688,1024]{2,1,0:T(8,128)(2,1)} custom-call(f32[128,2688]{1,0:T(8,128)S(1)} %get-tuple-element.48.refs_0_, f32[128,2688]{1,0:T(8,128)S(1)} %get-tuple-element.49.refs_1_, bf16[128,1024]{1,0:T(8,128)(2,1)S(1)} %get-tuple-element.50.refs_2_, bf16[128,1024]{1,0:T(8,128)(2,1)S(1)} %get-tuple-element.51.refs_3_), custom_call_target="tpu_custom_call" | custom-call | flops 1409286144 | bytes 5505024 | tf_op jit(solution)/shard_map/down/pallas_call | solution.py:165
  39.5 0.4 %collective-permute-done.12 = bf16[8,1024]{1,0:T(8,128)(2,1)S(1)} collective-permute-done((bf16[8,1024]{1,0:T(8,128)(2,1)S(1)}, bf16[8,1024]{1,0:T(8,128)(2,1)S(1)}, u32[]{:S(2)}, u32[]{:S(2)}) %collective-permute-start.12) | collective-permute-done | bytes 16416 | tf_op jit(solution)/shard_map/ppermute | solution.py:32
  39.9 0.0 collective-permute-done.11
  39.9 0.4 %collective-permute-done.13 = bf16[8,1024]{1,0:T(8,128)(2,1)S(1)} collective-permute-done((bf16[8,1024]{1,0:T(8,128)(2,1)S(1)}, bf16[8,1024]{1,0:T(8,128)(2,1)S(1)}, u32[]{:S(2)}, u32[]{:S(2)}) %collective-permute-start.13) | collective-permute-done | bytes 16416 | tf_op jit(solution)/shard_map/ppermute | solution.py:32
  40.3 0.6 %slice_add_fusion.1 = f32[8,1024]{1,0:T(8,128)} fusion(f32[32,1024]{1,0:T(8,128)S(1)} %get-tuple-element.56, bf16[8,1024]{1,0:T(8,128)(2,1)S(1)} %collective-permute-done.13, bf16[8,1024]{1,0:T(8,128)(2,1)S(1)} %collective-permute-done.12, bf16[8,1024]{1,0:T(8,128)(2,1)S(1)} %collective-permute-done.11), kind=kLoop, calls=%fused_computation.4 | loop fusion | flops 49152 | bytes 114688 | tf_op jit(solution)/shard_map/add | solution.py:230
  (5 shorter events, 0.1 us)
Async XLA Ops:
  1.5 8.7 %collective-permute-start = (bf16[8,2176]{1,0:T(8,128)(2,1)S(1)}, bf16[8,2176]{1,0:T(8,128)(2,1)S(1)}, u32[]{:S(2)}, u32[]{:S(2)}) collective-permute-start(bf16[8,2176]{1,0:T(8,128)(2,1)S(1)} %pack.1), channel_id=1, source_target_pairs={{0,4},{1,5},{2,6},{3,7},{4,0},{5,1},{6,2},{7,3},{8,9},{9,8},{10,11... | collective-permute-start | bytes 104456 | tf_op jit(solution)/shard_map/ppermute | solution.py:32
  5.6 5.7 %collective-permute-start.2 = (bf16[8,2176]{1,0:T(8,128)(2,1)S(1)}, bf16[8,2176]{1,0:T(8,128)(2,1)S(1)}, u32[]{:S(2)}, u32[]{:S(2)}) collective-permute-start(bf16[8,2176]{1,0:T(8,128)(2,1)S(1)} %pack.1), channel_id=1, source_target_pairs={{0,6},{1,7},{2,4},{3,5},{4,2},{5,3},{6,0},{7,1},{8,25},{9,24},{10,... | collective-permute-start | bytes 104456 | tf_op jit(solution)/shard_map/ppermute | solution.py:32
  7.0 4.4 %collective-permute-start.1 = (bf16[8,2176]{1,0:T(8,128)(2,1)S(1)}, bf16[8,2176]{1,0:T(8,128)(2,1)S(1)}, u32[]{:S(2)}, u32[]{:S(2)}) collective-permute-start(bf16[8,2176]{1,0:T(8,128)(2,1)S(1)} %pack.1), channel_id=1, source_target_pairs={{0,2},{1,3},{2,0},{3,1},{4,6},{5,7},{6,4},{7,5},{8,24},{9,25},{10,... | collective-permute-start | bytes 104456 | tf_op jit(solution)/shard_map/ppermute | solution.py:32
  11.4 6.6 %collective-permute-start.5 = (bf16[32,2176]{1,0:T(8,128)(2,1)S(1)}, bf16[32,2176]{1,0:T(8,128)(2,1)S(1)}, u32[]{:S(2)}, u32[]{:S(2)}) collective-permute-start(bf16[32,2176]{1,0:T(8,128)(2,1)S(1)} %pad_maximum_fusion.1), channel_id=1, source_target_pairs={{0,17},{1,16},{2,19},{3,18},{4,21},{5,20},{6,23},{7,22},{8,14},{9,... | collective-permute-start | bytes 417800 | tf_op jit(solution)/shard_map/ppermute | solution.py:32
  13.9 5.1 %collective-permute-start.4 = (bf16[32,2176]{1,0:T(8,128)(2,1)S(1)}, bf16[32,2176]{1,0:T(8,128)(2,1)S(1)}, u32[]{:S(2)}, u32[]{:S(2)}) collective-permute-start(bf16[32,2176]{1,0:T(8,128)(2,1)S(1)} %pad_maximum_fusion.1), channel_id=1, source_target_pairs={{0,16},{1,17},{2,18},{3,19},{4,20},{5,21},{6,22},{7,23},{8,10},{9,... | collective-permute-start | bytes 417800 | tf_op jit(solution)/shard_map/ppermute | solution.py:32
  14.4 5.1 %collective-permute-start.3 = (bf16[32,2176]{1,0:T(8,128)(2,1)S(1)}, bf16[32,2176]{1,0:T(8,128)(2,1)S(1)}, u32[]{:S(2)}, u32[]{:S(2)}) collective-permute-start(bf16[32,2176]{1,0:T(8,128)(2,1)S(1)} %pad_maximum_fusion.1), channel_id=1, source_target_pairs={{0,1},{1,0},{2,3},{3,2},{4,5},{5,4},{6,7},{7,6},{8,12},{9,13},{10,... | collective-permute-start | bytes 417800 | tf_op jit(solution)/shard_map/ppermute | solution.py:32
  19.5 2.0 %collective-permute-start.6 = (bf16[128,2176]{1,0:T(8,128)(2,1)S(1)}, bf16[128,2176]{1,0:T(8,128)(2,1)S(1)}, u32[]{:S(2)}, u32[]{:S(2)}) collective-permute-start(bf16[128,2176]{1,0:T(8,128)(2,1)S(1)} %pad_maximum_fusion.rows.refs_2_), channel_id=1, source_target_pairs={{0,8},{1,9},{2,10},{3,11},{4,12},{5,13},{6,14},{7,15},{8,0},{9,1},... | collective-permute-start | bytes 1671176 | tf_op jit(solution)/shard_map/ppermute | solution.py:32
  24.0 1.6 %collective-permute-start.7 = (bf16[128,1024]{1,0:T(8,128)(2,1)S(1)}, bf16[128,1024]{1,0:T(8,128)(2,1)S(1)}, u32[]{:S(2)}, u32[]{:S(2)}) collective-permute-start(bf16[128,1024]{1,0:T(8,128)(2,1)S(1)} %get-tuple-element.45), channel_id=1, source_target_pairs={{0,8},{1,9},{2,10},{3,11},{4,12},{5,13},{6,14},{7,15},{8,0},{9,1},... | collective-permute-start | bytes 786440 | tf_op jit(solution)/shard_map/ppermute | solution.py:32
  25.7 7.3 %collective-permute-start.8 = (bf16[32,1024]{1,0:T(8,128)(2,1)S(1)}, bf16[32,1024]{1,0:T(8,128)(2,1)S(1)}, u32[]{:S(2)}, u32[]{:S(2)}) collective-permute-start(bf16[32,1024]{1,0:T(8,128)(2,1)S(1)} %get-tuple-element.59), channel_id=1, source_target_pairs={{0,1},{1,0},{2,3},{3,2},{4,5},{5,4},{6,7},{7,6},{8,12},{9,13},{10,... | collective-permute-start | bytes 196616 | tf_op jit(solution)/shard_map/ppermute | solution.py:32
  26.8 6.2 %collective-permute-start.10 = (bf16[32,1024]{1,0:T(8,128)(2,1)S(1)}, bf16[32,1024]{1,0:T(8,128)(2,1)S(1)}, u32[]{:S(2)}, u32[]{:S(2)}) collective-permute-start(bf16[32,1024]{1,0:T(8,128)(2,1)S(1)} %get-tuple-element.60), channel_id=1, source_target_pairs={{0,17},{1,16},{2,19},{3,18},{4,21},{5,20},{6,23},{7,22},{8,14},{9,... | collective-permute-start | bytes 196616 | tf_op jit(solution)/shard_map/ppermute | solution.py:32
  28.7 4.3 %collective-permute-start.9 = (bf16[32,1024]{1,0:T(8,128)(2,1)S(1)}, bf16[32,1024]{1,0:T(8,128)(2,1)S(1)}, u32[]{:S(2)}, u32[]{:S(2)}) collective-permute-start(bf16[32,1024]{1,0:T(8,128)(2,1)S(1)} %get-tuple-element.61), channel_id=1, source_target_pairs={{0,16},{1,17},{2,18},{3,19},{4,20},{5,21},{6,22},{7,23},{8,10},{9,... | collective-permute-start | bytes 196616 | tf_op jit(solution)/shard_map/ppermute | solution.py:32
  33.0 6.9 %collective-permute-start.11 = (bf16[8,1024]{1,0:T(8,128)(2,1)S(1)}, bf16[8,1024]{1,0:T(8,128)(2,1)S(1)}, u32[]{:S(2)}, u32[]{:S(2)}) collective-permute-start(bf16[8,1024]{1,0:T(8,128)(2,1)S(1)} %get-tuple-element.62), channel_id=1, source_target_pairs={{0,4},{1,5},{2,6},{3,7},{4,0},{5,1},{6,2},{7,3},{8,9},{9,8},{10,11... | collective-permute-start | bytes 49160 | tf_op jit(solution)/shard_map/ppermute | solution.py:32
  34.8 5.5 %collective-permute-start.13 = (bf16[8,1024]{1,0:T(8,128)(2,1)S(1)}, bf16[8,1024]{1,0:T(8,128)(2,1)S(1)}, u32[]{:S(2)}, u32[]{:S(2)}) collective-permute-start(bf16[8,1024]{1,0:T(8,128)(2,1)S(1)} %get-tuple-element.63), channel_id=1, source_target_pairs={{0,6},{1,7},{2,4},{3,5},{4,2},{5,3},{6,0},{7,1},{8,25},{9,24},{10,... | collective-permute-start | bytes 49160 | tf_op jit(solution)/shard_map/ppermute | solution.py:32
  36.2 3.7 %collective-permute-start.12 = (bf16[8,1024]{1,0:T(8,128)(2,1)S(1)}, bf16[8,1024]{1,0:T(8,128)(2,1)S(1)}, u32[]{:S(2)}, u32[]{:S(2)}) collective-permute-start(bf16[8,1024]{1,0:T(8,128)(2,1)S(1)} %get-tuple-element.64), channel_id=1, source_target_pairs={{0,2},{1,3},{2,0},{3,1},{4,6},{5,7},{6,4},{7,5},{8,24},{9,25},{10,... | collective-permute-start | bytes 49160 | tf_op jit(solution)/shard_map/ppermute | solution.py:32
